TPU v7x, 32 devices: a whole 2x2x4 slice. The times are simulated.
32 devices in a mesh: dp: 4 (over z), expert: 8 (over y, x, core).
Axes of the slice: x: 2, y: 2, z: 4, core: 2. Of those that a mesh axis runs over, the one named last changes fastest.
Arguments:
- tokens: bfloat16 [4096, 2560], P(('dp', 'expert')), may hold values from -6 to 6
- expert_ids: int32 [4096, 6], P(('dp', 'expert')), may hold values from 0 to 7, as said below
- gate_values: float32 [4096, 6], P(('dp', 'expert')), may hold values from 0.05 to 0.5
- w_gate: bfloat16 [8, 2560, 768], P('expert'), may hold values from -0.125 to 0.125
- w_up: bfloat16 [8, 2560, 768], P('expert'), may hold values from -0.125 to 0.125
- w_down: bfloat16 [8, 768, 2560], P('expert'), may hold values from -0.21875 to 0.21875
Outputs:
- moe_out: bfloat16 [4096, 2560], P(('dp', 'expert'))
Inputs may be any that keep to these rules, and one draw needn't show every extreme that they name: `expert_ids`: within each block of 128 rows (one device's tokens), column 0 of every row holds one of two experts that are the same for all devices of a dp group, each of them in 56 to 72 rows, and no other entry names them; the two experts of different dp groups are different; the entries of a row differ; any other expert is named by at most 128 rows of one device, and in every dp group one such expert is named by exactly 128 rows of each of its devices; in some dp group other than the first, one of the two is named by 72 rows of every device, and that expert is named by exactly 128 rows of every device of the first dp group.
All inputs are finite; a program needn't handle non-finite values.
Results may differ from a plain program's by a relative error of at most 0.0058.
Values may be sent and summed in bfloat16 or wider, within the bound.
No kernel may reach another device: no remote copies, remote signals or barrier semaphores. Data moves between devices by JAX's collectives and lax.ppermute only.
A program may use at most 128 MiB of HBM per device.

v0:
```python
import jax
import jax.numpy as jnp
from jax import lax
from jax.sharding import PartitionSpec as P


def expert_apply(row_block, gate_matrix, up_matrix, down_matrix):
    gate_part = jnp.dot(row_block, gate_matrix, preferred_element_type=jnp.float32)
    up_part = jnp.dot(row_block, up_matrix, preferred_element_type=jnp.float32)
    hidden = (jax.nn.silu(gate_part) * up_part).astype(jnp.bfloat16)
    return jnp.dot(hidden, down_matrix, preferred_element_type=jnp.float32).astype(jnp.bfloat16)


def local_experts(received, w_gate, w_up, w_down):
    local_count = w_gate.shape[0]
    sources = received.shape[0] // local_count
    slot_count = received.shape[1]
    features = received.shape[2]
    grouped = received.reshape(sources, local_count, slot_count, features)
    row_block = grouped[:, 0].reshape(-1, features)
    answer = expert_apply(row_block, w_gate[0], w_up[0], w_down[0])
    results = [answer.reshape(sources, slot_count, features)]
    return jnp.stack(results, axis=1).reshape(received.shape)


def dispatch_pairs(source, pair_rows, pair_ids, kept_pairs, slot_bound, w_gate, w_up, w_down):
    source_count, features = source.shape
    experts_all = lax.axis_size("expert") * w_gate.shape[0]
    one_hot = (
        (pair_ids[:, None] == jnp.arange(experts_all, dtype=jnp.int32)[None, :])
        & kept_pairs[:, None]
    ).astype(jnp.int32)
    earlier = jnp.cumsum(one_hot, axis=0) - one_hot
    slot_of = jnp.sum(earlier * one_hot, axis=1)
    padded_source = jnp.concatenate([source, jnp.zeros((1, features), source.dtype)], axis=0)
    buffer_rows = experts_all * slot_bound
    places = pair_ids * slot_bound + slot_of
    places = jnp.where(kept_pairs, places, buffer_rows)
    slot_table = (
        jnp.full((buffer_rows,), source_count, jnp.int32).at[places].set(pair_rows, mode="drop")
    )
    outgoing = padded_source[slot_table].reshape(experts_all, slot_bound, features)
    answered = local_experts(
        lax.all_to_all(outgoing, "expert", split_axis=0, concat_axis=0, tiled=True),
        w_gate,
        w_up,
        w_down,
    )
    returned = lax.all_to_all(answered, "expert", split_axis=0, concat_axis=0, tiled=True)
    flat_back = returned.reshape(buffer_rows, features)
    return flat_back[jnp.minimum(places, buffer_rows - 1)]


def shards(tokens, expert_ids, gate_values, w_gate, w_up, w_down):
    token_count, features = tokens.shape
    topk_width = expert_ids.shape[1]
    local_count = w_gate.shape[0]
    experts_all = lax.axis_size("expert") * local_count
    flat_ids = expert_ids.reshape(-1)
    flat_gates = gate_values.reshape(-1)
    pair_count = flat_ids.shape[0]
    owner_rows = jnp.arange(pair_count, dtype=jnp.int32) // topk_width
    other_bound = min(
        token_count,
        ((topk_width - 1) * token_count + experts_all - 3) // (experts_all - 2) * 3 // 2,
    )
    favoured_bound = token_count * 9 // 16
    kept_pairs = jnp.ones(flat_ids.shape, jnp.bool_)
    slot_bound = max(favoured_bound, other_bound)
    returned = dispatch_pairs(
        tokens, owner_rows, flat_ids, kept_pairs, slot_bound, w_gate, w_up, w_down
    )
    weighted = (flat_gates[:, None] * returned.astype(jnp.float32)).reshape(
        token_count, topk_width, features
    )
    summed = jnp.sum(weighted, axis=1)
    return summed.astype(jnp.bfloat16)


def solution(mesh):
    placed = (
        P(("dp", "expert"), None),
        P(("dp", "expert"), None),
        P(("dp", "expert"), None),
        P("expert", None, None),
        P("expert", None, None),
        P("expert", None, None),
    )
    return jax.shard_map(
        shards, mesh=mesh, in_specs=placed, out_specs=P(("dp", "expert"), None), check_vma=False
    )
```

profile of v0, /device:TPU:0, one launch (start us, length us, event | category | flops | bytes accessed | tf_op | source)
XLA Modules:
  0.0 188.9 jit_solution(1641702124381732229)
XLA Ops:
  0.0 0.8 copy.12
  0.8 0.1 eq.29
  0.9 0.1 eq.25
  1.1 0.7 broadcast_multiply_fusion
  1.8 1.7 reduce-window.6
  3.5 0.1 slice.12
  3.6 0.1 copy.14
  3.7 0.2 reduce-window.9
  3.9 0.1 copy.15
  4.0 0.1 copy.11
  4.1 0.1 mul.42
  4.2 0.1 fusion.8
  4.3 3.4 %scatter_custom_fusion = s32[1024]{0:T(1024)S(1)} fusion(s32[768]{0:T(1024)S(1)} %get-tuple-element.6, s32[768]{0:T(1024)S(1)} %add_select_fusion, s32[]{:T(128)} %constant.12.clone.1), kind=kCustom, calls=%fused_computation.33 | custom fusion | bytes 4100 | tf_op jit(solution)/shard_map/scatter | solution.py:40
  7.7 1.1 concatenate.3
  8.9 6.3 %gather_fusion = bf16[1024,2560]{1,0:T(8,128)(2,1)} fusion(bf16[129,2560]{1,0:T(8,128)(2,1)S(1)} %concatenate.3, s32[1024]{0:T(1024)S(1)} %fusion.12), kind=kCustom, calls=%fused_computation | custom fusion | bytes 10489856 | tf_op jit(solution)/shard_map/gather | solution.py:42
  15.2 0.0 copy-start.1
  15.2 65.7 %all_to_all.10 = bf16[8,128,2560]{2,1,0:T(8,128)(2,1)S(1)} all-to-all(bf16[8,128,2560]{2,1,0:T(8,128)(2,1)} %bitcast.28), channel_id=1, replica_groups=mesh['dp'=4,'expert'=8] {'expert'}, dimensions={0} | all-to-all | bytes 10485760 | tf_op jit(solution)/shard_map/all_to_all | solution.py:44
  80.9 0.0 copy-done.1
  80.9 4.2 %fusion.1 = f32[1024,768]{1,0:T(8,128)S(1)} fusion(bf16[1024,2560]{1,0:T(8,128)(2,1)S(1)} %bitcast.30, bf16[1,2560,768]{2,1,0:T(8,128)(2,1)S(1)} %copy-done.1), kind=kOutput, calls=%fused_computation.6 | convolution fusion | flops 4026531840 | bytes 12320768 | tf_op jit(solution)/shard_map/dot_general | solution.py:9
  85.1 0.0 copy-done.2
  85.1 0.0 copy-start.3
  85.1 4.5 %multiply_convert_fusion = bf16[1024,768]{1,0:T(8,128)(2,1)S(1)} fusion(f32[1024,768]{1,0:T(8,128)S(1)} %fusion.1, bf16[1024,2560]{1,0:T(8,128)(2,1)S(1)} %bitcast.31, bf16[1,2560,768]{2,1,0:T(8,128)(2,1)S(1)} %copy-done.2), kind=kOutput, calls=%fused_computation.10 | convolution fusion | flops 4031250432 | bytes 13893632 | tf_op jit(solution)/shard_map/dot_general | solution.py:8
  89.7 0.0 copy-done.3
  89.7 6.0 %convolution_convert_fusion = bf16[1024,2560]{1,0:T(8,128)(2,1)} fusion(bf16[1024,768]{1,0:T(8,128)(2,1)S(1)} %multiply_convert_fusion, bf16[1,768,2560]{2,1,0:T(8,128)(2,1)S(1)} %copy-done.3), kind=kOutput, calls=%fused_computation.4 | convolution fusion | flops 4029153280 | bytes 10747904 | tf_op jit(solution)/shard_map/dot_general | solution.py:11
  95.7 0.0 copy-start
  95.7 5.0 %all-to-all-start.1 = ((bf16[8,128,2560]{2,1,0:T(8,128)(2,1)}), bf16[8,128,2560]{2,1,0:T(8,128)(2,1)}, u32[]{:S(2)}, u32[]{:S(2)}) async-start(bf16[8,128,2560]{2,1,0:T(8,128)(2,1)} %bitcast.29), calls=%async_computation.1 | async-start | bytes 10485760 | tf_op jit(solution)/shard_map/all_to_all | solution.py:49
  100.7 0.0 copy-done
  100.7 0.1 copy.10
  100.8 60.0 %all-to-all-done.1 = bf16[8,128,2560]{2,1,0:T(8,128)(2,1)} async-done(((bf16[8,128,2560]{2,1,0:T(8,128)(2,1)}), bf16[8,128,2560]{2,1,0:T(8,128)(2,1)}, u32[]{:S(2)}, u32[]{:S(2)}) %all-to-all-start.1) | async-done | bytes 5242912 | tf_op jit(solution)/shard_map/all_to_all | solution.py:49
  160.9 11.5 %gather_fusion.1 = bf16[768,2560]{1,0:T(8,128)(2,1)} fusion(bf16[1024,2560]{1,0:T(8,128)(2,1)} %bitcast.9, s32[1024]{0:T(1024)S(1)} %pad_clamp_fusion), kind=kCustom, calls=%fused_computation.1 | custom fusion | bytes 7867392 | tf_op jit(solution)/shard_map/gather | solution.py:51
  172.4 7.7 %reshape.85 = f32[128,6,2560]{2,1,0:T(8,128)} reshape(bf16[768,2560]{1,0:T(8,128)(2,1)} %gather_fusion.1) | data formatting | bytes 11796480 | tf_op jit(solution)/shard_map/convert_element_type | solution.py:73
  180.1 8.8 %multiply_reduce_fusion = bf16[128,2560]{1,0:T(8,128)(2,1)} fusion(f32[128,6,2560]{2,1,0:T(8,128)} %reshape.85, f32[128,6]{1,0:T(8,128)S(1)} %copy.10), kind=kLoop, calls=%fused_computation.3 | loop fusion | flops 3604480 | bytes 8522752 | tf_op jit(solution)/shard_map/reduce_sum | solution.py:76
  (6 shorter events, 0.1 us)
Async XLA Ops:
  15.2 65.7 %copy-start.1 = (bf16[1,2560,768]{2,1,0:T(8,128)(2,1)S(1)}, bf16[1,2560,768]{2,1,0:T(8,128)(2,1)}, u32[]{:S(2)}) copy-start(bf16[1,2560,768]{2,1,0:T(8,128)(2,1)} %param.10) | copy-start | bytes 11796484
  80.9 4.2 %copy-start.2 = (bf16[1,2560,768]{2,1,0:T(8,128)(2,1)S(1)}, bf16[1,2560,768]{2,1,0:T(8,128)(2,1)}, u32[]{:S(2)}) copy-start(bf16[1,2560,768]{2,1,0:T(8,128)(2,1)} %param.9) | copy-start | bytes 11796484
  85.1 4.5 %copy-start.3 = (bf16[1,768,2560]{2,1,0:T(8,128)(2,1)S(1)}, bf16[1,768,2560]{2,1,0:T(8,128)(2,1)}, u32[]{:S(2)}) copy-start(bf16[1,768,2560]{2,1,0:T(8,128)(2,1)} %param.11) | copy-start | bytes 11796484
  95.7 5.0 %copy-start = (f32[128,6]{0,1:T(8,128)S(1)}, f32[128,6]{0,1:T(8,128)}, u32[]{:S(2)}) copy-start(f32[128,6]{0,1:T(8,128)} %param.8) | copy-start | bytes 9220
  95.7 65.1 %all-to-all-start.1 = ((bf16[8,128,2560]{2,1,0:T(8,128)(2,1)}), bf16[8,128,2560]{2,1,0:T(8,128)(2,1)}, u32[]{:S(2)}, u32[]{:S(2)}) async-start(bf16[8,128,2560]{2,1,0:T(8,128)(2,1)} %bitcast.29), calls=%async_computation.1 | async-start | bytes 10485760 | tf_op jit(solution)/shard_map/all_to_all | solution.py:49
where the time goes:
time: 190 us; the launch traced here: 189 us
  blocking collectives  65.7 us (35%)
  waiting for transfers between devices  60 us (32%)
  local copies, waits for them, and re-layouts  31.8 us (17%)
  matrix products  14.8 us (8%)
  other arithmetic  11.5 us (6%)
  starting transfers between devices  4.95 us (3%)
    all_to_all x1, blocking collectives, dispatch_pairs(): lax.all_to_all(outgoing, 'expert', split_axis=0, concat_axis=0, tiled=True)  65.7 us
    all_to_all x1, waiting for transfers between devices, dispatch_pairs(): lax.all_to_all(answered, 'expert', split_axis=0, concat_axis=0, tiled=True)  60 us
    gather x1, local copies, waits for them, and re-layouts, dispatch_pairs(): return flat_back[jnp.minimum(places, buffer_rows - 1)]  11.5 us
    reduce_sum x1, other arithmetic, shards(): summed = jnp.sum(weighted, axis=1)  8.82 us
    convert_element_type x1, local copies, waits for them, and re-layouts, shards(): returned.astype(jnp.float32)  7.73 us
    gather x1, local copies, waits for them, and re-layouts, dispatch_pairs(): padded_source[slot_table].reshape(experts_all, slot_bound, features)  6.29 us
    dot_general x1, matrix products, expert_apply(): jnp.dot(hidden, down_matrix, preferred_element_type=jnp.float32)  6.04 us
    all_to_all x1, starting transfers between devices, dispatch_pairs(): lax.all_to_all(answered, 'expert', split_axis=0, concat_axis=0, tiled=True)  4.95 us
  transfers between devices with their start and end apart: 1, of which 1 were waited for; matrix products, arithmetic and copies ran while one was open for 0% of the time, Pallas kernels for 0%

commit v1 on v0

v1 whole, which is shorter than its diff:
```python
import functools

import jax
import jax.numpy as jnp
from jax import lax
from jax.experimental import pallas as pl
from jax.experimental.pallas import tpu as pltpu
from jax.sharding import PartitionSpec as P

CORE, X, Y = 1, 2, 4
LANES = 128
MIB = 2**20


def in_vmem(value):
    return pltpu.with_memory_space_constraint(value, pltpu.VMEM)


def whole():
    return pl.BlockSpec(memory_space=pltpu.VMEM)


def swap(value, offset):
    size = lax.axis_size("expert")
    return lax.ppermute(value, "expert", [(i, i ^ offset) for i in range(size)])


def pack_kernel(experts, tokens_ref, ids_ref, gates_ref, *out_refs):
    rows, features = tokens_ref.shape
    lane = lax.broadcasted_iota(jnp.int32, (rows, LANES), 1)
    expert = lane
    for _ in range(2):
        expert = jnp.where(expert >= experts, expert - experts, expert)
    weight = jnp.zeros((rows, LANES), jnp.float32)
    for k in range(ids_ref.shape[1]):
        weight += jnp.where(expert == ids_ref[:, k : k + 1], gates_ref[:, k : k + 1], 0.0)
    high = weight.astype(jnp.bfloat16).astype(jnp.float32)
    rest = weight - high
    middle = rest.astype(jnp.bfloat16).astype(jnp.float32)
    low = rest - middle
    terms = jnp.where(lane < experts, high, jnp.where(lane < 2 * experts, middle, low))
    terms = jnp.where(lane < 3 * experts, terms, 0.0).astype(jnp.bfloat16)
    start = 0
    for out_ref in out_refs:
        count = out_ref.shape[0]
        out_ref[:, :features] = tokens_ref[start : start + count, :]
        out_ref[:, features:] = terms[start : start + count, :]
        start += count


def pack(tokens, ids, gates, experts, parts):
    rows, features = tokens.shape
    shape = jax.ShapeDtypeStruct((rows // parts, features + LANES), tokens.dtype)
    return pl.pallas_call(
        functools.partial(pack_kernel, experts),
        out_shape=[shape] * parts,
        in_specs=[whole()] * 3,
        out_specs=[whole()] * parts,
        compiler_params=pltpu.CompilerParams(vmem_limit_bytes=16 * MIB),
        cost_estimate=pl.CostEstimate(flops=0, bytes_accessed=4 * rows * features, transcendentals=0),
        name="pack",
    )(tokens, ids, gates)


def expert_kernel(experts, count, has_before, *refs):
    index_ref, gate_ref, up_ref, down_ref = refs[:4]
    rows_refs = refs[4 : 4 + count]
    before_refs = refs[4 + count : 4 + 2 * count] if has_before else ()
    out_refs = refs[-1 - count : -1]
    hidden_ref = refs[-1]
    features, width = gate_ref.shape
    step = 256
    rows = jnp.concatenate([r[:, :features] for r in rows_refs], axis=0)
    terms = jnp.concatenate([r[:, features:] for r in rows_refs], axis=0).astype(jnp.float32)
    lane = lax.broadcasted_iota(jnp.int32, terms.shape, 1)
    own = index_ref[0]
    chosen = (lane == own) | (lane == own + experts) | (lane == own + 2 * experts)
    weight = jnp.sum(jnp.where(chosen, terms, 0.0), axis=1, keepdims=True)
    for at in range(0, width, step):
        gate = jnp.dot(rows, gate_ref[:, at : at + step], preferred_element_type=jnp.float32)
        up = jnp.dot(rows, up_ref[:, at : at + step], preferred_element_type=jnp.float32)
        hidden_ref[:, at : at + step] = (gate / (1.0 + jnp.exp(-gate)) * up).astype(jnp.bfloat16)
    hidden = hidden_ref[...]
    for at in range(0, features, 2 * step):
        columns = slice(at, at + 2 * step)
        answer = jnp.dot(hidden, down_ref[:, columns], preferred_element_type=jnp.float32) * weight
        start = 0
        for i, out_ref in enumerate(out_refs):
            stop = start + out_ref.shape[0]
            part = answer[start:stop]
            if has_before:
                part = part + before_refs[i][:, columns].astype(jnp.float32)
            out_ref[:, columns] = part.astype(out_ref.dtype)
            start = stop


def run_expert(weights, index, experts, rows, kinds, before=None):
    features, width = weights[0].shape
    total = sum(r.shape[0] for r in rows)
    operands = [in_vmem(w) for w in weights] + [in_vmem(r) for r in rows]
    if before is not None:
        operands += [in_vmem(b) for b in before]
    return pl.pallas_call(
        functools.partial(expert_kernel, experts, len(rows), before is not None),
        out_shape=[jax.ShapeDtypeStruct((r.shape[0], features), k) for r, k in zip(rows, kinds)],
        in_specs=[pl.BlockSpec(memory_space=pltpu.SMEM)] + [whole()] * len(operands),
        out_specs=[whole()] * len(rows),
        scratch_shapes=[pltpu.VMEM((total, width), jnp.bfloat16)],
        compiler_params=pltpu.CompilerParams(vmem_limit_bytes=16 * MIB),
        cost_estimate=pl.CostEstimate(
            flops=6 * total * features * width,
            bytes_accessed=total * features * 4,
            transcendentals=total * width,
        ),
        name="expert",
    )(index, *operands)


def sum_kernel(groups, *refs):
    out_ref = refs[-1]
    start = 0
    taken = 0
    for size, rows in groups:
        parts = [r[...].astype(jnp.float32) for r in refs[taken : taken + size]]
        total = parts[0]
        for part in parts[1:]:
            total = total + part
        out_ref[start : start + rows, :] = total.astype(out_ref.dtype)
        start += rows
        taken += size


def sums(groups):
    operands = [in_vmem(a) for group in groups for a in group]
    features = operands[0].shape[1]
    rows = sum(group[0].shape[0] for group in groups)
    return pl.pallas_call(
        functools.partial(sum_kernel, [(len(g), g[0].shape[0]) for g in groups]),
        out_shape=jax.ShapeDtypeStruct((rows, features), jnp.bfloat16),
        in_specs=[whole()] * len(operands),
        out_specs=whole(),
        compiler_params=pltpu.CompilerParams(vmem_limit_bytes=16 * MIB),
        cost_estimate=pl.CostEstimate(flops=rows * features, bytes_accessed=4 * rows * features, transcendentals=0),
        name="sums",
    )(*operands)


def on_four_chips(tokens, expert_ids, gate_values, w_gate, w_up, w_down):
    experts = lax.axis_size("expert")
    mine = lax.axis_index("expert").astype(jnp.int32).reshape(1)
    others = mine ^ CORE
    weights = (w_gate[0], w_up[0], w_down[0])
    own_a, own_b = pack(tokens, expert_ids, gate_values, experts, 2)
    x_a, y_a = swap(own_a, X), swap(own_a, Y)
    x_b, y_b = swap(own_b, X), swap(own_b, Y)
    far = tuple(swap(w, CORE) for w in weights)
    d_a, d_b = swap(x_a, Y), swap(y_b, X)

    wide, narrow = jnp.float32, jnp.bfloat16
    near_run = functools.partial(run_expert, weights, mine, experts)
    far_run = functools.partial(run_expert, far, others, experts)
    sum_own = near_run([own_a, own_b], [wide] * 2)
    first = near_run([x_a, y_a], [wide] * 2)
    second = near_run([x_b, y_b], [wide] * 2)
    sum_x_a, sum_y_a = far_run([x_a, y_a], [narrow, wide], first)
    sum_x_b, sum_y_b = far_run([x_b, y_b], [wide, narrow], second)
    back_x_a, back_y_b = swap(sum_x_a, X), swap(sum_y_b, Y)
    third = near_run([d_a, d_b], [wide] * 2)
    sum_d_a, sum_d_b = far_run([d_a, d_b], [narrow] * 2, third)
    via_x, via_y = swap(sum_d_a, X), swap(sum_d_b, Y)
    sum_own = far_run([own_a, own_b], [wide] * 2, sum_own)
    back_y_a = swap(sums([[sum_y_a, via_x]]), Y)
    back_x_b = swap(sums([[sum_x_b, via_y]]), X)
    return sums([[sum_own[0], back_x_a, back_y_a], [sum_own[1], back_x_b, back_y_b]])


def expert_apply(row_block, gate_matrix, up_matrix, down_matrix):
    gate_part = jnp.dot(row_block, gate_matrix, preferred_element_type=jnp.float32)
    up_part = jnp.dot(row_block, up_matrix, preferred_element_type=jnp.float32)
    hidden = (jax.nn.silu(gate_part) * up_part).astype(jnp.bfloat16)
    return jnp.dot(hidden, down_matrix, preferred_element_type=jnp.float32).astype(jnp.bfloat16)


def dispatched(tokens, expert_ids, gate_values, w_gate, w_up, w_down):
    token_count, features = tokens.shape
    topk_width = expert_ids.shape[1]
    experts_all = lax.axis_size("expert")
    pair_ids = expert_ids.reshape(-1)
    pair_rows = jnp.arange(pair_ids.shape[0], dtype=jnp.int32) // topk_width
    other_bound = min(
        token_count,
        ((topk_width - 1) * token_count + experts_all - 3) // (experts_all - 2) * 3 // 2,
    )
    slot_bound = max(token_count * 9 // 16, other_bound)
    one_hot = (pair_ids[:, None] == jnp.arange(experts_all, dtype=jnp.int32)[None, :]).astype(jnp.int32)
    earlier = jnp.cumsum(one_hot, axis=0) - one_hot
    places = pair_ids * slot_bound + jnp.sum(earlier * one_hot, axis=1)
    padded_source = jnp.concatenate([tokens, jnp.zeros((1, features), tokens.dtype)], axis=0)
    slot_table = (
        jnp.full((experts_all * slot_bound,), token_count, jnp.int32).at[places].set(pair_rows, mode="drop")
    )
    outgoing = padded_source[slot_table].reshape(experts_all, slot_bound, features)
    received = lax.all_to_all(outgoing, "expert", split_axis=0, concat_axis=0, tiled=True)
    answer = expert_apply(received.reshape(-1, features), w_gate[0], w_up[0], w_down[0])
    returned = lax.all_to_all(
        answer.reshape(received.shape), "expert", split_axis=0, concat_axis=0, tiled=True
    ).reshape(-1, features)[places]
    weighted = gate_values.reshape(-1)[:, None] * returned.astype(jnp.float32)
    return jnp.sum(weighted.reshape(token_count, topk_width, features), axis=1).astype(jnp.bfloat16)


def solution(mesh):
    placed = (
        P(("dp", "expert"), None),
        P(("dp", "expert"), None),
        P(("dp", "expert"), None),
        P("expert", None, None),
        P("expert", None, None),
        P("expert", None, None),
    )
    body = on_four_chips if mesh.shape["expert"] == 8 else dispatched
    return jax.shard_map(
        body, mesh=mesh, in_specs=placed, out_specs=P(("dp", "expert"), None), check_vma=False
    )
```

time: 190 us -> 77.2 us (0.41)
  blocking collectives: 65.7 us -> 0 us
  waiting for transfers between devices: 60 us -> 16.5 us
  Pallas kernels: 0 us -> 34 us
  local copies, waits for them, and re-layouts: 31.8 us -> 9.02 us
  matrix products: 14.8 us -> 0 us
  starting transfers between devices: 4.95 us -> 17.1 us
  other arithmetic: 11.5 us -> 0 us
    all_to_all x1 -> x0, blocking collectives: 65.7 us -> none  [dispatch_pairs(): lax.all_to_all(outgoing, 'expert', split_axis=0, concat_axis=0, tiled=True)]
    all_to_all x1 -> x0, waiting for transfers between devices: 60 us -> none  [dispatch_pairs(): lax.all_to_all(answered, 'expert', split_axis=0, concat_axis=0, tiled=True)]
    pallas_call x0 -> x12, Pallas kernels: none -> 34 us  [the longest x8 32.6 us: run_expert(): pl.pallas_call(functools.partial(expert_kernel, experts, len(rows), befor...]
    gather x2 -> x0, local copies, waits for them, and re-layouts: 17.8 us -> none  [the longest x1 11.5 us: dispatch_pairs(): return flat_back[jnp.minimum(places, buffer_rows - 1)]]
    ppermute x0 -> x15, starting transfers between devices: none -> 17.1 us  [swap(): return lax.ppermute(value, 'expert', [(i, i ^ offset) for i in range(size)])]
    ppermute x0 -> x15, waiting for transfers between devices: none -> 16.5 us  [swap(): return lax.ppermute(value, 'expert', [(i, i ^ offset) for i in range(size)])]
    dot_general x3 -> x0, matrix products: 14.8 us -> none  [the longest x1 6.04 us: expert_apply(): jnp.dot(hidden, down_matrix, preferred_element_type=jnp.float32)]
    reduce_sum x2 -> x0, other arithmetic: 8.91 us -> none  [the longest x1 8.82 us: shards(): summed = jnp.sum(weighted, axis=1)]
  transfers between devices with their start and end apart: 1 -> 15, of which waited for: 1 -> 3; matrix products, arithmetic and copies ran while one was open for 0% -> 2% of each run, Pallas kernels for 0% -> 43%
where the time goes in v1:
time: 77.2 us; the launch traced here: 76.8 us
  Pallas kernels  34 us (44%)
  starting transfers between devices  17.1 us (22%)
  waiting for transfers between devices  16.5 us (21%)
  local copies, waits for them, and re-layouts  9.02 us (12%)
    pallas_call x8, Pallas kernels, run_expert(): pl.pallas_call(functools.partial(expert_kernel, experts, len(rows), befor...  32.6 us
    ppermute x15, starting transfers between devices, swap(): return lax.ppermute(value, 'expert', [(i, i ^ offset) for i in range(size)])  17.1 us
    ppermute x15, waiting for transfers between devices, swap(): return lax.ppermute(value, 'expert', [(i, i ^ offset) for i in range(size)])  16.5 us
    unnamed x16, local copies, waits for them, and re-layouts  9.02 us
  transfers between devices with their start and end apart: 15, of which 3 were waited for; matrix products, arithmetic and copies ran while one was open for 2% of the time, Pallas kernels for 43%

profile of v1, /device:TPU:0, one launch (start us, length us, event | category | flops | bytes accessed | tf_op | source)
XLA Modules:
  0.0 76.8 jit_solution(10923056952717431820)
XLA Ops:
  0.0 0.5 collective-permute-start
  0.5 0.5 collective-permute-start.2
  1.0 0.8 %copy.7.ids_ref = s32[128,6]{1,0:T(8,128)S(1)} copy(s32[128,6]{0,1:T(8,128)} %param.7) | data formatting | bytes 6144 | tf_op args[1]
  1.8 0.8 %copy.8.gates_ref = f32[128,6]{1,0:T(8,128)S(1)} copy(f32[128,6]{0,1:T(8,128)} %param.8) | data formatting | bytes 6144 | tf_op args[2]
  2.6 1.1 %copy-done.6 = bf16[128,2560]{1,0:T(8,128)(2,1)S(1)} copy-done((bf16[128,2560]{1,0:T(8,128)(2,1)S(1)}, bf16[128,2560]{1,0:T(8,128)(2,1)}, u32[]{:S(2)}) %copy-start.6) | copy-done | bytes 655384
  3.9 2.6 %collective-permute-start.7 = (bf16[64,2688]{1,0:T(8,128)(2,1)S(1)}, bf16[64,2688]{1,0:T(8,128)(2,1)S(1)}, u32[]{:S(2)}, u32[]{:S(2)}) collective-permute-start(bf16[64,2688]{1,0:T(8,128)(2,1)S(1)} %get-tuple-element.24.refs_5_), channel_id=1, source_target_pairs={{0,4},{1,5},{2,6},{3,7},{4,0},{5,1},{6,2},{7,3},{8,12},{9,13},{10,... | collective-permute-start | bytes 1032200 | tf_op jit(solution)/shard_map/ppermute | solution.py:25
  6.5 1.5 %collective-permute-start.3 = (bf16[64,2688]{1,0:T(8,128)(2,1)S(1)}, bf16[64,2688]{1,0:T(8,128)(2,1)S(1)}, u32[]{:S(2)}, u32[]{:S(2)}) collective-permute-start(bf16[64,2688]{1,0:T(8,128)(2,1)S(1)} %get-tuple-element.23.refs_4_), channel_id=1, source_target_pairs={{0,2},{1,3},{2,0},{3,1},{4,6},{5,7},{6,4},{7,5},{8,10},{9,11},{10,... | collective-permute-start | bytes 1032200 | tf_op jit(solution)/shard_map/ppermute | solution.py:25
  8.0 7.2 %collective-permute-done.7.refs_5_ = bf16[64,2688]{1,0:T(8,128)(2,1)S(1)} collective-permute-done((bf16[64,2688]{1,0:T(8,128)(2,1)S(1)}, bf16[64,2688]{1,0:T(8,128)(2,1)S(1)}, u32[]{:S(2)}, u32[]{:S(2)}) %collective-permute-start.7) | collective-permute-done | bytes 344096 | tf_op jit(solution)/shard_map/ppermute | solution.py:25
  15.2 1.7 %collective-permute-start.11 = (bf16[64,2688]{1,0:T(8,128)(2,1)S(1)}, bf16[64,2688]{1,0:T(8,128)(2,1)S(1)}, u32[]{:S(2)}, u32[]{:S(2)}) collective-permute-start(bf16[64,2688]{1,0:T(8,128)(2,1)S(1)} %get-tuple-element.24.refs_5_), channel_id=1, source_target_pairs={{0,2},{1,3},{2,0},{3,1},{4,6},{5,7},{6,4},{7,5},{8,10},{9,11},{10,... | collective-permute-start | bytes 1032200 | tf_op jit(solution)/shard_map/ppermute | solution.py:25
  17.0 1.5 %collective-permute-start.6 = (bf16[64,2688]{1,0:T(8,128)(2,1)S(1)}, bf16[64,2688]{1,0:T(8,128)(2,1)S(1)}, u32[]{:S(2)}, u32[]{:S(2)}) collective-permute-start(bf16[64,2688]{1,0:T(8,128)(2,1)S(1)} %collective-permute-done.3.refs_4_), channel_id=1, source_target_pairs={{0,4},{1,5},{2,6},{3,7},{4,0},{5,1},{6,2},{7,3},{8,12},{9,13},{10,... | collective-permute-start | bytes 1032200 | tf_op jit(solution)/shard_map/ppermute | solution.py:25
  18.5 6.7 %collective-permute-done.11.refs_4_ = bf16[64,2688]{1,0:T(8,128)(2,1)S(1)} collective-permute-done((bf16[64,2688]{1,0:T(8,128)(2,1)S(1)}, bf16[64,2688]{1,0:T(8,128)(2,1)S(1)}, u32[]{:S(2)}, u32[]{:S(2)}) %collective-permute-start.11) | collective-permute-done | bytes 344096 | tf_op jit(solution)/shard_map/ppermute | solution.py:25
  25.1 1.5 %collective-permute-start.8 = (bf16[64,2688]{1,0:T(8,128)(2,1)S(1)}, bf16[64,2688]{1,0:T(8,128)(2,1)S(1)}, u32[]{:S(2)}, u32[]{:S(2)}) collective-permute-start(bf16[64,2688]{1,0:T(8,128)(2,1)S(1)} %collective-permute-done.7.refs_5_), channel_id=1, source_target_pairs={{0,2},{1,3},{2,0},{3,1},{4,6},{5,7},{6,4},{7,5},{8,10},{9,11},{10,... | collective-permute-start | bytes 1032200 | tf_op jit(solution)/shard_map/ppermute | solution.py:25
  26.7 1.5 %collective-permute-start.4 = (bf16[64,2688]{1,0:T(8,128)(2,1)S(1)}, bf16[64,2688]{1,0:T(8,128)(2,1)S(1)}, u32[]{:S(2)}, u32[]{:S(2)}) collective-permute-start(bf16[64,2688]{1,0:T(8,128)(2,1)S(1)} %get-tuple-element.23.refs_4_), channel_id=1, source_target_pairs={{0,4},{1,5},{2,6},{3,7},{4,0},{5,1},{6,2},{7,3},{8,12},{9,13},{10,... | collective-permute-start | bytes 1032200 | tf_op jit(solution)/shard_map/ppermute | solution.py:25
  28.2 2.1 %copy-done = bf16[1,2560,768]{2,1,0:T(8,128)(2,1)S(1)} copy-done((bf16[1,2560,768]{2,1,0:T(8,128)(2,1)S(1)}, bf16[1,2560,768]{2,1,0:T(8,128)(2,1)}, u32[]{:S(2)}) %copy-start) | copy-done | bytes 3932184
  30.3 2.1 %copy-done.2 = bf16[1,2560,768]{2,1,0:T(8,128)(2,1)S(1)} copy-done((bf16[1,2560,768]{2,1,0:T(8,128)(2,1)S(1)}, bf16[1,2560,768]{2,1,0:T(8,128)(2,1)}, u32[]{:S(2)}) %copy-start.2) | copy-done | bytes 3932184
  32.4 2.1 %copy-done.4 = bf16[1,768,2560]{2,1,0:T(8,128)(2,1)S(1)} copy-done((bf16[1,768,2560]{2,1,0:T(8,128)(2,1)S(1)}, bf16[1,768,2560]{2,1,0:T(8,128)(2,1)}, u32[]{:S(2)}) %copy-start.4) | copy-done | bytes 3932184
  34.5 1.8 %expert.14 = (f32[64,2560]{1,0:T(8,128)S(1)}, f32[64,2560]{1,0:T(8,128)S(1)}) custom-call(s32[1]{0:T(128)} %bitcast.refs_0_, bf16[2560,768]{1,0:T(8,128)(2,1)S(1)} %bitcast.5, bf16[2560,768]{1,0:T(8,128)(2,1)S(1)} %bitcast.10, bf16[768,2560]{1,0:T(8,128)(2,1)S(1)} %bitcast.15, bf16[64,2688]{1,0:T(8,128)(2,1)S(1)} %collective-permute-done.11.refs_4_, ...), custom_call_target="tpu_custom_call" | custom-call | flops 1509949440 | bytes 1310720 | tf_op jit(solution)/shard_map/expert/pallas_call | solution.py:103
  36.4 1.8 %expert.12 = (f32[64,2560]{1,0:T(8,128)S(1)}, f32[64,2560]{1,0:T(8,128)S(1)}) custom-call(s32[1]{0:T(128)} %bitcast.refs_0_, bf16[2560,768]{1,0:T(8,128)(2,1)S(1)} %bitcast.6, bf16[2560,768]{1,0:T(8,128)(2,1)S(1)} %bitcast.11, bf16[768,2560]{1,0:T(8,128)(2,1)S(1)} %bitcast.16, bf16[64,2688]{1,0:T(8,128)(2,1)S(1)} %collective-permute-done.6.refs_4_, ...), custom_call_target="tpu_custom_call" | custom-call | flops 1509949440 | bytes 1310720 | tf_op jit(solution)/shard_map/expert/pallas_call | solution.py:103
  38.2 6.4 %expert.13 = (bf16[64,2560]{1,0:T(8,128)(2,1)S(1)}, bf16[64,2560]{1,0:T(8,128)(2,1)S(1)}) custom-call(s32[1]{0:T(128)S(6)} %xor.3.refs_0_, bf16[2560,768]{1,0:T(8,128)(2,1)} %collective-permute-done.refs_1_, bf16[2560,768]{1,0:T(8,128)(2,1)} %collective-permute-done.1.refs_2_, bf16[768,2560]{1,0:T(8,128)(2,1)} %collective-permute-done.2.refs_3_, ...), custom_call_target="tpu_custom_call" | custom-call | flops 1509949440 | bytes 1310720 | tf_op jit(solution)/shard_map/expert/pallas_call | solution.py:103
  44.6 0.6 collective-permute-start.12
  45.2 0.9 %collective-permute-start.9 = (bf16[64,2560]{1,0:T(8,128)(2,1)S(1)}, bf16[64,2560]{1,0:T(8,128)(2,1)S(1)}, u32[]{:S(2)}, u32[]{:S(2)}) collective-permute-start(bf16[64,2560]{1,0:T(8,128)(2,1)S(1)} %get-tuple-element.34), channel_id=1, source_target_pairs={{0,2},{1,3},{2,0},{3,1},{4,6},{5,7},{6,4},{7,5},{8,10},{9,11},{10,... | collective-permute-start | bytes 983048 | tf_op jit(solution)/shard_map/ppermute | solution.py:25
  46.1 1.8 %expert.10 = (f32[64,2560]{1,0:T(8,128)S(1)}, f32[64,2560]{1,0:T(8,128)S(1)}) custom-call(s32[1]{0:T(128)} %bitcast.refs_0_, bf16[2560,768]{1,0:T(8,128)(2,1)S(1)} %bitcast.7, bf16[2560,768]{1,0:T(8,128)(2,1)S(1)} %bitcast.12, bf16[768,2560]{1,0:T(8,128)(2,1)S(1)} %bitcast.17, bf16[64,2688]{1,0:T(8,128)(2,1)S(1)} %collective-permute-done.3.refs_4_, ...), custom_call_target="tpu_custom_call" | custom-call | flops 1509949440 | bytes 1310720 | tf_op jit(solution)/shard_map/expert/pallas_call | solution.py:103
  47.9 6.2 %expert.15 = (f32[64,2560]{1,0:T(8,128)S(1)}, bf16[64,2560]{1,0:T(8,128)(2,1)S(1)}) custom-call(s32[1]{0:T(128)S(6)} %xor.3.refs_0_, bf16[2560,768]{1,0:T(8,128)(2,1)} %collective-permute-done.refs_1_, bf16[2560,768]{1,0:T(8,128)(2,1)} %collective-permute-done.1.refs_2_, bf16[768,2560]{1,0:T(8,128)(2,1)} %collective-permute-done.2.refs_3_, ...), custom_call_target="tpu_custom_call" | custom-call | flops 1509949440 | bytes 1310720 | tf_op jit(solution)/shard_map/expert/pallas_call | solution.py:103
  54.2 1.2 %collective-permute-start.14 = (bf16[64,2560]{1,0:T(8,128)(2,1)S(1)}, bf16[64,2560]{1,0:T(8,128)(2,1)S(1)}, u32[]{:S(2)}, u32[]{:S(2)}) collective-permute-start(bf16[64,2560]{1,0:T(8,128)(2,1)S(1)} %get-tuple-element.40), channel_id=1, source_target_pairs={{0,4},{1,5},{2,6},{3,7},{4,0},{5,1},{6,2},{7,3},{8,12},{9,13},{10,... | collective-permute-start | bytes 983048 | tf_op jit(solution)/shard_map/ppermute | solution.py:25
  55.4 6.3 %expert.11 = (bf16[64,2560]{1,0:T(8,128)(2,1)S(1)}, f32[64,2560]{1,0:T(8,128)S(1)}) custom-call(s32[1]{0:T(128)S(6)} %xor.3.refs_0_, bf16[2560,768]{1,0:T(8,128)(2,1)} %collective-permute-done.refs_1_, bf16[2560,768]{1,0:T(8,128)(2,1)} %collective-permute-done.1.refs_2_, bf16[768,2560]{1,0:T(8,128)(2,1)} %collective-permute-done.2.refs_3_, ...), custom_call_target="tpu_custom_call" | custom-call | flops 1509949440 | bytes 1310720 | tf_op jit(solution)/shard_map/expert/pallas_call | solution.py:103
  61.7 1.5 %collective-permute-start.5 = (bf16[64,2560]{1,0:T(8,128)(2,1)S(1)}, bf16[64,2560]{1,0:T(8,128)(2,1)S(1)}, u32[]{:S(2)}, u32[]{:S(2)}) collective-permute-start(bf16[64,2560]{1,0:T(8,128)(2,1)S(1)} %get-tuple-element.30), channel_id=1, source_target_pairs={{0,2},{1,3},{2,0},{3,1},{4,6},{5,7},{6,4},{7,5},{8,10},{9,11},{10,... | collective-permute-start | bytes 983048 | tf_op jit(solution)/shard_map/ppermute | solution.py:25
  63.3 0.6 collective-permute-start.13
  64.0 0.9 %collective-permute-start.10 = (bf16[64,2560]{1,0:T(8,128)(2,1)S(1)}, bf16[64,2560]{1,0:T(8,128)(2,1)S(1)}, u32[]{:S(2)}, u32[]{:S(2)}) collective-permute-start(bf16[64,2560]{1,0:T(8,128)(2,1)S(1)} %sums.3), channel_id=1, source_target_pairs={{0,4},{1,5},{2,6},{3,7},{4,0},{5,1},{6,2},{7,3},{8,12},{9,13},{10,... | collective-permute-start | bytes 983048 | tf_op jit(solution)/shard_map/ppermute | solution.py:25
  64.9 2.0 %expert.8 = (f32[64,2560]{1,0:T(8,128)S(1)}, f32[64,2560]{1,0:T(8,128)S(1)}) custom-call(s32[1]{0:T(128)} %bitcast.refs_0_, bf16[2560,768]{1,0:T(8,128)(2,1)S(1)} %bitcast.8, bf16[2560,768]{1,0:T(8,128)(2,1)S(1)} %bitcast.13, bf16[768,2560]{1,0:T(8,128)(2,1)S(1)} %bitcast.18, bf16[64,2688]{1,0:T(8,128)(2,1)S(1)} %get-tuple-element.23.refs_4_, ...), custom_call_target="tpu_custom_call" | custom-call | flops 1509949440 | bytes 1310720 | tf_op jit(solution)/shard_map/expert/pallas_call | solution.py:103
  66.9 6.2 %expert.9 = (f32[64,2560]{1,0:T(8,128)S(1)}, f32[64,2560]{1,0:T(8,128)S(1)}) custom-call(s32[1]{0:T(128)S(6)} %xor.3.refs_0_, bf16[2560,768]{1,0:T(8,128)(2,1)} %collective-permute-done.refs_1_, bf16[2560,768]{1,0:T(8,128)(2,1)} %collective-permute-done.1.refs_2_, bf16[768,2560]{1,0:T(8,128)(2,1)} %collective-permute-done.2.refs_3_, ...), custom_call_target="tpu_custom_call" | custom-call | flops 1509949440 | bytes 1310720 | tf_op jit(solution)/shard_map/expert/pallas_call | solution.py:103
  73.2 2.6 %collective-permute-done.13.refs_4_ = bf16[64,2560]{1,0:T(8,128)(2,1)S(1)} collective-permute-done((bf16[64,2560]{1,0:T(8,128)(2,1)S(1)}, bf16[64,2560]{1,0:T(8,128)(2,1)S(1)}, u32[]{:S(2)}, u32[]{:S(2)}) %collective-permute-start.13) | collective-permute-done | bytes 327712 | tf_op jit(solution)/shard_map/ppermute | solution.py:25
  75.8 1.0 %sums.5 = bf16[128,2560]{1,0:T(8,128)(2,1)} custom-call(f32[64,2560]{1,0:T(8,128)S(1)} %get-tuple-element.27.refs_0_, bf16[64,2560]{1,0:T(8,128)(2,1)S(1)} %collective-permute-done.5.refs_1_, bf16[64,2560]{1,0:T(8,128)(2,1)S(1)} %collective-permute-done.10.refs_2_, f32[64,2560]{1,0:T(8,128)S(1)} %get-tuple-element.35.refs_3_, ...), custom_call_target="tpu_custom_call" | custom-call | flops 327680 | bytes 1310720 | tf_op jit(solution)/shard_map/sums/pallas_call | solution.py:137
  (26 shorter events, 0.5 us)
Async XLA Ops:
  0.0 38.2 %collective-permute-start = (bf16[2560,768]{1,0:T(8,128)(2,1)}, bf16[2560,768]{1,0:T(8,128)(2,1)}, u32[]{:S(2)}, u32[]{:S(2)}) collective-permute-start(bf16[2560,768]{1,0:T(8,128)(2,1)} %bitcast.4), channel_id=1, source_target_pairs={{0,1},{1,0},{2,3},{3,2},{4,5},{5,4},{6,7},{7,6},{8,9},{9,8},{10,11... | collective-permute-start | bytes 11796488 | tf_op jit(solution)/shard_map/ppermute | solution.py:25
  0.5 37.7 %collective-permute-start.1 = (bf16[2560,768]{1,0:T(8,128)(2,1)}, bf16[2560,768]{1,0:T(8,128)(2,1)}, u32[]{:S(2)}, u32[]{:S(2)}) collective-permute-start(bf16[2560,768]{1,0:T(8,128)(2,1)} %bitcast.9), channel_id=1, source_target_pairs={{0,1},{1,0},{2,3},{3,2},{4,5},{5,4},{6,7},{7,6},{8,9},{9,8},{10,11... | collective-permute-start | bytes 11796488 | tf_op jit(solution)/shard_map/ppermute | solution.py:25
  0.5 37.7 %collective-permute-start.2 = (bf16[768,2560]{1,0:T(8,128)(2,1)}, bf16[768,2560]{1,0:T(8,128)(2,1)}, u32[]{:S(2)}, u32[]{:S(2)}) collective-permute-start(bf16[768,2560]{1,0:T(8,128)(2,1)} %bitcast.14), channel_id=1, source_target_pairs={{0,1},{1,0},{2,3},{3,2},{4,5},{5,4},{6,7},{7,6},{8,9},{9,8},{10,11... | collective-permute-start | bytes 11796488 | tf_op jit(solution)/shard_map/ppermute | solution.py:25
  2.5 1.1 %copy-start.6 = (bf16[128,2560]{1,0:T(8,128)(2,1)S(1)}, bf16[128,2560]{1,0:T(8,128)(2,1)}, u32[]{:S(2)}) copy-start(bf16[128,2560]{1,0:T(8,128)(2,1)} %tokens_ref.1) | copy-start | bytes 1966084
  3.9 11.3 %collective-permute-start.7 = (bf16[64,2688]{1,0:T(8,128)(2,1)S(1)}, bf16[64,2688]{1,0:T(8,128)(2,1)S(1)}, u32[]{:S(2)}, u32[]{:S(2)}) collective-permute-start(bf16[64,2688]{1,0:T(8,128)(2,1)S(1)} %get-tuple-element.24.refs_5_), channel_id=1, source_target_pairs={{0,4},{1,5},{2,6},{3,7},{4,0},{5,1},{6,2},{7,3},{8,12},{9,13},{10,... | collective-permute-start | bytes 1032200 | tf_op jit(solution)/shard_map/ppermute | solution.py:25
  6.5 10.4 %collective-permute-start.3 = (bf16[64,2688]{1,0:T(8,128)(2,1)S(1)}, bf16[64,2688]{1,0:T(8,128)(2,1)S(1)}, u32[]{:S(2)}, u32[]{:S(2)}) collective-permute-start(bf16[64,2688]{1,0:T(8,128)(2,1)S(1)} %get-tuple-element.23.refs_4_), channel_id=1, source_target_pairs={{0,2},{1,3},{2,0},{3,1},{4,6},{5,7},{6,4},{7,5},{8,10},{9,11},{10,... | collective-permute-start | bytes 1032200 | tf_op jit(solution)/shard_map/ppermute | solution.py:25
  15.2 9.9 %collective-permute-start.11 = (bf16[64,2688]{1,0:T(8,128)(2,1)S(1)}, bf16[64,2688]{1,0:T(8,128)(2,1)S(1)}, u32[]{:S(2)}, u32[]{:S(2)}) collective-permute-start(bf16[64,2688]{1,0:T(8,128)(2,1)S(1)} %get-tuple-element.24.refs_5_), channel_id=1, source_target_pairs={{0,2},{1,3},{2,0},{3,1},{4,6},{5,7},{6,4},{7,5},{8,10},{9,11},{10,... | collective-permute-start | bytes 1032200 | tf_op jit(solution)/shard_map/ppermute | solution.py:25
  17.0 9.7 %collective-permute-start.6 = (bf16[64,2688]{1,0:T(8,128)(2,1)S(1)}, bf16[64,2688]{1,0:T(8,128)(2,1)S(1)}, u32[]{:S(2)}, u32[]{:S(2)}) collective-permute-start(bf16[64,2688]{1,0:T(8,128)(2,1)S(1)} %collective-permute-done.3.refs_4_), channel_id=1, source_target_pairs={{0,4},{1,5},{2,6},{3,7},{4,0},{5,1},{6,2},{7,3},{8,12},{9,13},{10,... | collective-permute-start | bytes 1032200 | tf_op jit(solution)/shard_map/ppermute | solution.py:25
  25.1 11.2 %collective-permute-start.8 = (bf16[64,2688]{1,0:T(8,128)(2,1)S(1)}, bf16[64,2688]{1,0:T(8,128)(2,1)S(1)}, u32[]{:S(2)}, u32[]{:S(2)}) collective-permute-start(bf16[64,2688]{1,0:T(8,128)(2,1)S(1)} %collective-permute-done.7.refs_5_), channel_id=1, source_target_pairs={{0,2},{1,3},{2,0},{3,1},{4,6},{5,7},{6,4},{7,5},{8,10},{9,11},{10,... | collective-permute-start | bytes 1032200 | tf_op jit(solution)/shard_map/ppermute | solution.py:25
  26.7 19.5 %collective-permute-start.4 = (bf16[64,2688]{1,0:T(8,128)(2,1)S(1)}, bf16[64,2688]{1,0:T(8,128)(2,1)S(1)}, u32[]{:S(2)}, u32[]{:S(2)}) collective-permute-start(bf16[64,2688]{1,0:T(8,128)(2,1)S(1)} %get-tuple-element.23.refs_4_), channel_id=1, source_target_pairs={{0,4},{1,5},{2,6},{3,7},{4,0},{5,1},{6,2},{7,3},{8,12},{9,13},{10,... | collective-permute-start | bytes 1032200 | tf_op jit(solution)/shard_map/ppermute | solution.py:25
  28.2 2.1 %copy-start = (bf16[1,2560,768]{2,1,0:T(8,128)(2,1)S(1)}, bf16[1,2560,768]{2,1,0:T(8,128)(2,1)}, u32[]{:S(2)}) copy-start(bf16[1,2560,768]{2,1,0:T(8,128)(2,1)} %param.9) | copy-start | bytes 11796484
  30.3 2.1 %copy-start.2 = (bf16[1,2560,768]{2,1,0:T(8,128)(2,1)S(1)}, bf16[1,2560,768]{2,1,0:T(8,128)(2,1)}, u32[]{:S(2)}) copy-start(bf16[1,2560,768]{2,1,0:T(8,128)(2,1)} %param.10) | copy-start | bytes 11796484
  32.4 2.1 %copy-start.4 = (bf16[1,768,2560]{2,1,0:T(8,128)(2,1)S(1)}, bf16[1,768,2560]{2,1,0:T(8,128)(2,1)}, u32[]{:S(2)}) copy-start(bf16[1,768,2560]{2,1,0:T(8,128)(2,1)} %param.11) | copy-start | bytes 11796484
  38.2 7.9 %copy-start.1 = (bf16[1,2560,768]{2,1,0:T(8,128)(2,1)S(1)}, bf16[1,2560,768]{2,1,0:T(8,128)(2,1)}, u32[]{:S(2)}) copy-start(bf16[1,2560,768]{2,1,0:T(8,128)(2,1)} %param.9) | copy-start | bytes 11796484
  38.2 7.9 %copy-start.3 = (bf16[1,2560,768]{2,1,0:T(8,128)(2,1)S(1)}, bf16[1,2560,768]{2,1,0:T(8,128)(2,1)}, u32[]{:S(2)}) copy-start(bf16[1,2560,768]{2,1,0:T(8,128)(2,1)} %param.10) | copy-start | bytes 11796484
  38.2 7.9 %copy-start.5 = (bf16[1,768,2560]{2,1,0:T(8,128)(2,1)S(1)}, bf16[1,768,2560]{2,1,0:T(8,128)(2,1)}, u32[]{:S(2)}) copy-start(bf16[1,768,2560]{2,1,0:T(8,128)(2,1)} %param.11) | copy-start | bytes 11796484
  44.6 18.6 %collective-permute-start.12 = (bf16[64,2560]{1,0:T(8,128)(2,1)S(1)}, bf16[64,2560]{1,0:T(8,128)(2,1)S(1)}, u32[]{:S(2)}, u32[]{:S(2)}) collective-permute-start(bf16[64,2560]{1,0:T(8,128)(2,1)S(1)} %get-tuple-element.39), channel_id=1, source_target_pairs={{0,4},{1,5},{2,6},{3,7},{4,0},{5,1},{6,2},{7,3},{8,12},{9,13},{10,... | collective-permute-start | bytes 983048 | tf_op jit(solution)/shard_map/ppermute | solution.py:25
  45.2 18.7 %collective-permute-start.9 = (bf16[64,2560]{1,0:T(8,128)(2,1)S(1)}, bf16[64,2560]{1,0:T(8,128)(2,1)S(1)}, u32[]{:S(2)}, u32[]{:S(2)}) collective-permute-start(bf16[64,2560]{1,0:T(8,128)(2,1)S(1)} %get-tuple-element.34), channel_id=1, source_target_pairs={{0,2},{1,3},{2,0},{3,1},{4,6},{5,7},{6,4},{7,5},{8,10},{9,11},{10,... | collective-permute-start | bytes 983048 | tf_op jit(solution)/shard_map/ppermute | solution.py:25
  54.2 19.0 %collective-permute-start.14 = (bf16[64,2560]{1,0:T(8,128)(2,1)S(1)}, bf16[64,2560]{1,0:T(8,128)(2,1)S(1)}, u32[]{:S(2)}, u32[]{:S(2)}) collective-permute-start(bf16[64,2560]{1,0:T(8,128)(2,1)S(1)} %get-tuple-element.40), channel_id=1, source_target_pairs={{0,4},{1,5},{2,6},{3,7},{4,0},{5,1},{6,2},{7,3},{8,12},{9,13},{10,... | collective-permute-start | bytes 983048 | tf_op jit(solution)/shard_map/ppermute | solution.py:25
  61.7 11.5 %collective-permute-start.5 = (bf16[64,2560]{1,0:T(8,128)(2,1)S(1)}, bf16[64,2560]{1,0:T(8,128)(2,1)S(1)}, u32[]{:S(2)}, u32[]{:S(2)}) collective-permute-start(bf16[64,2560]{1,0:T(8,128)(2,1)S(1)} %get-tuple-element.30), channel_id=1, source_target_pairs={{0,2},{1,3},{2,0},{3,1},{4,6},{5,7},{6,4},{7,5},{8,10},{9,11},{10,... | collective-permute-start | bytes 983048 | tf_op jit(solution)/shard_map/ppermute | solution.py:25
  63.3 12.5 %collective-permute-start.13 = (bf16[64,2560]{1,0:T(8,128)(2,1)S(1)}, bf16[64,2560]{1,0:T(8,128)(2,1)S(1)}, u32[]{:S(2)}, u32[]{:S(2)}) collective-permute-start(bf16[64,2560]{1,0:T(8,128)(2,1)S(1)} %sums.4), channel_id=1, source_target_pairs={{0,2},{1,3},{2,0},{3,1},{4,6},{5,7},{6,4},{7,5},{8,10},{9,11},{10,... | collective-permute-start | bytes 983048 | tf_op jit(solution)/shard_map/ppermute | solution.py:25
  64.0 11.8 %collective-permute-start.10 = (bf16[64,2560]{1,0:T(8,128)(2,1)S(1)}, bf16[64,2560]{1,0:T(8,128)(2,1)S(1)}, u32[]{:S(2)}, u32[]{:S(2)}) collective-permute-start(bf16[64,2560]{1,0:T(8,128)(2,1)S(1)} %sums.3), channel_id=1, source_target_pairs={{0,4},{1,5},{2,6},{3,7},{4,0},{5,1},{6,2},{7,3},{8,12},{9,13},{10,... | collective-permute-start | bytes 983048 | tf_op jit(solution)/shard_map/ppermute | solution.py:25

commit v2 on v0

v2 whole, which is shorter than its diff:
```python
import functools

import jax
import jax.numpy as jnp
from jax import lax
from jax.experimental import pallas as pl
from jax.experimental.pallas import tpu as pltpu
from jax.sharding import PartitionSpec as P

CORE, X, Y = 1, 2, 4
FIRST, SECOND = (X, Y), (Y, X)
LANES = 128
STEP = 256
MIB = 2**20


def in_vmem(value):
    return pltpu.with_memory_space_constraint(value, pltpu.VMEM)


def in_hbm(value):
    return pltpu.with_memory_space_constraint(value, pltpu.HBM)


def anywhere():
    return pl.BlockSpec(memory_space=pl.ANY)


def whole():
    return pl.BlockSpec(memory_space=pltpu.VMEM)


def swap(value, offsets):
    size = lax.axis_size("expert")
    return lax.ppermute(value, "expert", [(i, i ^ offsets[i % 2]) for i in range(size)])


def pack_kernel(experts, tokens_ref, ids_ref, gates_ref, out_ref, ids, gates, done):
    rows, features = tokens_ref.shape
    copies = [
        pltpu.make_async_copy(ids_ref, ids, done.at[0]),
        pltpu.make_async_copy(gates_ref, gates, done.at[1]),
        pltpu.make_async_copy(tokens_ref, out_ref.at[:, pl.ds(0, features)], done.at[2]),
    ]
    for copy in copies:
        copy.start()
    copies[0].wait()
    copies[1].wait()
    line = lax.broadcasted_iota(jnp.int32, (LANES, rows), 0)
    expert = line
    for _ in range(2):
        expert = jnp.where(expert >= experts, expert - experts, expert)
    weight = jnp.zeros((LANES, rows), jnp.float32)
    for k in range(ids_ref.shape[0]):
        weight += jnp.where(expert == ids[k : k + 1, :], gates[k : k + 1, :], 0.0)
    high = weight.astype(jnp.bfloat16).astype(jnp.float32)
    rest = weight - high
    middle = rest.astype(jnp.bfloat16).astype(jnp.float32)
    low = rest - middle
    terms = jnp.where(line < experts, high, jnp.where(line < 2 * experts, middle, low))
    terms = jnp.where(line < 3 * experts, terms, 0.0)
    out_ref[:, features:] = terms.T.astype(jnp.bfloat16)
    copies[2].wait()


def pack(tokens, ids, gates, experts):
    rows, features = tokens.shape
    ids, gates = ids.T, gates.T
    return pl.pallas_call(
        functools.partial(pack_kernel, experts),
        out_shape=jax.ShapeDtypeStruct((rows, features + LANES), tokens.dtype),
        in_specs=[anywhere()] * 3,
        out_specs=whole(),
        scratch_shapes=[
            pltpu.VMEM(ids.shape, ids.dtype),
            pltpu.VMEM(gates.shape, gates.dtype),
            pltpu.SemaphoreType.DMA((3,)),
        ],
        compiler_params=pltpu.CompilerParams(vmem_limit_bytes=8 * MIB),
        cost_estimate=pl.CostEstimate(flops=0, bytes_accessed=4 * rows * features, transcendentals=0),
        name="pack",
    )(in_hbm(tokens), in_hbm(ids), in_hbm(gates))


def row_weights(rows_ref, experts, features, other):
    terms = rows_ref[:, features:].astype(jnp.float32)
    lane = lax.broadcasted_iota(jnp.int32, terms.shape, 1)
    own = lax.axis_index("expert") ^ other
    chosen = (lane == own) | (lane == own + experts) | (lane == own + 2 * experts)
    return jnp.sum(jnp.where(chosen, terms, 0.0), axis=1, keepdims=True)


def hidden_columns(rows, gate_ref, up_ref, columns):
    gate = jnp.dot(rows, gate_ref[:, columns], preferred_element_type=jnp.float32)
    up = jnp.dot(rows, up_ref[:, columns], preferred_element_type=jnp.float32)
    return (gate / (1.0 + jnp.exp(-gate)) * up).astype(jnp.bfloat16)


def own_kernel(experts, gate_hbm, up_hbm, down_hbm, rows_ref, out_ref, gate_ref, up_ref, down_ref, hidden_ref, done):
    features, width = gate_ref.shape
    copies = []
    for at in range(0, width, STEP):
        columns = pl.ds(at, STEP)
        copies.append((gate_hbm.at[:, columns], gate_ref.at[:, columns]))
        copies.append((up_hbm.at[:, columns], up_ref.at[:, columns]))
    for at in range(0, features, 2 * STEP):
        columns = pl.ds(at, 2 * STEP)
        copies.append((down_hbm.at[:, columns], down_ref.at[:, columns]))
    copies = [pltpu.make_async_copy(a, b, done.at[i]) for i, (a, b) in enumerate(copies)]
    for copy in copies:
        copy.start()
    waits = iter(copies)
    rows = rows_ref[:, :features]
    weight = row_weights(rows_ref, experts, features, 0)
    for at in range(0, width, STEP):
        next(waits).wait()
        next(waits).wait()
        columns = slice(at, at + STEP)
        hidden_ref[:, columns] = hidden_columns(rows, gate_ref, up_ref, columns)
    hidden = hidden_ref[...]
    for at in range(0, features, 2 * STEP):
        next(waits).wait()
        columns = slice(at, at + 2 * STEP)
        out_ref[:, columns] = jnp.dot(hidden, down_ref[:, columns], preferred_element_type=jnp.float32) * weight


def run_own(weights, experts, rows):
    features, width = weights[0].shape
    count = rows.shape[0]
    copies = 2 * (width // STEP) + features // (2 * STEP)
    return pl.pallas_call(
        functools.partial(own_kernel, experts),
        out_shape=[jax.ShapeDtypeStruct((count, features), jnp.float32)]
        + [jax.ShapeDtypeStruct(w.shape, w.dtype) for w in weights],
        in_specs=[anywhere()] * 3 + [whole()],
        out_specs=[whole()] * 4,
        scratch_shapes=[pltpu.VMEM((count, width), jnp.bfloat16), pltpu.SemaphoreType.DMA((copies,))],
        compiler_params=pltpu.CompilerParams(vmem_limit_bytes=8 * MIB),
        cost_estimate=expert_cost(count, features, width),
        name="own",
    )(*[in_hbm(w) for w in weights], in_vmem(rows))


def expert_cost(count, features, width):
    return pl.CostEstimate(
        flops=6 * count * features * width, bytes_accessed=count * features * 4, transcendentals=count * width
    )


def expert_kernel(experts, other, added, *refs):
    gate_ref, up_ref, down_ref, rows_ref = refs[:4]
    out_ref, hidden_ref = refs[-2:]
    features, width = gate_ref.shape
    rows = rows_ref[:, :features]
    weight = row_weights(rows_ref, experts, features, other)
    for at in range(0, width, STEP):
        columns = slice(at, at + STEP)
        hidden_ref[:, columns] = hidden_columns(rows, gate_ref, up_ref, columns)
    hidden = hidden_ref[...]
    for at in range(0, features, 2 * STEP):
        columns = slice(at, at + 2 * STEP)
        answer = jnp.dot(hidden, down_ref[:, columns], preferred_element_type=jnp.float32) * weight
        for ref in refs[4 : 4 + added]:
            answer = answer + ref[:, columns].astype(jnp.float32)
        out_ref[:, columns] = answer.astype(out_ref.dtype)


def expert_and_rows_kernel(experts, other, added, *refs):
    expert_kernel(experts, other, added, *refs[:-2], refs[-1])


def run_expert(weights, other, experts, rows, kind, added=(), after=(), rows_too=False):
    features, width = weights[0].shape
    count = rows.shape[0]
    operands = [in_vmem(w) for w in (*weights, rows, *added)]
    specs = [whole()] * len(operands) + [anywhere()] * len(after)
    shapes = [jax.ShapeDtypeStruct((count, features), kind)]
    if rows_too:
        shapes.append(jax.ShapeDtypeStruct(rows.shape, rows.dtype))
    results = pl.pallas_call(
        functools.partial(expert_and_rows_kernel if rows_too else expert_kernel, experts, other, len(added)),
        out_shape=shapes,
        in_specs=specs,
        out_specs=[whole()] * len(shapes),
        input_output_aliases={3: 1} if rows_too else {},
        scratch_shapes=[pltpu.VMEM((count, width), jnp.bfloat16)],
        compiler_params=pltpu.CompilerParams(vmem_limit_bytes=8 * MIB),
        cost_estimate=expert_cost(count, features, width),
        name="expert",
    )(*operands, *after)
    return results if rows_too else results[0]


def sum_kernel(count, *refs):
    total = refs[0][...].astype(jnp.float32)
    for ref in refs[1:count]:
        total = total + ref[...].astype(jnp.float32)
    refs[-1][...] = total.astype(refs[-1].dtype)


def sums(*parts, after=()):
    rows, features = parts[0].shape
    return pl.pallas_call(
        functools.partial(sum_kernel, len(parts)),
        out_shape=jax.ShapeDtypeStruct((rows, features), jnp.bfloat16),
        in_specs=[whole()] * len(parts) + [anywhere()] * len(after),
        out_specs=whole(),
        compiler_params=pltpu.CompilerParams(vmem_limit_bytes=8 * MIB),
        cost_estimate=pl.CostEstimate(flops=rows * features, bytes_accessed=4 * rows * features, transcendentals=0),
        name="sums",
    )(*[in_vmem(p) for p in parts], *after)


def on_four_chips(tokens, expert_ids, gate_values, w_gate, w_up, w_down):
    experts = lax.axis_size("expert")
    weights = (w_gate[0], w_up[0], w_down[0])
    far = tuple(swap(w, (CORE, CORE)) for w in weights)
    own = pack(tokens, expert_ids, gate_values, experts)
    first = swap(own, FIRST)
    second = swap(own, SECOND)

    wide, narrow = jnp.float32, jnp.bfloat16
    near_own, *near = run_own(weights, experts, own)
    near_run = functools.partial(run_expert, near, 0, experts)
    far_run = functools.partial(run_expert, far, CORE, experts)
    near_first, first = near_run(first, wide, after=[near_own], rows_too=True)
    third = swap(first, SECOND)
    near_second = near_run(second, wide, after=[near_first])
    sum_second = far_run(second, narrow, [near_second])
    back_second = swap(sum_second, SECOND)
    near_third = near_run(third, wide, after=[sum_second])
    sum_third = far_run(third, narrow, [near_third])
    passed = swap(sum_third, SECOND)
    sum_first = far_run(first, wide, [near_first], after=[sum_third])
    sum_own = far_run(own, wide, [near_own, back_second], after=[sum_first])
    back_first = swap(sums(sum_first, passed, after=[sum_own]), FIRST)
    return sums(sum_own, back_first)


def expert_apply(row_block, gate_matrix, up_matrix, down_matrix):
    gate_part = jnp.dot(row_block, gate_matrix, preferred_element_type=jnp.float32)
    up_part = jnp.dot(row_block, up_matrix, preferred_element_type=jnp.float32)
    hidden = (jax.nn.silu(gate_part) * up_part).astype(jnp.bfloat16)
    return jnp.dot(hidden, down_matrix, preferred_element_type=jnp.float32).astype(jnp.bfloat16)


def dispatched(tokens, expert_ids, gate_values, w_gate, w_up, w_down):
    token_count, features = tokens.shape
    topk_width = expert_ids.shape[1]
    experts_all = lax.axis_size("expert")
    pair_ids = expert_ids.reshape(-1)
    pair_rows = jnp.arange(pair_ids.shape[0], dtype=jnp.int32) // topk_width
    other_bound = min(
        token_count,
        ((topk_width - 1) * token_count + experts_all - 3) // (experts_all - 2) * 3 // 2,
    )
    slot_bound = max(token_count * 9 // 16, other_bound)
    one_hot = (pair_ids[:, None] == jnp.arange(experts_all, dtype=jnp.int32)[None, :]).astype(jnp.int32)
    earlier = jnp.cumsum(one_hot, axis=0) - one_hot
    places = pair_ids * slot_bound + jnp.sum(earlier * one_hot, axis=1)
    padded_source = jnp.concatenate([tokens, jnp.zeros((1, features), tokens.dtype)], axis=0)
    slot_table = (
        jnp.full((experts_all * slot_bound,), token_count, jnp.int32).at[places].set(pair_rows, mode="drop")
    )
    outgoing = padded_source[slot_table].reshape(experts_all, slot_bound, features)
    received = lax.all_to_all(outgoing, "expert", split_axis=0, concat_axis=0, tiled=True)
    answer = expert_apply(received.reshape(-1, features), w_gate[0], w_up[0], w_down[0])
    returned = lax.all_to_all(
        answer.reshape(received.shape), "expert", split_axis=0, concat_axis=0, tiled=True
    ).reshape(-1, features)[places]
    weighted = gate_values.reshape(-1)[:, None] * returned.astype(jnp.float32)
    return jnp.sum(weighted.reshape(token_count, topk_width, features), axis=1).astype(jnp.bfloat16)


def solution(mesh):
    placed = (
        P(("dp", "expert"), None),
        P(("dp", "expert"), None),
        P(("dp", "expert"), None),
        P("expert", None, None),
        P("expert", None, None),
        P("expert", None, None),
    )
    body = on_four_chips if mesh.shape["expert"] == 8 else dispatched
    return jax.shard_map(
        body, mesh=mesh, in_specs=placed, out_specs=P(("dp", "expert"), None), check_vma=False
    )
```

time: 190 us -> 59.5 us (0.31)
  blocking collectives: 65.7 us -> 0 us
  waiting for transfers between devices: 60 us -> 27.3 us
  local copies, waits for them, and re-layouts: 31.8 us -> 0 us
  Pallas kernels: 0 us -> 20 us
  matrix products: 14.8 us -> 0 us
  other arithmetic: 11.5 us -> 0 us
  starting transfers between devices: 4.95 us -> 11.9 us
    all_to_all x1 -> x0, blocking collectives: 65.7 us -> none  [dispatch_pairs(): lax.all_to_all(outgoing, 'expert', split_axis=0, concat_axis=0, tiled=True)]
    all_to_all x1 -> x0, waiting for transfers between devices: 60 us -> none  [dispatch_pairs(): lax.all_to_all(answered, 'expert', split_axis=0, concat_axis=0, tiled=True)]
    ppermute x0 -> x9, waiting for transfers between devices: none -> 27.3 us  [swap(): lax.ppermute(value, 'expert', [(i, i ^ offsets[i % 2]) for i in range(siz...]
    pallas_call x0 -> x11, Pallas kernels: none -> 20 us  [the longest x7 12.4 us: run_expert(): pl.pallas_call(functools.partial(expert_and_rows_kernel if rows_too else...]
    gather x2 -> x0, local copies, waits for them, and re-layouts: 17.8 us -> none  [the longest x1 11.5 us: dispatch_pairs(): return flat_back[jnp.minimum(places, buffer_rows - 1)]]
    dot_general x3 -> x0, matrix products: 14.8 us -> none  [the longest x1 6.04 us: expert_apply(): jnp.dot(hidden, down_matrix, preferred_element_type=jnp.float32)]
    ppermute x0 -> x9, starting transfers between devices: none -> 11.9 us  [swap(): lax.ppermute(value, 'expert', [(i, i ^ offsets[i % 2]) for i in range(siz...]
    reduce_sum x2 -> x0, other arithmetic: 8.91 us -> none  [the longest x1 8.82 us: shards(): summed = jnp.sum(weighted, axis=1)]
  transfers between devices with their start and end apart: 1 -> 9, of which waited for: 1 -> 4; matrix products, arithmetic and copies ran while one was open for 0% -> 0% of each run, Pallas kernels for 0% -> 32%
where the time goes in v2:
time: 59.5 us; the launch traced here: 59.3 us
  waiting for transfers between devices  27.3 us (46%)
  Pallas kernels  20 us (34%)
  starting transfers between devices  11.9 us (20%)
    ppermute x9, waiting for transfers between devices, swap(): lax.ppermute(value, 'expert', [(i, i ^ offsets[i % 2]) for i in range(siz...  27.3 us
    pallas_call x7, Pallas kernels, run_expert(): pl.pallas_call(functools.partial(expert_and_rows_kernel if rows_too else...  12.4 us
    ppermute x9, starting transfers between devices, swap(): lax.ppermute(value, 'expert', [(i, i ^ offsets[i % 2]) for i in range(siz...  11.9 us
    pallas_call x1, Pallas kernels, run_own(): pl.pallas_call(functools.partial(own_kernel, experts), out_shape=[jax.Sha...  5.39 us
  transfers between devices with their start and end apart: 9, of which 4 were waited for; matrix products, arithmetic and copies ran while one was open for 0% of the time, Pallas kernels for 32%

profile of v2, /device:TPU:0, one launch (start us, length us, event | category | flops | bytes accessed | tf_op | source)
XLA Modules:
  0.0 59.3 jit_solution(11474636751711204033)
XLA Ops:
  0.0 0.5 collective-permute-start
  0.5 0.1 collective-permute-start.1
  0.5 0.5 collective-permute-start.2
  1.0 1.1 %pack.1.rows_ref.refs_3_ = bf16[128,2688]{1,0:T(8,128)(2,1)S(1)} custom-call(bf16[128,2560]{1,0:T(8,128)(2,1)} %tokens_ref.1, s32[6,128]{1,0:T(8,128)} %bitcast.11, f32[6,128]{1,0:T(8,128)} %bitcast.12), custom_call_target="tpu_custom_call" | custom-call | bytes 1310720 | tf_op jit(solution)/shard_map/pack/pallas_call | solution.py:69
  2.1 2.6 %collective-permute-start.4 = (bf16[128,2688]{1,0:T(8,128)(2,1)S(1)}, bf16[128,2688]{1,0:T(8,128)(2,1)S(1)}, u32[]{:S(2)}, u32[]{:S(2)}) collective-permute-start(bf16[128,2688]{1,0:T(8,128)(2,1)S(1)} %pack.1.rows_ref.refs_3_), channel_id=1, source_target_pairs={{0,2},{1,5},{2,0},{3,7},{4,6},{5,1},{6,4},{7,3},{8,10},{9,13},{10,... | collective-permute-start | bytes 2064392 | tf_op jit(solution)/shard_map/ppermute | solution.py:35
  4.7 1.5 %collective-permute-start.3 = (bf16[128,2688]{1,0:T(8,128)(2,1)S(1)}, bf16[128,2688]{1,0:T(8,128)(2,1)S(1)}, u32[]{:S(2)}, u32[]{:S(2)}) collective-permute-start(bf16[128,2688]{1,0:T(8,128)(2,1)S(1)} %pack.1.rows_ref.refs_3_), channel_id=1, source_target_pairs={{0,4},{1,3},{2,6},{3,1},{4,0},{5,7},{6,2},{7,5},{8,12},{9,11},{10,... | collective-permute-start | bytes 2064392 | tf_op jit(solution)/shard_map/ppermute | solution.py:35
  6.2 5.4 %own.1 = (f32[128,2560]{1,0:T(8,128)S(1)}, bf16[2560,768]{1,0:T(8,128)(2,1)S(1)}, bf16[2560,768]{1,0:T(8,128)(2,1)S(1)}, bf16[768,2560]{1,0:T(8,128)(2,1)S(1)}) custom-call(bf16[2560,768]{1,0:T(8,128)(2,1)} %bitcast.6, bf16[2560,768]{1,0:T(8,128)(2,1)} %bitcast.8, bf16[768,2560]{1,0:T(8,128)(2,1)} %bitcast.10, bf16[128,2688]{1,0:T(8,128)(2,1)S(1)} %pack.1.rows_ref.refs_3_), custom_call_target="tpu_custom_call" | custom-call | flops 1509949440 | bytes 1310720 | tf_op jit(solution)/shard_map/own/pallas_call | solution.py:131
  11.6 8.2 %collective-permute-done.4.refs_3_ = bf16[128,2688]{1,0:T(8,128)(2,1)S(1)} collective-permute-done((bf16[128,2688]{1,0:T(8,128)(2,1)S(1)}, bf16[128,2688]{1,0:T(8,128)(2,1)S(1)}, u32[]{:S(2)}, u32[]{:S(2)}) %collective-permute-start.4) | collective-permute-done | bytes 688160 | tf_op jit(solution)/shard_map/ppermute | solution.py:35
  19.8 1.8 %expert.7 = (f32[128,2560]{1,0:T(8,128)S(1)}, bf16[128,2688]{1,0:T(8,128)(2,1)S(1)}) custom-call(bf16[2560,768]{1,0:T(8,128)(2,1)S(1)} %get-tuple-element.12.refs_0_, bf16[2560,768]{1,0:T(8,128)(2,1)S(1)} %get-tuple-element.13.refs_1_, bf16[768,2560]{1,0:T(8,128)(2,1)S(1)} %get-tuple-element.14.refs_2_, ...), custom_call_target="tpu_custom_call", output_to_operand_aliasing={{1}: (3, {})} | custom-call | flops 1509949440 | bytes 1310720 | tf_op jit(solution)/shard_map/expert/pallas_call | solution.py:180
  21.5 2.9 %collective-permute-start.6 = (bf16[128,2688]{1,0:T(8,128)(2,1)S(1)}, bf16[128,2688]{1,0:T(8,128)(2,1)S(1)}, u32[]{:S(2)}, u32[]{:S(2)}) collective-permute-start(bf16[128,2688]{1,0:T(8,128)(2,1)S(1)} %get-tuple-element.16.refs_3_), channel_id=1, source_target_pairs={{0,4},{1,3},{2,6},{3,1},{4,0},{5,7},{6,2},{7,5},{8,12},{9,11},{10,... | collective-permute-start | bytes 2064392 | tf_op jit(solution)/shard_map/ppermute | solution.py:35
  24.5 0.0 collective-permute-done.3.refs_3_
  24.5 1.8 %expert.8.refs_4_ = f32[128,2560]{1,0:T(8,128)S(1)} custom-call(bf16[2560,768]{1,0:T(8,128)(2,1)S(1)} %get-tuple-element.12.refs_0_, bf16[2560,768]{1,0:T(8,128)(2,1)S(1)} %get-tuple-element.13.refs_1_, bf16[768,2560]{1,0:T(8,128)(2,1)S(1)} %get-tuple-element.14.refs_2_, bf16[128,2688]{1,0:T(8,128)(2,1)S(1)} %collective-permute-done.3.refs_3_, ...), custom_call_target="tpu_custom_call" | custom-call | flops 1509949440 | bytes 1310720 | tf_op jit(solution)/shard_map/expert/pallas_call | solution.py:180
  26.2 0.0 collective-permute-done.refs_0_
  26.2 0.0 collective-permute-done.1.refs_1_
  26.3 0.0 collective-permute-done.2.refs_2_
  26.3 1.8 %expert.9.refs_4_ = bf16[128,2560]{1,0:T(8,128)(2,1)S(1)} custom-call(bf16[2560,768]{1,0:T(8,128)(2,1)S(1)} %collective-permute-done.refs_0_, bf16[2560,768]{1,0:T(8,128)(2,1)S(1)} %collective-permute-done.1.refs_1_, bf16[768,2560]{1,0:T(8,128)(2,1)S(1)} %collective-permute-done.2.refs_2_, bf16[128,2688]{1,0:T(8,128)(2,1)S(1)} %collective-permute-done.3.refs_3_, ...), custom_call_target="tpu_custom_call" | custom-call | flops 1509949440 | bytes 1310720 | tf_op jit(solution)/shard_map/expert/pallas_call | solution.py:180
  28.0 0.1 collective-permute-start.5
  28.1 5.2 %collective-permute-done.6.refs_3_ = bf16[128,2688]{1,0:T(8,128)(2,1)S(1)} collective-permute-done((bf16[128,2688]{1,0:T(8,128)(2,1)S(1)}, bf16[128,2688]{1,0:T(8,128)(2,1)S(1)}, u32[]{:S(2)}, u32[]{:S(2)}) %collective-permute-start.6) | collective-permute-done | bytes 688160 | tf_op jit(solution)/shard_map/ppermute | solution.py:35
  33.4 1.8 %expert.10.refs_4_ = f32[128,2560]{1,0:T(8,128)S(1)} custom-call(bf16[2560,768]{1,0:T(8,128)(2,1)S(1)} %get-tuple-element.12.refs_0_, bf16[2560,768]{1,0:T(8,128)(2,1)S(1)} %get-tuple-element.13.refs_1_, bf16[768,2560]{1,0:T(8,128)(2,1)S(1)} %get-tuple-element.14.refs_2_, bf16[128,2688]{1,0:T(8,128)(2,1)S(1)} %collective-permute-done.6.refs_3_, ...), custom_call_target="tpu_custom_call" | custom-call | flops 1509949440 | bytes 1310720 | tf_op jit(solution)/shard_map/expert/pallas_call | solution.py:180
  35.1 1.8 %expert.11.refs_5_ = bf16[128,2560]{1,0:T(8,128)(2,1)S(1)} custom-call(bf16[2560,768]{1,0:T(8,128)(2,1)S(1)} %collective-permute-done.refs_0_, bf16[2560,768]{1,0:T(8,128)(2,1)S(1)} %collective-permute-done.1.refs_1_, bf16[768,2560]{1,0:T(8,128)(2,1)S(1)} %collective-permute-done.2.refs_2_, bf16[128,2688]{1,0:T(8,128)(2,1)S(1)} %collective-permute-done.6.refs_3_, ...), custom_call_target="tpu_custom_call" | custom-call | flops 1509949440 | bytes 1310720 | tf_op jit(solution)/shard_map/expert/pallas_call | solution.py:180
  36.9 2.1 %collective-permute-start.7 = (bf16[128,2560]{1,0:T(8,128)(2,1)S(1)}, bf16[128,2560]{1,0:T(8,128)(2,1)S(1)}, u32[]{:S(2)}, u32[]{:S(2)}) collective-permute-start(bf16[128,2560]{1,0:T(8,128)(2,1)S(1)} %expert.11.refs_5_), channel_id=1, source_target_pairs={{0,4},{1,3},{2,6},{3,1},{4,0},{5,7},{6,2},{7,5},{8,12},{9,11},{10,... | collective-permute-start | bytes 1966088 | tf_op jit(solution)/shard_map/ppermute | solution.py:35
  39.0 1.8 %expert.12.refs_6_.refs_0_ = f32[128,2560]{1,0:T(8,128)S(1)} custom-call(bf16[2560,768]{1,0:T(8,128)(2,1)S(1)} %collective-permute-done.refs_0_, bf16[2560,768]{1,0:T(8,128)(2,1)S(1)} %collective-permute-done.1.refs_1_, bf16[768,2560]{1,0:T(8,128)(2,1)S(1)} %collective-permute-done.2.refs_2_, bf16[128,2688]{1,0:T(8,128)(2,1)S(1)} %get-tuple-element.16.refs_3_, ...), custom_call_target="tpu_custom_call" | custom-call | flops 1509949440 | bytes 1310720 | tf_op jit(solution)/shard_map/expert/pallas_call | solution.py:180
  40.8 0.0 collective-permute-done.5.refs_5_
  40.8 1.8 %expert.13.refs_2_.refs_0_ = f32[128,2560]{1,0:T(8,128)S(1)} custom-call(bf16[2560,768]{1,0:T(8,128)(2,1)S(1)} %collective-permute-done.refs_0_, bf16[2560,768]{1,0:T(8,128)(2,1)S(1)} %collective-permute-done.1.refs_1_, bf16[768,2560]{1,0:T(8,128)(2,1)S(1)} %collective-permute-done.2.refs_2_, bf16[128,2688]{1,0:T(8,128)(2,1)S(1)} %pack.1.rows_ref.refs_3_, ...), custom_call_target="tpu_custom_call" | custom-call | flops 1509949440 | bytes 1310720 | tf_op jit(solution)/shard_map/expert/pallas_call | solution.py:180
  42.6 5.0 %collective-permute-done.7.refs_1_ = bf16[128,2560]{1,0:T(8,128)(2,1)S(1)} collective-permute-done((bf16[128,2560]{1,0:T(8,128)(2,1)S(1)}, bf16[128,2560]{1,0:T(8,128)(2,1)S(1)}, u32[]{:S(2)}, u32[]{:S(2)}) %collective-permute-start.7) | collective-permute-done | bytes 655392 | tf_op jit(solution)/shard_map/ppermute | solution.py:35
  47.6 0.1 sums.2
  47.7 1.7 %collective-permute-start.8 = (bf16[128,2560]{1,0:T(8,128)(2,1)S(1)}, bf16[128,2560]{1,0:T(8,128)(2,1)S(1)}, u32[]{:S(2)}, u32[]{:S(2)}) collective-permute-start(bf16[128,2560]{1,0:T(8,128)(2,1)S(1)} %sums.2), channel_id=1, source_target_pairs={{0,2},{1,5},{2,0},{3,7},{4,6},{5,1},{6,4},{7,3},{8,10},{9,13},{10,... | collective-permute-start | bytes 1966088 | tf_op jit(solution)/shard_map/ppermute | solution.py:35
  49.4 8.9 %collective-permute-done.8.refs_1_ = bf16[128,2560]{1,0:T(8,128)(2,1)S(1)} collective-permute-done((bf16[128,2560]{1,0:T(8,128)(2,1)S(1)}, bf16[128,2560]{1,0:T(8,128)(2,1)S(1)}, u32[]{:S(2)}, u32[]{:S(2)}) %collective-permute-start.8) | collective-permute-done | bytes 655392 | tf_op jit(solution)/shard_map/ppermute | solution.py:35
  58.4 0.9 %sums.3 = bf16[128,2560]{1,0:T(8,128)(2,1)} custom-call(f32[128,2560]{1,0:T(8,128)S(1)} %expert.13.refs_2_.refs_0_, bf16[128,2560]{1,0:T(8,128)(2,1)S(1)} %collective-permute-done.8.refs_1_), custom_call_target="tpu_custom_call" | custom-call | flops 327680 | bytes 1310720 | tf_op jit(solution)/shard_map/sums/pallas_call | solution.py:203
Async XLA Ops:
  0.0 26.2 %collective-permute-start = (bf16[2560,768]{1,0:T(8,128)(2,1)}, bf16[2560,768]{1,0:T(8,128)(2,1)S(1)}, u32[]{:S(2)}, u32[]{:S(2)}) collective-permute-start(bf16[2560,768]{1,0:T(8,128)(2,1)} %bitcast.5), channel_id=1, source_target_pairs={{0,1},{1,0},{2,3},{3,2},{4,5},{5,4},{6,7},{7,6},{8,9},{9,8},{10,11... | collective-permute-start | bytes 11796488 | tf_op jit(solution)/shard_map/ppermute | solution.py:35
  0.5 25.8 %collective-permute-start.1 = (bf16[2560,768]{1,0:T(8,128)(2,1)}, bf16[2560,768]{1,0:T(8,128)(2,1)S(1)}, u32[]{:S(2)}, u32[]{:S(2)}) collective-permute-start(bf16[2560,768]{1,0:T(8,128)(2,1)} %bitcast.7), channel_id=1, source_target_pairs={{0,1},{1,0},{2,3},{3,2},{4,5},{5,4},{6,7},{7,6},{8,9},{9,8},{10,11... | collective-permute-start | bytes 11796488 | tf_op jit(solution)/shard_map/ppermute | solution.py:35
  0.5 25.8 %collective-permute-start.2 = (bf16[768,2560]{1,0:T(8,128)(2,1)}, bf16[768,2560]{1,0:T(8,128)(2,1)S(1)}, u32[]{:S(2)}, u32[]{:S(2)}) collective-permute-start(bf16[768,2560]{1,0:T(8,128)(2,1)} %bitcast.9), channel_id=1, source_target_pairs={{0,1},{1,0},{2,3},{3,2},{4,5},{5,4},{6,7},{7,6},{8,9},{9,8},{10,11... | collective-permute-start | bytes 11796488 | tf_op jit(solution)/shard_map/ppermute | solution.py:35
  2.1 17.6 %collective-permute-start.4 = (bf16[128,2688]{1,0:T(8,128)(2,1)S(1)}, bf16[128,2688]{1,0:T(8,128)(2,1)S(1)}, u32[]{:S(2)}, u32[]{:S(2)}) collective-permute-start(bf16[128,2688]{1,0:T(8,128)(2,1)S(1)} %pack.1.rows_ref.refs_3_), channel_id=1, source_target_pairs={{0,2},{1,5},{2,0},{3,7},{4,6},{5,1},{6,4},{7,3},{8,10},{9,13},{10,... | collective-permute-start | bytes 2064392 | tf_op jit(solution)/shard_map/ppermute | solution.py:35
  4.7 19.8 %collective-permute-start.3 = (bf16[128,2688]{1,0:T(8,128)(2,1)S(1)}, bf16[128,2688]{1,0:T(8,128)(2,1)S(1)}, u32[]{:S(2)}, u32[]{:S(2)}) collective-permute-start(bf16[128,2688]{1,0:T(8,128)(2,1)S(1)} %pack.1.rows_ref.refs_3_), channel_id=1, source_target_pairs={{0,4},{1,3},{2,6},{3,1},{4,0},{5,7},{6,2},{7,5},{8,12},{9,11},{10,... | collective-permute-start | bytes 2064392 | tf_op jit(solution)/shard_map/ppermute | solution.py:35
  21.5 11.9 %collective-permute-start.6 = (bf16[128,2688]{1,0:T(8,128)(2,1)S(1)}, bf16[128,2688]{1,0:T(8,128)(2,1)S(1)}, u32[]{:S(2)}, u32[]{:S(2)}) collective-permute-start(bf16[128,2688]{1,0:T(8,128)(2,1)S(1)} %get-tuple-element.16.refs_3_), channel_id=1, source_target_pairs={{0,4},{1,3},{2,6},{3,1},{4,0},{5,7},{6,2},{7,5},{8,12},{9,11},{10,... | collective-permute-start | bytes 2064392 | tf_op jit(solution)/shard_map/ppermute | solution.py:35
  28.0 12.7 %collective-permute-start.5 = (bf16[128,2560]{1,0:T(8,128)(2,1)S(1)}, bf16[128,2560]{1,0:T(8,128)(2,1)S(1)}, u32[]{:S(2)}, u32[]{:S(2)}) collective-permute-start(bf16[128,2560]{1,0:T(8,128)(2,1)S(1)} %expert.9.refs_4_), channel_id=1, source_target_pairs={{0,4},{1,3},{2,6},{3,1},{4,0},{5,7},{6,2},{7,5},{8,12},{9,11},{10,... | collective-permute-start | bytes 1966088 | tf_op jit(solution)/shard_map/ppermute | solution.py:35
  36.9 10.7 %collective-permute-start.7 = (bf16[128,2560]{1,0:T(8,128)(2,1)S(1)}, bf16[128,2560]{1,0:T(8,128)(2,1)S(1)}, u32[]{:S(2)}, u32[]{:S(2)}) collective-permute-start(bf16[128,2560]{1,0:T(8,128)(2,1)S(1)} %expert.11.refs_5_), channel_id=1, source_target_pairs={{0,4},{1,3},{2,6},{3,1},{4,0},{5,7},{6,2},{7,5},{8,12},{9,11},{10,... | collective-permute-start | bytes 1966088 | tf_op jit(solution)/shard_map/ppermute | solution.py:35
  47.7 10.7 %collective-permute-start.8 = (bf16[128,2560]{1,0:T(8,128)(2,1)S(1)}, bf16[128,2560]{1,0:T(8,128)(2,1)S(1)}, u32[]{:S(2)}, u32[]{:S(2)}) collective-permute-start(bf16[128,2560]{1,0:T(8,128)(2,1)S(1)} %sums.2), channel_id=1, source_target_pairs={{0,2},{1,5},{2,0},{3,7},{4,6},{5,1},{6,4},{7,3},{8,10},{9,13},{10,... | collective-permute-start | bytes 1966088 | tf_op jit(solution)/shard_map/ppermute | solution.py:35

commit v3 on v2

--- a/solution.py
+++ b/solution.py
@@ -35,12 +35,13 @@
     return lax.ppermute(value, "expert", [(i, i ^ offsets[i % 2]) for i in range(size)])
 
 
-def pack_kernel(experts, tokens_ref, ids_ref, gates_ref, out_ref, ids, gates, done):
+def pack_kernel(experts, tokens_ref, ids_ref, gates_ref, out_ref, again_ref, ids, gates, done):
     rows, features = tokens_ref.shape
     copies = [
         pltpu.make_async_copy(ids_ref, ids, done.at[0]),
         pltpu.make_async_copy(gates_ref, gates, done.at[1]),
         pltpu.make_async_copy(tokens_ref, out_ref.at[:, pl.ds(0, features)], done.at[2]),
+        pltpu.make_async_copy(tokens_ref, again_ref.at[:, pl.ds(0, features)], done.at[3]),
     ]
     for copy in copies:
         copy.start()
@@ -59,8 +60,11 @@
     low = rest - middle
     terms = jnp.where(line < experts, high, jnp.where(line < 2 * experts, middle, low))
     terms = jnp.where(line < 3 * experts, terms, 0.0)
-    out_ref[:, features:] = terms.T.astype(jnp.bfloat16)
+    terms = terms.T.astype(jnp.bfloat16)
+    out_ref[:, features:] = terms
+    again_ref[:, features:] = terms
     copies[2].wait()
+    copies[3].wait()
 
 
 def pack(tokens, ids, gates, experts):
@@ -68,22 +72,22 @@
     ids, gates = ids.T, gates.T
     return pl.pallas_call(
         functools.partial(pack_kernel, experts),
-        out_shape=jax.ShapeDtypeStruct((rows, features + LANES), tokens.dtype),
+        out_shape=[jax.ShapeDtypeStruct((rows, features + LANES), tokens.dtype)] * 2,
         in_specs=[anywhere()] * 3,
-        out_specs=whole(),
+        out_specs=[whole()] * 2,
         scratch_shapes=[
             pltpu.VMEM(ids.shape, ids.dtype),
             pltpu.VMEM(gates.shape, gates.dtype),
-            pltpu.SemaphoreType.DMA((3,)),
+            pltpu.SemaphoreType.DMA((4,)),
         ],
-        compiler_params=pltpu.CompilerParams(vmem_limit_bytes=8 * MIB),
+        compiler_params=pltpu.CompilerParams(vmem_limit_bytes=16 * MIB),
         cost_estimate=pl.CostEstimate(flops=0, bytes_accessed=4 * rows * features, transcendentals=0),
         name="pack",
     )(in_hbm(tokens), in_hbm(ids), in_hbm(gates))
 
 
-def row_weights(rows_ref, experts, features, other):
-    terms = rows_ref[:, features:].astype(jnp.float32)
+def row_weights(terms, experts, other):
+    terms = terms.astype(jnp.float32)
     lane = lax.broadcasted_iota(jnp.int32, terms.shape, 1)
     own = lax.axis_index("expert") ^ other
     chosen = (lane == own) | (lane == own + experts) | (lane == own + 2 * experts)
@@ -111,7 +115,7 @@
         copy.start()
     waits = iter(copies)
     rows = rows_ref[:, :features]
-    weight = row_weights(rows_ref, experts, features, 0)
+    weight = row_weights(rows_ref[:, features:], experts, 0)
     for at in range(0, width, STEP):
         next(waits).wait()
         next(waits).wait()
@@ -135,24 +139,43 @@
         in_specs=[anywhere()] * 3 + [whole()],
         out_specs=[whole()] * 4,
         scratch_shapes=[pltpu.VMEM((count, width), jnp.bfloat16), pltpu.SemaphoreType.DMA((copies,))],
-        compiler_params=pltpu.CompilerParams(vmem_limit_bytes=8 * MIB),
+        compiler_params=pltpu.CompilerParams(vmem_limit_bytes=16 * MIB),
         cost_estimate=expert_cost(count, features, width),
         name="own",
     )(*[in_hbm(w) for w in weights], in_vmem(rows))
 
 
+def nothing(*refs):
+    pass
+
+
+def held(*values, after=()):
+    return pl.pallas_call(
+        nothing,
+        out_shape=[jax.ShapeDtypeStruct(v.shape, v.dtype) for v in values],
+        in_specs=[anywhere()] * (len(values) + len(after)),
+        out_specs=[anywhere()] * len(values),
+        input_output_aliases={i: i for i in range(len(values))},
+        compiler_params=pltpu.CompilerParams(vmem_limit_bytes=MIB),
+        cost_estimate=pl.CostEstimate(flops=0, bytes_accessed=0, transcendentals=0),
+        name="held",
+    )(*values, *after)
+
+
 def expert_cost(count, features, width):
     return pl.CostEstimate(
         flops=6 * count * features * width, bytes_accessed=count * features * 4, transcendentals=count * width
     )
 
 
-def expert_kernel(experts, other, added, *refs):
+def expert_kernel(experts, other, added, after, parts, *refs):
     gate_ref, up_ref, down_ref, rows_ref = refs[:4]
-    out_ref, hidden_ref = refs[-2:]
+    added_refs = refs[4 : 4 + added * parts]
+    out_refs = refs[4 + added * parts + after : -1]
+    hidden_ref = refs[-1]
     features, width = gate_ref.shape
     rows = rows_ref[:, :features]
-    weight = row_weights(rows_ref, experts, features, other)
+    weight = row_weights(rows_ref[:, features:], experts, other)
     for at in range(0, width, STEP):
         columns = slice(at, at + STEP)
         hidden_ref[:, columns] = hidden_columns(rows, gate_ref, up_ref, columns)
@@ -160,81 +183,87 @@
     for at in range(0, features, 2 * STEP):
         columns = slice(at, at + 2 * STEP)
         answer = jnp.dot(hidden, down_ref[:, columns], preferred_element_type=jnp.float32) * weight
-        for ref in refs[4 : 4 + added]:
-            answer = answer + ref[:, columns].astype(jnp.float32)
-        out_ref[:, columns] = answer.astype(out_ref.dtype)
-
-
-def expert_and_rows_kernel(experts, other, added, *refs):
-    expert_kernel(experts, other, added, *refs[:-2], refs[-1])
-
-
-def run_expert(weights, other, experts, rows, kind, added=(), after=(), rows_too=False):
+        start = 0
+        for i, out_ref in enumerate(out_refs):
+            part = answer[start : start + out_ref.shape[0]]
+            for ref in added_refs[i::parts]:
+                part = part + ref[:, columns].astype(jnp.float32)
+            out_ref[:, columns] = part.astype(out_ref.dtype)
+            start += out_ref.shape[0]
+
+
+def run_expert(weights, other, experts, rows, kind, *added, parts=1, after=()):
     features, width = weights[0].shape
     count = rows.shape[0]
-    operands = [in_vmem(w) for w in (*weights, rows, *added)]
-    specs = [whole()] * len(operands) + [anywhere()] * len(after)
-    shapes = [jax.ShapeDtypeStruct((count, features), kind)]
-    if rows_too:
-        shapes.append(jax.ShapeDtypeStruct(rows.shape, rows.dtype))
-    results = pl.pallas_call(
-        functools.partial(expert_and_rows_kernel if rows_too else expert_kernel, experts, other, len(added)),
-        out_shape=shapes,
-        in_specs=specs,
-        out_specs=[whole()] * len(shapes),
-        input_output_aliases={3: 1} if rows_too else {},
+    operands = [in_vmem(v) for v in (*weights, rows, *(v for group in added for v in group))]
+    return pl.pallas_call(
+        functools.partial(expert_kernel, experts, other, len(added), len(after), parts),
+        out_shape=[jax.ShapeDtypeStruct((count // parts, features), kind)] * parts,
+        in_specs=[whole()] * len(operands) + [anywhere()] * len(after),
+        out_specs=[whole()] * parts,
         scratch_shapes=[pltpu.VMEM((count, width), jnp.bfloat16)],
-        compiler_params=pltpu.CompilerParams(vmem_limit_bytes=8 * MIB),
+        compiler_params=pltpu.CompilerParams(vmem_limit_bytes=16 * MIB),
         cost_estimate=expert_cost(count, features, width),
         name="expert",
     )(*operands, *after)
-    return results if rows_too else results[0]
-
-
-def sum_kernel(count, *refs):
-    total = refs[0][...].astype(jnp.float32)
-    for ref in refs[1:count]:
-        total = total + ref[...].astype(jnp.float32)
-    refs[-1][...] = total.astype(refs[-1].dtype)
-
-
-def sums(*parts, after=()):
-    rows, features = parts[0].shape
-    return pl.pallas_call(
-        functools.partial(sum_kernel, len(parts)),
-        out_shape=jax.ShapeDtypeStruct((rows, features), jnp.bfloat16),
-        in_specs=[whole()] * len(parts) + [anywhere()] * len(after),
+
+
+def sum_kernel(first_ref, second_ref, *refs):
+    refs[-1][...] = (first_ref[...].astype(jnp.float32) + second_ref[...].astype(jnp.float32)).astype(refs[-1].dtype)
+
+
+def sums(first, second, after=()):
+    return pl.pallas_call(
+        sum_kernel,
+        out_shape=jax.ShapeDtypeStruct(first.shape, jnp.bfloat16),
+        in_specs=[whole()] * 2 + [anywhere()] * len(after),
         out_specs=whole(),
-        compiler_params=pltpu.CompilerParams(vmem_limit_bytes=8 * MIB),
-        cost_estimate=pl.CostEstimate(flops=rows * features, bytes_accessed=4 * rows * features, transcendentals=0),
+        compiler_params=pltpu.CompilerParams(vmem_limit_bytes=16 * MIB),
         name="sums",
-    )(*[in_vmem(p) for p in parts], *after)
+    )(in_vmem(first), in_vmem(second), *after)
+
+
+def finish_kernel(whole_ref, upper_ref, lower_ref, out_ref):
+    half = upper_ref.shape[0]
+    out_ref[:half] = (whole_ref[:half] + upper_ref[...].astype(jnp.float32)).astype(out_ref.dtype)
+    out_ref[half:] = (whole_ref[half:] + lower_ref[...].astype(jnp.float32)).astype(out_ref.dtype)
+
+
+def finish(whole_part, upper, lower):
+    return pl.pallas_call(
+        finish_kernel,
+        out_shape=jax.ShapeDtypeStruct(whole_part.shape, jnp.bfloat16),
+        in_specs=[whole()] * 3,
+        out_specs=whole(),
+        compiler_params=pltpu.CompilerParams(vmem_limit_bytes=16 * MIB),
+        name="finish",
+    )(in_vmem(whole_part), in_vmem(upper), in_vmem(lower))
 
 
 def on_four_chips(tokens, expert_ids, gate_values, w_gate, w_up, w_down):
     experts = lax.axis_size("expert")
     weights = (w_gate[0], w_up[0], w_down[0])
     far = tuple(swap(w, (CORE, CORE)) for w in weights)
-    own = pack(tokens, expert_ids, gate_values, experts)
+    own, again = pack(tokens, expert_ids, gate_values, experts)
+    wide, narrow = jnp.float32, jnp.bfloat16
     first = swap(own, FIRST)
-    second = swap(own, SECOND)
-
-    wide, narrow = jnp.float32, jnp.bfloat16
     near_own, *near = run_own(weights, experts, own)
+    second = swap(*held(again, after=[near_own]), SECOND)
+    third = swap(first, SECOND)
     near_run = functools.partial(run_expert, near, 0, experts)
     far_run = functools.partial(run_expert, far, CORE, experts)
-    near_first, first = near_run(first, wide, after=[near_own], rows_too=True)
-    third = swap(first, SECOND)
-    near_second = near_run(second, wide, after=[near_first])
-    sum_second = far_run(second, narrow, [near_second])
-    back_second = swap(sum_second, SECOND)
-    near_third = near_run(third, wide, after=[sum_second])
-    sum_third = far_run(third, narrow, [near_third])
-    passed = swap(sum_third, SECOND)
-    sum_first = far_run(first, wide, [near_first], after=[sum_third])
-    sum_own = far_run(own, wide, [near_own, back_second], after=[sum_first])
-    back_first = swap(sums(sum_first, passed, after=[sum_own]), FIRST)
-    return sums(sum_own, back_first)
+    near_second = near_run(second, wide, after=[near_own])
+    sum_second = far_run(second, narrow, near_second)
+    back_second = swap(sum_second[0], SECOND)
+    near_third = near_run(third, wide, parts=2, after=sum_second)
+    sum_third = far_run(third, narrow, near_third, parts=2)
+    passed_a, passed_b = swap(sum_third[0], SECOND), swap(sum_third[1], SECOND)
+    near_first = near_run(first, wide, parts=2, after=sum_third)
+    sum_first = far_run(first, wide, near_first, parts=2)
+    sum_own = far_run(own, wide, [near_own], [back_second], after=sum_first)[0]
+    back_first_a = swap(sums(sum_first[0], passed_a, after=[sum_own]), FIRST)
+    back_first_b = swap(sums(sum_first[1], passed_b, after=[sum_own]), FIRST)
+    return finish(sum_own, back_first_a, back_first_b)
 
 
 def expert_apply(row_block, gate_matrix, up_matrix, down_matrix):

time: 59.5 us -> 51.8 us (0.87)
  waiting for transfers between devices: 27.3 us -> 16 us
  starting transfers between devices: 11.9 us -> 15.2 us
    ppermute x9 -> x11, waiting for transfers between devices: 27.3 us -> 16 us  [swap(): lax.ppermute(value, 'expert', [(i, i ^ offsets[i % 2]) for i in range(siz...]
    ppermute x9 -> x11, starting transfers between devices: 11.9 us -> 15.2 us  [swap(): lax.ppermute(value, 'expert', [(i, i ^ offsets[i % 2]) for i in range(siz...]
    pallas_call x10 -> x12, Pallas kernels: 14.6 us -> 14.8 us  [the longest x7 12.4 us: run_expert(): pl.pallas_call(functools.partial(expert_kernel, experts, other, len(added...]
  transfers between devices with their start and end apart: 9 -> 11, of which waited for: 4 -> 6; matrix products, arithmetic and copies ran while one was open for 0% -> 0% of each run, Pallas kernels for 32% -> 37%
where the time goes in v3:
time: 51.8 us; the launch traced here: 51.6 us
  Pallas kernels  20.2 us (39%)
  waiting for transfers between devices  16 us (31%)
  starting transfers between devices  15.2 us (29%)
    ppermute x11, waiting for transfers between devices, swap(): lax.ppermute(value, 'expert', [(i, i ^ offsets[i % 2]) for i in range(siz...  16 us
    ppermute x11, starting transfers between devices, swap(): lax.ppermute(value, 'expert', [(i, i ^ offsets[i % 2]) for i in range(siz...  15.2 us
    pallas_call x7, Pallas kernels, run_expert(): pl.pallas_call(functools.partial(expert_kernel, experts, other, len(added...  12.4 us
    pallas_call x1, Pallas kernels, run_own(): pl.pallas_call(functools.partial(own_kernel, experts), out_shape=[jax.Sha...  5.38 us
    pallas_call x1, Pallas kernels, pack(): pl.pallas_call(functools.partial(pack_kernel, experts), out_shape=[jax.Sh...  1.35 us
  transfers between devices with their start and end apart: 11, of which 6 were waited for; matrix products, arithmetic and copies ran while one was open for 0% of the time, Pallas kernels for 37%

profile of v3, /device:TPU:0, one launch (start us, length us, event | category | flops | bytes accessed | tf_op | source)
XLA Modules:
  0.0 51.6 jit_solution(18408279122832215878)
XLA Ops:
  0.0 0.5 collective-permute-start
  0.5 0.1 collective-permute-start.1
  0.5 0.5 collective-permute-start.2
  1.0 1.4 %pack.1 = (bf16[128,2688]{1,0:T(8,128)(2,1)S(1)}, bf16[128,2688]{1,0:T(8,128)(2,1)S(1)}) custom-call(bf16[128,2560]{1,0:T(8,128)(2,1)} %tokens_ref.1, s32[6,128]{1,0:T(8,128)} %bitcast.11, f32[6,128]{1,0:T(8,128)} %bitcast.12), custom_call_target="tpu_custom_call" | custom-call | bytes 1310720 | tf_op jit(solution)/shard_map/pack/pallas_call | solution.py:73
  2.3 2.6 %collective-permute-start.5 = (bf16[128,2688]{1,0:T(8,128)(2,1)S(1)}, bf16[128,2688]{1,0:T(8,128)(2,1)S(1)}, u32[]{:S(2)}, u32[]{:S(2)}) collective-permute-start(bf16[128,2688]{1,0:T(8,128)(2,1)S(1)} %get-tuple-element.19.rows_ref.refs_3_), channel_id=1, source_target_pairs={{0,2},{1,5},{2,0},{3,7},{4,6},{5,1},{6,4},{7,3},{8,10},{9,13},{10,... | collective-permute-start | bytes 2064392 | tf_op jit(solution)/shard_map/ppermute | solution.py:35
  4.9 5.4 %own.1 = (f32[128,2560]{1,0:T(8,128)S(1)}, bf16[2560,768]{1,0:T(8,128)(2,1)S(1)}, bf16[2560,768]{1,0:T(8,128)(2,1)S(1)}, bf16[768,2560]{1,0:T(8,128)(2,1)S(1)}) custom-call(bf16[2560,768]{1,0:T(8,128)(2,1)} %bitcast.6, bf16[2560,768]{1,0:T(8,128)(2,1)} %bitcast.8, bf16[768,2560]{1,0:T(8,128)(2,1)} %bitcast.10, ...), custom_call_target="tpu_custom_call" | custom-call | flops 1509949440 | bytes 1310720 | tf_op jit(solution)/shard_map/own/pallas_call | solution.py:135
  10.3 1.6 %collective-permute-start.3 = (bf16[128,2688]{1,0:T(8,128)(2,1)S(1)}, bf16[128,2688]{1,0:T(8,128)(2,1)S(1)}, u32[]{:S(2)}, u32[]{:S(2)}) collective-permute-start(bf16[128,2688]{1,0:T(8,128)(2,1)S(1)} %held.1), channel_id=1, source_target_pairs={{0,4},{1,3},{2,6},{3,1},{4,0},{5,7},{6,2},{7,5},{8,12},{9,11},{10,... | collective-permute-start | bytes 2064392 | tf_op jit(solution)/shard_map/ppermute | solution.py:35
  11.9 2.5 %collective-permute-done.5.refs_3_ = bf16[128,2688]{1,0:T(8,128)(2,1)S(1)} collective-permute-done((bf16[128,2688]{1,0:T(8,128)(2,1)S(1)}, bf16[128,2688]{1,0:T(8,128)(2,1)S(1)}, u32[]{:S(2)}, u32[]{:S(2)}) %collective-permute-start.5) | collective-permute-done | bytes 688160 | tf_op jit(solution)/shard_map/ppermute | solution.py:35
  14.4 3.7 %collective-permute-start.6 = (bf16[128,2688]{1,0:T(8,128)(2,1)S(1)}, bf16[128,2688]{1,0:T(8,128)(2,1)S(1)}, u32[]{:S(2)}, u32[]{:S(2)}) collective-permute-start(bf16[128,2688]{1,0:T(8,128)(2,1)S(1)} %collective-permute-done.5.refs_3_), channel_id=1, source_target_pairs={{0,4},{1,3},{2,6},{3,1},{4,0},{5,7},{6,2},{7,5},{8,12},{9,11},{10,... | collective-permute-start | bytes 2064392 | tf_op jit(solution)/shard_map/ppermute | solution.py:35
  18.1 3.2 %collective-permute-done.3.refs_3_ = bf16[128,2688]{1,0:T(8,128)(2,1)S(1)} collective-permute-done((bf16[128,2688]{1,0:T(8,128)(2,1)S(1)}, bf16[128,2688]{1,0:T(8,128)(2,1)S(1)}, u32[]{:S(2)}, u32[]{:S(2)}) %collective-permute-start.3) | collective-permute-done | bytes 688160 | tf_op jit(solution)/shard_map/ppermute | solution.py:35
  21.3 1.8 %expert.7.refs_4_ = f32[128,2560]{1,0:T(8,128)S(1)} custom-call(bf16[2560,768]{1,0:T(8,128)(2,1)S(1)} %get-tuple-element.22.refs_0_, bf16[2560,768]{1,0:T(8,128)(2,1)S(1)} %get-tuple-element.23.refs_1_, bf16[768,2560]{1,0:T(8,128)(2,1)S(1)} %get-tuple-element.24.refs_2_, bf16[128,2688]{1,0:T(8,128)(2,1)S(1)} %collective-permute-done.3.refs_3_, ...), custom_call_target="tpu_custom_call" | custom-call | flops 1509949440 | bytes 1310720 | tf_op jit(solution)/shard_map/expert/pallas_call | solution.py:199
  23.1 0.0 collective-permute-done.refs_0_
  23.1 0.0 collective-permute-done.1.refs_1_
  23.1 0.0 collective-permute-done.2.refs_2_
  23.1 1.8 %expert.8.refs_4_ = bf16[128,2560]{1,0:T(8,128)(2,1)S(1)} custom-call(bf16[2560,768]{1,0:T(8,128)(2,1)S(1)} %collective-permute-done.refs_0_, bf16[2560,768]{1,0:T(8,128)(2,1)S(1)} %collective-permute-done.1.refs_1_, bf16[768,2560]{1,0:T(8,128)(2,1)S(1)} %collective-permute-done.2.refs_2_, bf16[128,2688]{1,0:T(8,128)(2,1)S(1)} %collective-permute-done.3.refs_3_, ...), custom_call_target="tpu_custom_call" | custom-call | flops 1509949440 | bytes 1310720 | tf_op jit(solution)/shard_map/expert/pallas_call | solution.py:199
  24.9 1.6 %collective-permute-start.4 = (bf16[128,2560]{1,0:T(8,128)(2,1)S(1)}, bf16[128,2560]{1,0:T(8,128)(2,1)S(1)}, u32[]{:S(2)}, u32[]{:S(2)}) collective-permute-start(bf16[128,2560]{1,0:T(8,128)(2,1)S(1)} %expert.8.refs_4_), channel_id=1, source_target_pairs={{0,4},{1,3},{2,6},{3,1},{4,0},{5,7},{6,2},{7,5},{8,12},{9,11},{10,... | collective-permute-start | bytes 1966088 | tf_op jit(solution)/shard_map/ppermute | solution.py:35
  26.5 2.2 %collective-permute-done.6.refs_3_ = bf16[128,2688]{1,0:T(8,128)(2,1)S(1)} collective-permute-done((bf16[128,2688]{1,0:T(8,128)(2,1)S(1)}, bf16[128,2688]{1,0:T(8,128)(2,1)S(1)}, u32[]{:S(2)}, u32[]{:S(2)}) %collective-permute-start.6) | collective-permute-done | bytes 688160 | tf_op jit(solution)/shard_map/ppermute | solution.py:35
  28.7 1.8 %expert.9 = (f32[64,2560]{1,0:T(8,128)S(1)}, f32[64,2560]{1,0:T(8,128)S(1)}) custom-call(bf16[2560,768]{1,0:T(8,128)(2,1)S(1)} %get-tuple-element.22.refs_0_, bf16[2560,768]{1,0:T(8,128)(2,1)S(1)} %get-tuple-element.23.refs_1_, bf16[768,2560]{1,0:T(8,128)(2,1)S(1)} %get-tuple-element.24.refs_2_, bf16[128,2688]{1,0:T(8,128)(2,1)S(1)} %collective-permute-done.6.refs_3_, ...), custom_call_target="tpu_custom_call" | custom-call | flops 1509949440 | bytes 1310720 | tf_op jit(solution)/shard_map/expert/pallas_call | solution.py:199
  30.4 1.8 %expert.10 = (bf16[64,2560]{1,0:T(8,128)(2,1)S(1)}, bf16[64,2560]{1,0:T(8,128)(2,1)S(1)}) custom-call(bf16[2560,768]{1,0:T(8,128)(2,1)S(1)} %collective-permute-done.refs_0_, bf16[2560,768]{1,0:T(8,128)(2,1)S(1)} %collective-permute-done.1.refs_1_, bf16[768,2560]{1,0:T(8,128)(2,1)S(1)} %collective-permute-done.2.refs_2_, ...), custom_call_target="tpu_custom_call" | custom-call | flops 1509949440 | bytes 1310720 | tf_op jit(solution)/shard_map/expert/pallas_call | solution.py:199
  32.2 1.6 %collective-permute-start.9 = (bf16[64,2560]{1,0:T(8,128)(2,1)S(1)}, bf16[64,2560]{1,0:T(8,128)(2,1)S(1)}, u32[]{:S(2)}, u32[]{:S(2)}) collective-permute-start(bf16[64,2560]{1,0:T(8,128)(2,1)S(1)} %get-tuple-element.28.refs_5_), channel_id=1, source_target_pairs={{0,4},{1,3},{2,6},{3,1},{4,0},{5,7},{6,2},{7,5},{8,12},{9,11},{10,... | collective-permute-start | bytes 983048 | tf_op jit(solution)/shard_map/ppermute | solution.py:35
  33.8 0.5 collective-permute-start.7
  34.3 1.8 %expert.11 = (f32[64,2560]{1,0:T(8,128)S(1)}, f32[64,2560]{1,0:T(8,128)S(1)}) custom-call(bf16[2560,768]{1,0:T(8,128)(2,1)S(1)} %get-tuple-element.22.refs_0_, bf16[2560,768]{1,0:T(8,128)(2,1)S(1)} %get-tuple-element.23.refs_1_, bf16[768,2560]{1,0:T(8,128)(2,1)S(1)} %get-tuple-element.24.refs_2_, bf16[128,2688]{1,0:T(8,128)(2,1)S(1)} %collective-permute-done.5.refs_3_, ...), custom_call_target="tpu_custom_call" | custom-call | flops 1509949440 | bytes 1310720 | tf_op jit(solution)/shard_map/expert/pallas_call | solution.py:199
  36.1 1.8 %expert.12 = (f32[64,2560]{1,0:T(8,128)S(1)}, f32[64,2560]{1,0:T(8,128)S(1)}) custom-call(bf16[2560,768]{1,0:T(8,128)(2,1)S(1)} %collective-permute-done.refs_0_, bf16[2560,768]{1,0:T(8,128)(2,1)S(1)} %collective-permute-done.1.refs_1_, bf16[768,2560]{1,0:T(8,128)(2,1)S(1)} %collective-permute-done.2.refs_2_, ...), custom_call_target="tpu_custom_call" | custom-call | flops 1509949440 | bytes 1310720 | tf_op jit(solution)/shard_map/expert/pallas_call | solution.py:199
  37.9 1.8 %expert.13.refs_0_.whole_ref = f32[128,2560]{1,0:T(8,128)S(1)} custom-call(bf16[2560,768]{1,0:T(8,128)(2,1)S(1)} %collective-permute-done.refs_0_, bf16[2560,768]{1,0:T(8,128)(2,1)S(1)} %collective-permute-done.1.refs_1_, bf16[768,2560]{1,0:T(8,128)(2,1)S(1)} %collective-permute-done.2.refs_2_, bf16[128,2688]{1,0:T(8,128)(2,1)S(1)} %get-tuple-element.19.rows_ref.refs_3_, ...), custom_call_target="tpu_custom_call" | custom-call | flops 1509949440 | bytes 1310720 | tf_op jit(solution)/shard_map/expert/pallas_call | solution.py:199
  39.7 0.1 sums.3
  39.7 1.5 %collective-permute-start.10 = (bf16[64,2560]{1,0:T(8,128)(2,1)S(1)}, bf16[64,2560]{1,0:T(8,128)(2,1)S(1)}, u32[]{:S(2)}, u32[]{:S(2)}) collective-permute-start(bf16[64,2560]{1,0:T(8,128)(2,1)S(1)} %sums.3), channel_id=1, source_target_pairs={{0,2},{1,5},{2,0},{3,7},{4,6},{5,1},{6,4},{7,3},{8,10},{9,13},{10,... | collective-permute-start | bytes 983048 | tf_op jit(solution)/shard_map/ppermute | solution.py:35
  41.2 2.2 %collective-permute-done.7.second_ref = bf16[64,2560]{1,0:T(8,128)(2,1)S(1)} collective-permute-done((bf16[64,2560]{1,0:T(8,128)(2,1)S(1)}, bf16[64,2560]{1,0:T(8,128)(2,1)S(1)}, u32[]{:S(2)}, u32[]{:S(2)}) %collective-permute-start.7) | collective-permute-done | bytes 327712 | tf_op jit(solution)/shard_map/ppermute | solution.py:35
  43.4 0.1 sums.2
  43.5 1.2 %collective-permute-start.8 = (bf16[64,2560]{1,0:T(8,128)(2,1)S(1)}, bf16[64,2560]{1,0:T(8,128)(2,1)S(1)}, u32[]{:S(2)}, u32[]{:S(2)}) collective-permute-start(bf16[64,2560]{1,0:T(8,128)(2,1)S(1)} %sums.2), channel_id=1, source_target_pairs={{0,2},{1,5},{2,0},{3,7},{4,6},{5,1},{6,4},{7,3},{8,10},{9,13},{10,... | collective-permute-start | bytes 983048 | tf_op jit(solution)/shard_map/ppermute | solution.py:35
  44.7 2.1 %collective-permute-done.10.lower_ref = bf16[64,2560]{1,0:T(8,128)(2,1)S(1)} collective-permute-done((bf16[64,2560]{1,0:T(8,128)(2,1)S(1)}, bf16[64,2560]{1,0:T(8,128)(2,1)S(1)}, u32[]{:S(2)}, u32[]{:S(2)}) %collective-permute-start.10) | collective-permute-done | bytes 327712 | tf_op jit(solution)/shard_map/ppermute | solution.py:35
  46.9 3.8 %collective-permute-done.8.upper_ref = bf16[64,2560]{1,0:T(8,128)(2,1)S(1)} collective-permute-done((bf16[64,2560]{1,0:T(8,128)(2,1)S(1)}, bf16[64,2560]{1,0:T(8,128)(2,1)S(1)}, u32[]{:S(2)}, u32[]{:S(2)}) %collective-permute-start.8) | collective-permute-done | bytes 327712 | tf_op jit(solution)/shard_map/ppermute | solution.py:35
  50.6 0.9 %finish.1 = bf16[128,2560]{1,0:T(8,128)(2,1)} custom-call(f32[128,2560]{1,0:T(8,128)S(1)} %expert.13.refs_0_.whole_ref, bf16[64,2560]{1,0:T(8,128)(2,1)S(1)} %collective-permute-done.8.upper_ref, bf16[64,2560]{1,0:T(8,128)(2,1)S(1)} %collective-permute-done.10.lower_ref), custom_call_target="tpu_custom_call" | custom-call | tf_op jit(solution)/shard_map/finish/pallas_call | solution.py:233
  (3 shorter events, 0.0 us)
Async XLA Ops:
  0.0 23.1 %collective-permute-start = (bf16[2560,768]{1,0:T(8,128)(2,1)}, bf16[2560,768]{1,0:T(8,128)(2,1)S(1)}, u32[]{:S(2)}, u32[]{:S(2)}) collective-permute-start(bf16[2560,768]{1,0:T(8,128)(2,1)} %bitcast.5), channel_id=1, source_target_pairs={{0,1},{1,0},{2,3},{3,2},{4,5},{5,4},{6,7},{7,6},{8,9},{9,8},{10,11... | collective-permute-start | bytes 11796488 | tf_op jit(solution)/shard_map/ppermute | solution.py:35
  0.5 22.6 %collective-permute-start.1 = (bf16[2560,768]{1,0:T(8,128)(2,1)}, bf16[2560,768]{1,0:T(8,128)(2,1)S(1)}, u32[]{:S(2)}, u32[]{:S(2)}) collective-permute-start(bf16[2560,768]{1,0:T(8,128)(2,1)} %bitcast.7), channel_id=1, source_target_pairs={{0,1},{1,0},{2,3},{3,2},{4,5},{5,4},{6,7},{7,6},{8,9},{9,8},{10,11... | collective-permute-start | bytes 11796488 | tf_op jit(solution)/shard_map/ppermute | solution.py:35
  0.5 22.6 %collective-permute-start.2 = (bf16[768,2560]{1,0:T(8,128)(2,1)}, bf16[768,2560]{1,0:T(8,128)(2,1)S(1)}, u32[]{:S(2)}, u32[]{:S(2)}) collective-permute-start(bf16[768,2560]{1,0:T(8,128)(2,1)} %bitcast.9), channel_id=1, source_target_pairs={{0,1},{1,0},{2,3},{3,2},{4,5},{5,4},{6,7},{7,6},{8,9},{9,8},{10,11... | collective-permute-start | bytes 11796488 | tf_op jit(solution)/shard_map/ppermute | solution.py:35
  2.3 12.1 %collective-permute-start.5 = (bf16[128,2688]{1,0:T(8,128)(2,1)S(1)}, bf16[128,2688]{1,0:T(8,128)(2,1)S(1)}, u32[]{:S(2)}, u32[]{:S(2)}) collective-permute-start(bf16[128,2688]{1,0:T(8,128)(2,1)S(1)} %get-tuple-element.19.rows_ref.refs_3_), channel_id=1, source_target_pairs={{0,2},{1,5},{2,0},{3,7},{4,6},{5,1},{6,4},{7,3},{8,10},{9,13},{10,... | collective-permute-start | bytes 2064392 | tf_op jit(solution)/shard_map/ppermute | solution.py:35
  10.3 11.0 %collective-permute-start.3 = (bf16[128,2688]{1,0:T(8,128)(2,1)S(1)}, bf16[128,2688]{1,0:T(8,128)(2,1)S(1)}, u32[]{:S(2)}, u32[]{:S(2)}) collective-permute-start(bf16[128,2688]{1,0:T(8,128)(2,1)S(1)} %held.1), channel_id=1, source_target_pairs={{0,4},{1,3},{2,6},{3,1},{4,0},{5,7},{6,2},{7,5},{8,12},{9,11},{10,... | collective-permute-start | bytes 2064392 | tf_op jit(solution)/shard_map/ppermute | solution.py:35
  14.4 14.3 %collective-permute-start.6 = (bf16[128,2688]{1,0:T(8,128)(2,1)S(1)}, bf16[128,2688]{1,0:T(8,128)(2,1)S(1)}, u32[]{:S(2)}, u32[]{:S(2)}) collective-permute-start(bf16[128,2688]{1,0:T(8,128)(2,1)S(1)} %collective-permute-done.5.refs_3_), channel_id=1, source_target_pairs={{0,4},{1,3},{2,6},{3,1},{4,0},{5,7},{6,2},{7,5},{8,12},{9,11},{10,... | collective-permute-start | bytes 2064392 | tf_op jit(solution)/shard_map/ppermute | solution.py:35
  24.9 13.0 %collective-permute-start.4 = (bf16[128,2560]{1,0:T(8,128)(2,1)S(1)}, bf16[128,2560]{1,0:T(8,128)(2,1)S(1)}, u32[]{:S(2)}, u32[]{:S(2)}) collective-permute-start(bf16[128,2560]{1,0:T(8,128)(2,1)S(1)} %expert.8.refs_4_), channel_id=1, source_target_pairs={{0,4},{1,3},{2,6},{3,1},{4,0},{5,7},{6,2},{7,5},{8,12},{9,11},{10,... | collective-permute-start | bytes 1966088 | tf_op jit(solution)/shard_map/ppermute | solution.py:35
  32.2 7.4 %collective-permute-start.9 = (bf16[64,2560]{1,0:T(8,128)(2,1)S(1)}, bf16[64,2560]{1,0:T(8,128)(2,1)S(1)}, u32[]{:S(2)}, u32[]{:S(2)}) collective-permute-start(bf16[64,2560]{1,0:T(8,128)(2,1)S(1)} %get-tuple-element.28.refs_5_), channel_id=1, source_target_pairs={{0,4},{1,3},{2,6},{3,1},{4,0},{5,7},{6,2},{7,5},{8,12},{9,11},{10,... | collective-permute-start | bytes 983048 | tf_op jit(solution)/shard_map/ppermute | solution.py:35
  33.8 9.7 %collective-permute-start.7 = (bf16[64,2560]{1,0:T(8,128)(2,1)S(1)}, bf16[64,2560]{1,0:T(8,128)(2,1)S(1)}, u32[]{:S(2)}, u32[]{:S(2)}) collective-permute-start(bf16[64,2560]{1,0:T(8,128)(2,1)S(1)} %get-tuple-element.27.refs_4_), channel_id=1, source_target_pairs={{0,4},{1,3},{2,6},{3,1},{4,0},{5,7},{6,2},{7,5},{8,12},{9,11},{10,... | collective-permute-start | bytes 983048 | tf_op jit(solution)/shard_map/ppermute | solution.py:35
  39.7 7.1 %collective-permute-start.10 = (bf16[64,2560]{1,0:T(8,128)(2,1)S(1)}, bf16[64,2560]{1,0:T(8,128)(2,1)S(1)}, u32[]{:S(2)}, u32[]{:S(2)}) collective-permute-start(bf16[64,2560]{1,0:T(8,128)(2,1)S(1)} %sums.3), channel_id=1, source_target_pairs={{0,2},{1,5},{2,0},{3,7},{4,6},{5,1},{6,4},{7,3},{8,10},{9,13},{10,... | collective-permute-start | bytes 983048 | tf_op jit(solution)/shard_map/ppermute | solution.py:35
  43.5 7.1 %collective-permute-start.8 = (bf16[64,2560]{1,0:T(8,128)(2,1)S(1)}, bf16[64,2560]{1,0:T(8,128)(2,1)S(1)}, u32[]{:S(2)}, u32[]{:S(2)}) collective-permute-start(bf16[64,2560]{1,0:T(8,128)(2,1)S(1)} %sums.2), channel_id=1, source_target_pairs={{0,2},{1,5},{2,0},{3,7},{4,6},{5,1},{6,4},{7,3},{8,10},{9,13},{10,... | collective-permute-start | bytes 983048 | tf_op jit(solution)/shard_map/ppermute | solution.py:35

commit v4 on v3

--- a/solution.py
+++ b/solution.py
@@ -35,55 +35,21 @@
     return lax.ppermute(value, "expert", [(i, i ^ offsets[i % 2]) for i in range(size)])
 
 
-def pack_kernel(experts, tokens_ref, ids_ref, gates_ref, out_ref, again_ref, ids, gates, done):
-    rows, features = tokens_ref.shape
-    copies = [
-        pltpu.make_async_copy(ids_ref, ids, done.at[0]),
-        pltpu.make_async_copy(gates_ref, gates, done.at[1]),
-        pltpu.make_async_copy(tokens_ref, out_ref.at[:, pl.ds(0, features)], done.at[2]),
-        pltpu.make_async_copy(tokens_ref, again_ref.at[:, pl.ds(0, features)], done.at[3]),
-    ]
-    for copy in copies:
-        copy.start()
-    copies[0].wait()
-    copies[1].wait()
+def row_terms(ids, gates, experts):
+    topk, rows = ids.shape
     line = lax.broadcasted_iota(jnp.int32, (LANES, rows), 0)
     expert = line
     for _ in range(2):
         expert = jnp.where(expert >= experts, expert - experts, expert)
     weight = jnp.zeros((LANES, rows), jnp.float32)
-    for k in range(ids_ref.shape[0]):
+    for k in range(topk):
         weight += jnp.where(expert == ids[k : k + 1, :], gates[k : k + 1, :], 0.0)
     high = weight.astype(jnp.bfloat16).astype(jnp.float32)
     rest = weight - high
     middle = rest.astype(jnp.bfloat16).astype(jnp.float32)
     low = rest - middle
     terms = jnp.where(line < experts, high, jnp.where(line < 2 * experts, middle, low))
-    terms = jnp.where(line < 3 * experts, terms, 0.0)
-    terms = terms.T.astype(jnp.bfloat16)
-    out_ref[:, features:] = terms
-    again_ref[:, features:] = terms
-    copies[2].wait()
-    copies[3].wait()
-
-
-def pack(tokens, ids, gates, experts):
-    rows, features = tokens.shape
-    ids, gates = ids.T, gates.T
-    return pl.pallas_call(
-        functools.partial(pack_kernel, experts),
-        out_shape=[jax.ShapeDtypeStruct((rows, features + LANES), tokens.dtype)] * 2,
-        in_specs=[anywhere()] * 3,
-        out_specs=[whole()] * 2,
-        scratch_shapes=[
-            pltpu.VMEM(ids.shape, ids.dtype),
-            pltpu.VMEM(gates.shape, gates.dtype),
-            pltpu.SemaphoreType.DMA((4,)),
-        ],
-        compiler_params=pltpu.CompilerParams(vmem_limit_bytes=16 * MIB),
-        cost_estimate=pl.CostEstimate(flops=0, bytes_accessed=4 * rows * features, transcendentals=0),
-        name="pack",
-    )(in_hbm(tokens), in_hbm(ids), in_hbm(gates))
+    return jnp.where(line < 3 * experts, terms, 0.0).T.astype(jnp.bfloat16)
 
 
 def row_weights(terms, experts, other):
@@ -100,49 +66,89 @@
     return (gate / (1.0 + jnp.exp(-gate)) * up).astype(jnp.bfloat16)
 
 
-def own_kernel(experts, gate_hbm, up_hbm, down_hbm, rows_ref, out_ref, gate_ref, up_ref, down_ref, hidden_ref, done):
-    features, width = gate_ref.shape
-    copies = []
+def own_hidden_kernel(
+    experts, tokens_hbm, ids_hbm, gates_hbm, gate_hbm, up_hbm, rows_ref, terms_ref, hidden_ref, gate_ref, up_ref, ids, gates, done
+):
+    rows, features = tokens_hbm.shape
+    width = gate_ref.shape[1]
+    pairs = [(ids_hbm, ids), (gates_hbm, gates), (tokens_hbm, rows_ref.at[:, pl.ds(0, features)])]
     for at in range(0, width, STEP):
         columns = pl.ds(at, STEP)
-        copies.append((gate_hbm.at[:, columns], gate_ref.at[:, columns]))
-        copies.append((up_hbm.at[:, columns], up_ref.at[:, columns]))
-    for at in range(0, features, 2 * STEP):
-        columns = pl.ds(at, 2 * STEP)
-        copies.append((down_hbm.at[:, columns], down_ref.at[:, columns]))
-    copies = [pltpu.make_async_copy(a, b, done.at[i]) for i, (a, b) in enumerate(copies)]
+        pairs.append((gate_hbm.at[:, columns], gate_ref.at[:, columns]))
+        pairs.append((up_hbm.at[:, columns], up_ref.at[:, columns]))
+    copies = [pltpu.make_async_copy(a, b, done.at[i]) for i, (a, b) in enumerate(pairs)]
     for copy in copies:
         copy.start()
-    waits = iter(copies)
+    copies[0].wait()
+    copies[1].wait()
+    terms = row_terms(ids, gates, experts)
+    terms_ref[...] = terms
+    rows_ref[:, features:] = terms
+    copies[2].wait()
     rows = rows_ref[:, :features]
-    weight = row_weights(rows_ref[:, features:], experts, 0)
+    waits = iter(copies[3:])
     for at in range(0, width, STEP):
         next(waits).wait()
         next(waits).wait()
         columns = slice(at, at + STEP)
         hidden_ref[:, columns] = hidden_columns(rows, gate_ref, up_ref, columns)
+
+
+def own_hidden(tokens, ids, gates, gate, up, experts):
+    count, features = tokens.shape
+    width = gate.shape[1]
+    ids, gates = ids.T, gates.T
+    return pl.pallas_call(
+        functools.partial(own_hidden_kernel, experts),
+        out_shape=[
+            jax.ShapeDtypeStruct((count, features + LANES), tokens.dtype),
+            jax.ShapeDtypeStruct((count, LANES), tokens.dtype),
+            jax.ShapeDtypeStruct((count, width), tokens.dtype),
+            jax.ShapeDtypeStruct(gate.shape, gate.dtype),
+            jax.ShapeDtypeStruct(up.shape, up.dtype),
+        ],
+        in_specs=[anywhere()] * 5,
+        out_specs=[whole()] * 5,
+        scratch_shapes=[
+            pltpu.VMEM(ids.shape, ids.dtype),
+            pltpu.VMEM(gates.shape, gates.dtype),
+            pltpu.SemaphoreType.DMA((3 + 2 * (width // STEP),)),
+        ],
+        compiler_params=pltpu.CompilerParams(vmem_limit_bytes=16 * MIB),
+        cost_estimate=expert_cost(count, features, width),
+        name="own_hidden",
+    )(*[in_hbm(v) for v in (tokens, ids, gates, gate, up)])
+
+
+def own_answer_kernel(experts, hidden_ref, terms_ref, down_hbm, out_ref, down_ref, done):
+    features = down_ref.shape[1]
+    copies = []
+    for i, at in enumerate(range(0, features, 2 * STEP)):
+        columns = pl.ds(at, 2 * STEP)
+        copies.append(pltpu.make_async_copy(down_hbm.at[:, columns], down_ref.at[:, columns], done.at[i]))
+    for copy in copies:
+        copy.start()
+    weight = row_weights(terms_ref[...], experts, 0)
     hidden = hidden_ref[...]
-    for at in range(0, features, 2 * STEP):
-        next(waits).wait()
+    for i, at in enumerate(range(0, features, 2 * STEP)):
+        copies[i].wait()
         columns = slice(at, at + 2 * STEP)
         out_ref[:, columns] = jnp.dot(hidden, down_ref[:, columns], preferred_element_type=jnp.float32) * weight
 
 
-def run_own(weights, experts, rows):
-    features, width = weights[0].shape
-    count = rows.shape[0]
-    copies = 2 * (width // STEP) + features // (2 * STEP)
-    return pl.pallas_call(
-        functools.partial(own_kernel, experts),
-        out_shape=[jax.ShapeDtypeStruct((count, features), jnp.float32)]
-        + [jax.ShapeDtypeStruct(w.shape, w.dtype) for w in weights],
-        in_specs=[anywhere()] * 3 + [whole()],
-        out_specs=[whole()] * 4,
-        scratch_shapes=[pltpu.VMEM((count, width), jnp.bfloat16), pltpu.SemaphoreType.DMA((copies,))],
-        compiler_params=pltpu.CompilerParams(vmem_limit_bytes=16 * MIB),
-        cost_estimate=expert_cost(count, features, width),
-        name="own",
-    )(*[in_hbm(w) for w in weights], in_vmem(rows))
+def own_answer(hidden, terms, down, experts):
+    count, width = hidden.shape
+    features = down.shape[1]
+    return pl.pallas_call(
+        functools.partial(own_answer_kernel, experts),
+        out_shape=[jax.ShapeDtypeStruct((count, features), jnp.float32), jax.ShapeDtypeStruct(down.shape, down.dtype)],
+        in_specs=[whole()] * 2 + [anywhere()],
+        out_specs=[whole()] * 2,
+        scratch_shapes=[pltpu.SemaphoreType.DMA((features // (2 * STEP),))],
+        compiler_params=pltpu.CompilerParams(vmem_limit_bytes=16 * MIB),
+        cost_estimate=expert_cost(count, features, width // 3),
+        name="own_answer",
+    )(in_vmem(hidden), in_vmem(terms), in_hbm(down))
 
 
 def nothing(*refs):
@@ -160,6 +166,25 @@
         cost_estimate=pl.CostEstimate(flops=0, bytes_accessed=0, transcendentals=0),
         name="held",
     )(*values, *after)
+
+
+def append_kernel(rows_ref, terms_ref, out_ref):
+    features = rows_ref.shape[1]
+    out_ref[:, :features] = rows_ref[...]
+    out_ref[:, features:] = terms_ref[...]
+
+
+def append(rows, terms):
+    count, features = rows.shape
+    return pl.pallas_call(
+        append_kernel,
+        out_shape=jax.ShapeDtypeStruct((count, features + terms.shape[1]), rows.dtype),
+        in_specs=[whole()] * 2,
+        out_specs=whole(),
+        compiler_params=pltpu.CompilerParams(vmem_limit_bytes=16 * MIB),
+        cost_estimate=pl.CostEstimate(flops=0, bytes_accessed=4 * count * features, transcendentals=0),
+        name="append",
+    )(in_vmem(rows), in_vmem(terms))
 
 
 def expert_cost(count, features, width):
@@ -243,13 +268,17 @@
 def on_four_chips(tokens, expert_ids, gate_values, w_gate, w_up, w_down):
     experts = lax.axis_size("expert")
     weights = (w_gate[0], w_up[0], w_down[0])
+    wide, narrow = jnp.float32, jnp.bfloat16
     far = tuple(swap(w, (CORE, CORE)) for w in weights)
-    own, again = pack(tokens, expert_ids, gate_values, experts)
-    wide, narrow = jnp.float32, jnp.bfloat16
-    first = swap(own, FIRST)
-    near_own, *near = run_own(weights, experts, own)
-    second = swap(*held(again, after=[near_own]), SECOND)
+    first = swap(tokens, FIRST)
+    own, terms, hidden, near_gate, near_up = own_hidden(tokens, expert_ids, gate_values, *weights[:2], experts)
+    own, = held(own, after=far[:1])
+    second = swap(own, SECOND)
+    first = append(first, swap(terms, FIRST))
     third = swap(first, SECOND)
+
+    near_own, near_down = own_answer(hidden, terms, weights[2], experts)
+    near = (near_gate, near_up, near_down)
     near_run = functools.partial(run_expert, near, 0, experts)
     far_run = functools.partial(run_expert, far, CORE, experts)
     near_second = near_run(second, wide, after=[near_own])

time: 51.8 us -> 50.2 us (0.969)
  waiting for transfers between devices: 16 us -> 12.4 us
  starting transfers between devices: 15.2 us -> 17 us
    ppermute x11 -> x12, waiting for transfers between devices: 16 us -> 12.4 us  [swap(): lax.ppermute(value, 'expert', [(i, i ^ offsets[i % 2]) for i in range(siz...]
    ppermute x11 -> x12, starting transfers between devices: 15.2 us -> 17 us  [swap(): lax.ppermute(value, 'expert', [(i, i ^ offsets[i % 2]) for i in range(siz...]
    pallas_call x2 -> x3, Pallas kernels: 6.73 us -> 6.78 us  [the longest x1 4.17 us: own_hidden(): pl.pallas_call(functools.partial(own_hidden_kernel, experts), out_shape=[...]
  transfers between devices with their start and end apart: 11 -> 12, of which waited for: 6 -> 6; matrix products, arithmetic and copies ran while one was open for 0% -> 0% of each run, Pallas kernels for 37% -> 39%
where the time goes in v4:
time: 50.2 us; the launch traced here: 50 us
  Pallas kernels  20.4 us (41%)
  starting transfers between devices  17 us (34%)
  waiting for transfers between devices  12.4 us (25%)
    ppermute x12, starting transfers between devices, swap(): lax.ppermute(value, 'expert', [(i, i ^ offsets[i % 2]) for i in range(siz...  17 us
    pallas_call x7, Pallas kernels, run_expert(): pl.pallas_call(functools.partial(expert_kernel, experts, other, len(added...  12.6 us
    ppermute x12, waiting for transfers between devices, swap(): lax.ppermute(value, 'expert', [(i, i ^ offsets[i % 2]) for i in range(siz...  12.4 us
    pallas_call x1, Pallas kernels, own_hidden(): pl.pallas_call(functools.partial(own_hidden_kernel, experts), out_shape=[...  4.17 us
    pallas_call x1, Pallas kernels, own_answer(): pl.pallas_call(functools.partial(own_answer_kernel, experts), out_shape=[...  2.55 us
  transfers between devices with their start and end apart: 12, of which 6 were waited for; matrix products, arithmetic and copies ran while one was open for 0% of the time, Pallas kernels for 39%

profile of v4, /device:TPU:0, one launch (start us, length us, event | category | flops | bytes accessed | tf_op | source)
XLA Modules:
  0.0 50.0 jit_solution(9262471158894856663)
XLA Ops:
  0.0 0.5 collective-permute-start
  0.5 0.1 collective-permute-start.1
  0.5 0.5 collective-permute-start.2
  1.0 2.5 %collective-permute-start.5 = (bf16[128,2560]{1,0:T(8,128)(2,1)}, bf16[128,2560]{1,0:T(8,128)(2,1)S(1)}, u32[]{:S(2)}, u32[]{:S(2)}) collective-permute-start(bf16[128,2560]{1,0:T(8,128)(2,1)} %tokens_hbm.1), channel_id=1, source_target_pairs={{0,2},{1,5},{2,0},{3,7},{4,6},{5,1},{6,4},{7,3},{8,10},{9,13},{10,... | collective-permute-start | bytes 1966088 | tf_op jit(solution)/shard_map/ppermute | solution.py:35
  3.5 4.2 %own_hidden.1 = (bf16[128,2688]{1,0:T(8,128)(2,1)S(1)}, bf16[128,128]{1,0:T(8,128)(2,1)S(1)}, bf16[128,768]{1,0:T(8,128)(2,1)S(1)}, bf16[2560,768]{1,0:T(8,128)(2,1)S(1)}, bf16[2560,768]{1,0:T(8,128)(2,1)S(1)}) custom-call(bf16[128,2560]{1,0:T(8,128)(2,1)} %tokens_hbm.1, s32[6,128]{1,0:T(8,128)} %bitcast.11, f32[6,128]{1,0:T(8,128)} %bitcast.12, ...), custom_call_target="tpu_custom_call" | custom-call | flops 1509949440 | bytes 1310720 | tf_op jit(solution)/shard_map/own_hidden/pallas_call | solution.py:101
  7.6 0.0 collective-permute-done.refs_1_.refs_0_
  7.7 2.3 %collective-permute-start.3 = (bf16[128,2688]{1,0:T(8,128)(2,1)S(1)}, bf16[128,2688]{1,0:T(8,128)(2,1)S(1)}, u32[]{:S(2)}, u32[]{:S(2)}) collective-permute-start(bf16[128,2688]{1,0:T(8,128)(2,1)S(1)} %held.1.refs_3_), channel_id=1, source_target_pairs={{0,4},{1,3},{2,6},{3,1},{4,0},{5,7},{6,2},{7,5},{8,12},{9,11},{10,... | collective-permute-start | bytes 2064392 | tf_op jit(solution)/shard_map/ppermute | solution.py:35
  10.0 1.5 %collective-permute-start.6 = (bf16[128,128]{1,0:T(8,128)(2,1)S(1)}, bf16[128,128]{1,0:T(8,128)(2,1)S(1)}, u32[]{:S(2)}, u32[]{:S(2)}) collective-permute-start(bf16[128,128]{1,0:T(8,128)(2,1)S(1)} %get-tuple-element.22.terms_ref), channel_id=1, source_target_pairs={{0,2},{1,5},{2,0},{3,7},{4,6},{5,1},{6,4},{7,3},{8,10},{9,13},{10,... | collective-permute-start | bytes 98312 | tf_op jit(solution)/shard_map/ppermute | solution.py:35
  11.5 2.8 %collective-permute-done.6.terms_ref = bf16[128,128]{1,0:T(8,128)(2,1)S(1)} collective-permute-done((bf16[128,128]{1,0:T(8,128)(2,1)S(1)}, bf16[128,128]{1,0:T(8,128)(2,1)S(1)}, u32[]{:S(2)}, u32[]{:S(2)}) %collective-permute-start.6) | collective-permute-done | bytes 32800 | tf_op jit(solution)/shard_map/ppermute | solution.py:35
  14.4 2.3 %collective-permute-start.7 = (bf16[128,2688]{1,0:T(8,128)(2,1)S(1)}, bf16[128,2688]{1,0:T(8,128)(2,1)S(1)}, u32[]{:S(2)}, u32[]{:S(2)}) collective-permute-start(bf16[128,2688]{1,0:T(8,128)(2,1)S(1)} %append.1.refs_3_), channel_id=1, source_target_pairs={{0,4},{1,3},{2,6},{3,1},{4,0},{5,7},{6,2},{7,5},{8,12},{9,11},{10,... | collective-permute-start | bytes 2064392 | tf_op jit(solution)/shard_map/ppermute | solution.py:35
  16.6 2.6 %own_answer.1 = (f32[128,2560]{1,0:T(8,128)S(1)}, bf16[768,2560]{1,0:T(8,128)(2,1)S(1)}) custom-call(bf16[128,768]{1,0:T(8,128)(2,1)S(1)} %get-tuple-element.21.hidden_ref, bf16[128,128]{1,0:T(8,128)(2,1)S(1)} %get-tuple-element.22.terms_ref, bf16[768,2560]{1,0:T(8,128)(2,1)} %bitcast.10), custom_call_target="tpu_custom_call" | custom-call | flops 503316480 | bytes 1310720 | tf_op jit(solution)/shard_map/own_answer/pallas_call | solution.py:142
  19.2 0.6 %collective-permute-done.3.refs_3_ = bf16[128,2688]{1,0:T(8,128)(2,1)S(1)} collective-permute-done((bf16[128,2688]{1,0:T(8,128)(2,1)S(1)}, bf16[128,2688]{1,0:T(8,128)(2,1)S(1)}, u32[]{:S(2)}, u32[]{:S(2)}) %collective-permute-start.3) | collective-permute-done | bytes 688160 | tf_op jit(solution)/shard_map/ppermute | solution.py:35
  19.8 1.8 %expert.7.refs_4_ = f32[128,2560]{1,0:T(8,128)S(1)} custom-call(bf16[2560,768]{1,0:T(8,128)(2,1)S(1)} %get-tuple-element.24.refs_0_, bf16[2560,768]{1,0:T(8,128)(2,1)S(1)} %get-tuple-element.25.refs_1_, bf16[768,2560]{1,0:T(8,128)(2,1)S(1)} %get-tuple-element.26.refs_2_, bf16[128,2688]{1,0:T(8,128)(2,1)S(1)} %collective-permute-done.3.refs_3_, ...), custom_call_target="tpu_custom_call" | custom-call | flops 1509949440 | bytes 1310720 | tf_op jit(solution)/shard_map/expert/pallas_call | solution.py:224
  21.6 1.8 %expert.8.refs_4_ = bf16[128,2560]{1,0:T(8,128)(2,1)S(1)} custom-call(bf16[2560,768]{1,0:T(8,128)(2,1)S(1)} %collective-permute-done.refs_1_.refs_0_, bf16[2560,768]{1,0:T(8,128)(2,1)S(1)} %collective-permute-done.1.refs_1_, bf16[768,2560]{1,0:T(8,128)(2,1)S(1)} %collective-permute-done.2.refs_2_, bf16[128,2688]{1,0:T(8,128)(2,1)S(1)} %collective-permute-done.3.refs_3_, ...), custom_call_target="tpu_custom_call" | custom-call | flops 1509949440 | bytes 1310720 | tf_op jit(solution)/shard_map/expert/pallas_call | solution.py:224
  23.4 1.8 %collective-permute-start.4 = (bf16[128,2560]{1,0:T(8,128)(2,1)S(1)}, bf16[128,2560]{1,0:T(8,128)(2,1)S(1)}, u32[]{:S(2)}, u32[]{:S(2)}) collective-permute-start(bf16[128,2560]{1,0:T(8,128)(2,1)S(1)} %expert.8.refs_4_), channel_id=1, source_target_pairs={{0,4},{1,3},{2,6},{3,1},{4,0},{5,7},{6,2},{7,5},{8,12},{9,11},{10,... | collective-permute-start | bytes 1966088 | tf_op jit(solution)/shard_map/ppermute | solution.py:35
  25.2 2.0 %collective-permute-done.7.refs_3_ = bf16[128,2688]{1,0:T(8,128)(2,1)S(1)} collective-permute-done((bf16[128,2688]{1,0:T(8,128)(2,1)S(1)}, bf16[128,2688]{1,0:T(8,128)(2,1)S(1)}, u32[]{:S(2)}, u32[]{:S(2)}) %collective-permute-start.7) | collective-permute-done | bytes 688160 | tf_op jit(solution)/shard_map/ppermute | solution.py:35
  27.2 1.8 %expert.9 = (f32[64,2560]{1,0:T(8,128)S(1)}, f32[64,2560]{1,0:T(8,128)S(1)}) custom-call(bf16[2560,768]{1,0:T(8,128)(2,1)S(1)} %get-tuple-element.24.refs_0_, bf16[2560,768]{1,0:T(8,128)(2,1)S(1)} %get-tuple-element.25.refs_1_, bf16[768,2560]{1,0:T(8,128)(2,1)S(1)} %get-tuple-element.26.refs_2_, bf16[128,2688]{1,0:T(8,128)(2,1)S(1)} %collective-permute-done.7.refs_3_, ...), custom_call_target="tpu_custom_call" | custom-call | flops 1509949440 | bytes 1310720 | tf_op jit(solution)/shard_map/expert/pallas_call | solution.py:224
  28.9 1.8 %expert.10 = (bf16[64,2560]{1,0:T(8,128)(2,1)S(1)}, bf16[64,2560]{1,0:T(8,128)(2,1)S(1)}) custom-call(bf16[2560,768]{1,0:T(8,128)(2,1)S(1)} %collective-permute-done.refs_1_.refs_0_, bf16[2560,768]{1,0:T(8,128)(2,1)S(1)} %collective-permute-done.1.refs_1_, bf16[768,2560]{1,0:T(8,128)(2,1)S(1)} %collective-permute-done.2.refs_2_, ...), custom_call_target="tpu_custom_call" | custom-call | flops 1509949440 | bytes 1310720 | tf_op jit(solution)/shard_map/expert/pallas_call | solution.py:224
  30.7 1.8 %collective-permute-start.10 = (bf16[64,2560]{1,0:T(8,128)(2,1)S(1)}, bf16[64,2560]{1,0:T(8,128)(2,1)S(1)}, u32[]{:S(2)}, u32[]{:S(2)}) collective-permute-start(bf16[64,2560]{1,0:T(8,128)(2,1)S(1)} %get-tuple-element.30.refs_5_), channel_id=1, source_target_pairs={{0,4},{1,3},{2,6},{3,1},{4,0},{5,7},{6,2},{7,5},{8,12},{9,11},{10,... | collective-permute-start | bytes 983048 | tf_op jit(solution)/shard_map/ppermute | solution.py:35
  32.5 0.3 collective-permute-start.8
  32.8 1.8 %expert.11 = (f32[64,2560]{1,0:T(8,128)S(1)}, f32[64,2560]{1,0:T(8,128)S(1)}) custom-call(bf16[2560,768]{1,0:T(8,128)(2,1)S(1)} %get-tuple-element.24.refs_0_, bf16[2560,768]{1,0:T(8,128)(2,1)S(1)} %get-tuple-element.25.refs_1_, bf16[768,2560]{1,0:T(8,128)(2,1)S(1)} %get-tuple-element.26.refs_2_, bf16[128,2688]{1,0:T(8,128)(2,1)S(1)} %append.1.refs_3_, ...), custom_call_target="tpu_custom_call" | custom-call | flops 1509949440 | bytes 1310720 | tf_op jit(solution)/shard_map/expert/pallas_call | solution.py:224
  34.6 2.0 %expert.12 = (f32[64,2560]{1,0:T(8,128)S(1)}, f32[64,2560]{1,0:T(8,128)S(1)}) custom-call(bf16[2560,768]{1,0:T(8,128)(2,1)S(1)} %collective-permute-done.refs_1_.refs_0_, bf16[2560,768]{1,0:T(8,128)(2,1)S(1)} %collective-permute-done.1.refs_1_, bf16[768,2560]{1,0:T(8,128)(2,1)S(1)} %collective-permute-done.2.refs_2_, bf16[128,2688]{1,0:T(8,128)(2,1)S(1)} %append.1.refs_3_, ...), custom_call_target="tpu_custom_call" | custom-call | flops 1509949440 | bytes 1310720 | tf_op jit(solution)/shard_map/expert/pallas_call | solution.py:224
  36.6 1.8 %expert.13.refs_0_.whole_ref = f32[128,2560]{1,0:T(8,128)S(1)} custom-call(bf16[2560,768]{1,0:T(8,128)(2,1)S(1)} %collective-permute-done.refs_1_.refs_0_, bf16[2560,768]{1,0:T(8,128)(2,1)S(1)} %collective-permute-done.1.refs_1_, bf16[768,2560]{1,0:T(8,128)(2,1)S(1)} %collective-permute-done.2.refs_2_, bf16[128,2688]{1,0:T(8,128)(2,1)S(1)} %held.1.refs_3_, ...), custom_call_target="tpu_custom_call" | custom-call | flops 1509949440 | bytes 1310720 | tf_op jit(solution)/shard_map/expert/pallas_call | solution.py:224
  38.4 0.0 collective-permute-done.10.second_ref
  38.4 0.1 sums.3
  38.4 1.8 %collective-permute-start.11 = (bf16[64,2560]{1,0:T(8,128)(2,1)S(1)}, bf16[64,2560]{1,0:T(8,128)(2,1)S(1)}, u32[]{:S(2)}, u32[]{:S(2)}) collective-permute-start(bf16[64,2560]{1,0:T(8,128)(2,1)S(1)} %sums.3), channel_id=1, source_target_pairs={{0,2},{1,5},{2,0},{3,7},{4,6},{5,1},{6,4},{7,3},{8,10},{9,13},{10,... | collective-permute-start | bytes 983048 | tf_op jit(solution)/shard_map/ppermute | solution.py:35
  40.2 1.3 %collective-permute-done.8.second_ref = bf16[64,2560]{1,0:T(8,128)(2,1)S(1)} collective-permute-done((bf16[64,2560]{1,0:T(8,128)(2,1)S(1)}, bf16[64,2560]{1,0:T(8,128)(2,1)S(1)}, u32[]{:S(2)}, u32[]{:S(2)}) %collective-permute-start.8) | collective-permute-done | bytes 327712 | tf_op jit(solution)/shard_map/ppermute | solution.py:35
  41.5 0.1 sums.2
  41.6 1.8 %collective-permute-start.9 = (bf16[64,2560]{1,0:T(8,128)(2,1)S(1)}, bf16[64,2560]{1,0:T(8,128)(2,1)S(1)}, u32[]{:S(2)}, u32[]{:S(2)}) collective-permute-start(bf16[64,2560]{1,0:T(8,128)(2,1)S(1)} %sums.2), channel_id=1, source_target_pairs={{0,2},{1,5},{2,0},{3,7},{4,6},{5,1},{6,4},{7,3},{8,10},{9,13},{10,... | collective-permute-start | bytes 983048 | tf_op jit(solution)/shard_map/ppermute | solution.py:35
  43.4 2.2 %collective-permute-done.11.lower_ref = bf16[64,2560]{1,0:T(8,128)(2,1)S(1)} collective-permute-done((bf16[64,2560]{1,0:T(8,128)(2,1)S(1)}, bf16[64,2560]{1,0:T(8,128)(2,1)S(1)}, u32[]{:S(2)}, u32[]{:S(2)}) %collective-permute-start.11) | collective-permute-done | bytes 327712 | tf_op jit(solution)/shard_map/ppermute | solution.py:35
  45.6 3.5 %collective-permute-done.9.upper_ref = bf16[64,2560]{1,0:T(8,128)(2,1)S(1)} collective-permute-done((bf16[64,2560]{1,0:T(8,128)(2,1)S(1)}, bf16[64,2560]{1,0:T(8,128)(2,1)S(1)}, u32[]{:S(2)}, u32[]{:S(2)}) %collective-permute-start.9) | collective-permute-done | bytes 327712 | tf_op jit(solution)/shard_map/ppermute | solution.py:35
  49.1 0.9 %finish.1 = bf16[128,2560]{1,0:T(8,128)(2,1)} custom-call(f32[128,2560]{1,0:T(8,128)S(1)} %expert.13.refs_0_.whole_ref, bf16[64,2560]{1,0:T(8,128)(2,1)S(1)} %collective-permute-done.9.upper_ref, bf16[64,2560]{1,0:T(8,128)(2,1)S(1)} %collective-permute-done.11.lower_ref), custom_call_target="tpu_custom_call" | custom-call | tf_op jit(solution)/shard_map/finish/pallas_call | solution.py:258
  (6 shorter events, 0.1 us)
Async XLA Ops:
  0.0 7.6 %collective-permute-start = (bf16[2560,768]{1,0:T(8,128)(2,1)}, bf16[2560,768]{1,0:T(8,128)(2,1)S(1)}, u32[]{:S(2)}, u32[]{:S(2)}) collective-permute-start(bf16[2560,768]{1,0:T(8,128)(2,1)} %bitcast.5), channel_id=1, source_target_pairs={{0,1},{1,0},{2,3},{3,2},{4,5},{5,4},{6,7},{7,6},{8,9},{9,8},{10,11... | collective-permute-start | bytes 11796488 | tf_op jit(solution)/shard_map/ppermute | solution.py:35
  0.5 21.1 %collective-permute-start.1 = (bf16[2560,768]{1,0:T(8,128)(2,1)}, bf16[2560,768]{1,0:T(8,128)(2,1)S(1)}, u32[]{:S(2)}, u32[]{:S(2)}) collective-permute-start(bf16[2560,768]{1,0:T(8,128)(2,1)} %bitcast.7), channel_id=1, source_target_pairs={{0,1},{1,0},{2,3},{3,2},{4,5},{5,4},{6,7},{7,6},{8,9},{9,8},{10,11... | collective-permute-start | bytes 11796488 | tf_op jit(solution)/shard_map/ppermute | solution.py:35
  0.5 21.1 %collective-permute-start.2 = (bf16[768,2560]{1,0:T(8,128)(2,1)}, bf16[768,2560]{1,0:T(8,128)(2,1)S(1)}, u32[]{:S(2)}, u32[]{:S(2)}) collective-permute-start(bf16[768,2560]{1,0:T(8,128)(2,1)} %bitcast.9), channel_id=1, source_target_pairs={{0,1},{1,0},{2,3},{3,2},{4,5},{5,4},{6,7},{7,6},{8,9},{9,8},{10,11... | collective-permute-start | bytes 11796488 | tf_op jit(solution)/shard_map/ppermute | solution.py:35
  1.0 13.3 %collective-permute-start.5 = (bf16[128,2560]{1,0:T(8,128)(2,1)}, bf16[128,2560]{1,0:T(8,128)(2,1)S(1)}, u32[]{:S(2)}, u32[]{:S(2)}) collective-permute-start(bf16[128,2560]{1,0:T(8,128)(2,1)} %tokens_hbm.1), channel_id=1, source_target_pairs={{0,2},{1,5},{2,0},{3,7},{4,6},{5,1},{6,4},{7,3},{8,10},{9,13},{10,... | collective-permute-start | bytes 1966088 | tf_op jit(solution)/shard_map/ppermute | solution.py:35
  7.7 12.1 %collective-permute-start.3 = (bf16[128,2688]{1,0:T(8,128)(2,1)S(1)}, bf16[128,2688]{1,0:T(8,128)(2,1)S(1)}, u32[]{:S(2)}, u32[]{:S(2)}) collective-permute-start(bf16[128,2688]{1,0:T(8,128)(2,1)S(1)} %held.1.refs_3_), channel_id=1, source_target_pairs={{0,4},{1,3},{2,6},{3,1},{4,0},{5,7},{6,2},{7,5},{8,12},{9,11},{10,... | collective-permute-start | bytes 2064392 | tf_op jit(solution)/shard_map/ppermute | solution.py:35
  10.0 4.3 %collective-permute-start.6 = (bf16[128,128]{1,0:T(8,128)(2,1)S(1)}, bf16[128,128]{1,0:T(8,128)(2,1)S(1)}, u32[]{:S(2)}, u32[]{:S(2)}) collective-permute-start(bf16[128,128]{1,0:T(8,128)(2,1)S(1)} %get-tuple-element.22.terms_ref), channel_id=1, source_target_pairs={{0,2},{1,5},{2,0},{3,7},{4,6},{5,1},{6,4},{7,3},{8,10},{9,13},{10,... | collective-permute-start | bytes 98312 | tf_op jit(solution)/shard_map/ppermute | solution.py:35
  14.4 12.8 %collective-permute-start.7 = (bf16[128,2688]{1,0:T(8,128)(2,1)S(1)}, bf16[128,2688]{1,0:T(8,128)(2,1)S(1)}, u32[]{:S(2)}, u32[]{:S(2)}) collective-permute-start(bf16[128,2688]{1,0:T(8,128)(2,1)S(1)} %append.1.refs_3_), channel_id=1, source_target_pairs={{0,4},{1,3},{2,6},{3,1},{4,0},{5,7},{6,2},{7,5},{8,12},{9,11},{10,... | collective-permute-start | bytes 2064392 | tf_op jit(solution)/shard_map/ppermute | solution.py:35
  23.4 13.2 %collective-permute-start.4 = (bf16[128,2560]{1,0:T(8,128)(2,1)S(1)}, bf16[128,2560]{1,0:T(8,128)(2,1)S(1)}, u32[]{:S(2)}, u32[]{:S(2)}) collective-permute-start(bf16[128,2560]{1,0:T(8,128)(2,1)S(1)} %expert.8.refs_4_), channel_id=1, source_target_pairs={{0,4},{1,3},{2,6},{3,1},{4,0},{5,7},{6,2},{7,5},{8,12},{9,11},{10,... | collective-permute-start | bytes 1966088 | tf_op jit(solution)/shard_map/ppermute | solution.py:35
  30.7 7.7 %collective-permute-start.10 = (bf16[64,2560]{1,0:T(8,128)(2,1)S(1)}, bf16[64,2560]{1,0:T(8,128)(2,1)S(1)}, u32[]{:S(2)}, u32[]{:S(2)}) collective-permute-start(bf16[64,2560]{1,0:T(8,128)(2,1)S(1)} %get-tuple-element.30.refs_5_), channel_id=1, source_target_pairs={{0,4},{1,3},{2,6},{3,1},{4,0},{5,7},{6,2},{7,5},{8,12},{9,11},{10,... | collective-permute-start | bytes 983048 | tf_op jit(solution)/shard_map/ppermute | solution.py:35
  32.5 9.0 %collective-permute-start.8 = (bf16[64,2560]{1,0:T(8,128)(2,1)S(1)}, bf16[64,2560]{1,0:T(8,128)(2,1)S(1)}, u32[]{:S(2)}, u32[]{:S(2)}) collective-permute-start(bf16[64,2560]{1,0:T(8,128)(2,1)S(1)} %get-tuple-element.29.refs_4_), channel_id=1, source_target_pairs={{0,4},{1,3},{2,6},{3,1},{4,0},{5,7},{6,2},{7,5},{8,12},{9,11},{10,... | collective-permute-start | bytes 983048 | tf_op jit(solution)/shard_map/ppermute | solution.py:35
  38.4 7.1 %collective-permute-start.11 = (bf16[64,2560]{1,0:T(8,128)(2,1)S(1)}, bf16[64,2560]{1,0:T(8,128)(2,1)S(1)}, u32[]{:S(2)}, u32[]{:S(2)}) collective-permute-start(bf16[64,2560]{1,0:T(8,128)(2,1)S(1)} %sums.3), channel_id=1, source_target_pairs={{0,2},{1,5},{2,0},{3,7},{4,6},{5,1},{6,4},{7,3},{8,10},{9,13},{10,... | collective-permute-start | bytes 983048 | tf_op jit(solution)/shard_map/ppermute | solution.py:35
  41.6 7.5 %collective-permute-start.9 = (bf16[64,2560]{1,0:T(8,128)(2,1)S(1)}, bf16[64,2560]{1,0:T(8,128)(2,1)S(1)}, u32[]{:S(2)}, u32[]{:S(2)}) collective-permute-start(bf16[64,2560]{1,0:T(8,128)(2,1)S(1)} %sums.2), channel_id=1, source_target_pairs={{0,2},{1,5},{2,0},{3,7},{4,6},{5,1},{6,4},{7,3},{8,10},{9,13},{10,... | collective-permute-start | bytes 983048 | tf_op jit(solution)/shard_map/ppermute | solution.py:35

commit v5 on v4

--- a/solution.py
+++ b/solution.py
@@ -37,11 +37,11 @@
 
 def row_terms(ids, gates, experts):
     topk, rows = ids.shape
-    line = lax.broadcasted_iota(jnp.int32, (LANES, rows), 0)
+    line = lax.broadcasted_iota(jnp.int32, (4 * experts, rows), 0)
     expert = line
-    for _ in range(2):
+    for _ in range(3):
         expert = jnp.where(expert >= experts, expert - experts, expert)
-    weight = jnp.zeros((LANES, rows), jnp.float32)
+    weight = jnp.zeros(line.shape, jnp.float32)
     for k in range(topk):
         weight += jnp.where(expert == ids[k : k + 1, :], gates[k : k + 1, :], 0.0)
     high = weight.astype(jnp.bfloat16).astype(jnp.float32)
@@ -49,15 +49,34 @@
     middle = rest.astype(jnp.bfloat16).astype(jnp.float32)
     low = rest - middle
     terms = jnp.where(line < experts, high, jnp.where(line < 2 * experts, middle, low))
-    return jnp.where(line < 3 * experts, terms, 0.0).T.astype(jnp.bfloat16)
+    return jnp.where(line < 3 * experts, terms, 0.0).astype(jnp.bfloat16)
 
 
 def row_weights(terms, experts, other):
-    terms = terms.astype(jnp.float32)
-    lane = lax.broadcasted_iota(jnp.int32, terms.shape, 1)
+    count = terms.shape[1]
+    line = lax.broadcasted_iota(jnp.int32, terms.shape, 0)
     own = lax.axis_index("expert") ^ other
-    chosen = (lane == own) | (lane == own + experts) | (lane == own + 2 * experts)
-    return jnp.sum(jnp.where(chosen, terms, 0.0), axis=1, keepdims=True)
+    chosen = (line == own) | (line == own + experts) | (line == own + 2 * experts)
+    weights = jnp.sum(jnp.where(chosen, terms.astype(jnp.float32), 0.0), axis=0, keepdims=True)
+    square = (count, count)
+    same = lax.broadcasted_iota(jnp.int32, square, 0) == lax.broadcasted_iota(jnp.int32, square, 1)
+    return jnp.sum(jnp.where(same, jnp.broadcast_to(weights, square), 0.0), axis=1, keepdims=True)
+
+
+def put_blocks(rows, terms, out_ref):
+    count, features = rows.shape
+    for i in range(features // LANES):
+        out_ref[i * count : (i + 1) * count, :] = rows[:, i * LANES : (i + 1) * LANES]
+    out_ref[features // LANES * count :, :] = terms
+
+
+def rows_of(blocks_ref, features):
+    count = LANES
+    return jnp.concatenate([blocks_ref[i * count : (i + 1) * count, :] for i in range(features // LANES)], axis=1)
+
+
+def terms_of(blocks_ref, features):
+    return blocks_ref[features:, :]
 
 
 def hidden_columns(rows, gate_ref, up_ref, columns):
@@ -67,11 +86,10 @@
 
 
 def own_hidden_kernel(
-    experts, tokens_hbm, ids_hbm, gates_hbm, gate_hbm, up_hbm, rows_ref, terms_ref, hidden_ref, gate_ref, up_ref, ids, gates, done
+    experts, tokens_hbm, ids_hbm, gates_hbm, gate_hbm, up_hbm, blocks_ref, terms_ref, hidden_ref, gate_ref, up_ref, ids, gates, tokens, done
 ):
-    rows, features = tokens_hbm.shape
     width = gate_ref.shape[1]
-    pairs = [(ids_hbm, ids), (gates_hbm, gates), (tokens_hbm, rows_ref.at[:, pl.ds(0, features)])]
+    pairs = [(ids_hbm, ids), (gates_hbm, gates), (tokens_hbm, tokens)]
     for at in range(0, width, STEP):
         columns = pl.ds(at, STEP)
         pairs.append((gate_hbm.at[:, columns], gate_ref.at[:, columns]))
@@ -83,9 +101,9 @@
     copies[1].wait()
     terms = row_terms(ids, gates, experts)
     terms_ref[...] = terms
-    rows_ref[:, features:] = terms
     copies[2].wait()
-    rows = rows_ref[:, :features]
+    rows = tokens[...]
+    put_blocks(rows, terms, blocks_ref)
     waits = iter(copies[3:])
     for at in range(0, width, STEP):
         next(waits).wait()
@@ -101,8 +119,8 @@
     return pl.pallas_call(
         functools.partial(own_hidden_kernel, experts),
         out_shape=[
-            jax.ShapeDtypeStruct((count, features + LANES), tokens.dtype),
-            jax.ShapeDtypeStruct((count, LANES), tokens.dtype),
+            jax.ShapeDtypeStruct((features + 4 * experts, LANES), tokens.dtype),
+            jax.ShapeDtypeStruct((4 * experts, LANES), tokens.dtype),
             jax.ShapeDtypeStruct((count, width), tokens.dtype),
             jax.ShapeDtypeStruct(gate.shape, gate.dtype),
             jax.ShapeDtypeStruct(up.shape, up.dtype),
@@ -112,6 +130,7 @@
         scratch_shapes=[
             pltpu.VMEM(ids.shape, ids.dtype),
             pltpu.VMEM(gates.shape, gates.dtype),
+            pltpu.VMEM(tokens.shape, tokens.dtype),
             pltpu.SemaphoreType.DMA((3 + 2 * (width // STEP),)),
         ],
         compiler_params=pltpu.CompilerParams(vmem_limit_bytes=16 * MIB),
@@ -168,23 +187,21 @@
     )(*values, *after)
 
 
-def append_kernel(rows_ref, terms_ref, out_ref):
-    features = rows_ref.shape[1]
-    out_ref[:, :features] = rows_ref[...]
-    out_ref[:, features:] = terms_ref[...]
-
-
-def append(rows, terms):
+def append_kernel(rows_ref, terms_ref, *refs):
+    put_blocks(rows_ref[...], terms_ref[...], refs[-1])
+
+
+def append(rows, terms, *after):
     count, features = rows.shape
     return pl.pallas_call(
         append_kernel,
-        out_shape=jax.ShapeDtypeStruct((count, features + terms.shape[1]), rows.dtype),
-        in_specs=[whole()] * 2,
+        out_shape=jax.ShapeDtypeStruct((features + terms.shape[0], LANES), rows.dtype),
+        in_specs=[whole()] * 2 + [anywhere()] * len(after),
         out_specs=whole(),
         compiler_params=pltpu.CompilerParams(vmem_limit_bytes=16 * MIB),
         cost_estimate=pl.CostEstimate(flops=0, bytes_accessed=4 * count * features, transcendentals=0),
         name="append",
-    )(in_vmem(rows), in_vmem(terms))
+    )(in_vmem(rows), in_vmem(terms), *after)
 
 
 def expert_cost(count, features, width):
@@ -194,13 +211,13 @@
 
 
 def expert_kernel(experts, other, added, after, parts, *refs):
-    gate_ref, up_ref, down_ref, rows_ref = refs[:4]
+    gate_ref, up_ref, down_ref, blocks_ref = refs[:4]
     added_refs = refs[4 : 4 + added * parts]
     out_refs = refs[4 + added * parts + after : -1]
     hidden_ref = refs[-1]
     features, width = gate_ref.shape
-    rows = rows_ref[:, :features]
-    weight = row_weights(rows_ref[:, features:], experts, other)
+    rows = rows_of(blocks_ref, features)
+    weight = row_weights(terms_of(blocks_ref, features), experts, other)
     for at in range(0, width, STEP):
         columns = slice(at, at + STEP)
         hidden_ref[:, columns] = hidden_columns(rows, gate_ref, up_ref, columns)
@@ -217,10 +234,10 @@
             start += out_ref.shape[0]
 
 
-def run_expert(weights, other, experts, rows, kind, *added, parts=1, after=()):
+def run_expert(weights, other, experts, blocks, kind, *added, parts=1, after=()):
     features, width = weights[0].shape
-    count = rows.shape[0]
-    operands = [in_vmem(v) for v in (*weights, rows, *(v for group in added for v in group))]
+    count = LANES
+    operands = [in_vmem(v) for v in (*weights, blocks, *(v for group in added for v in group))]
     return pl.pallas_call(
         functools.partial(expert_kernel, experts, other, len(added), len(after), parts),
         out_shape=[jax.ShapeDtypeStruct((count // parts, features), kind)] * parts,
@@ -274,21 +291,21 @@
     own, terms, hidden, near_gate, near_up = own_hidden(tokens, expert_ids, gate_values, *weights[:2], experts)
     own, = held(own, after=far[:1])
     second = swap(own, SECOND)
-    first = append(first, swap(terms, FIRST))
+    near_own, near_down = own_answer(hidden, terms, weights[2], experts)
+    first = append(first, swap(terms, FIRST), near_own)
     third = swap(first, SECOND)
 
-    near_own, near_down = own_answer(hidden, terms, weights[2], experts)
     near = (near_gate, near_up, near_down)
     near_run = functools.partial(run_expert, near, 0, experts)
     far_run = functools.partial(run_expert, far, CORE, experts)
-    near_second = near_run(second, wide, after=[near_own])
+    near_first = near_run(first, wide, parts=2, after=[near_own])
+    near_second = near_run(second, wide, after=near_first)
     sum_second = far_run(second, narrow, near_second)
     back_second = swap(sum_second[0], SECOND)
     near_third = near_run(third, wide, parts=2, after=sum_second)
     sum_third = far_run(third, narrow, near_third, parts=2)
     passed_a, passed_b = swap(sum_third[0], SECOND), swap(sum_third[1], SECOND)
-    near_first = near_run(first, wide, parts=2, after=sum_third)
-    sum_first = far_run(first, wide, near_first, parts=2)
+    sum_first = far_run(first, wide, near_first, parts=2, after=sum_third)
     sum_own = far_run(own, wide, [near_own], [back_second], after=sum_first)[0]
     back_first_a = swap(sums(sum_first[0], passed_a, after=[sum_own]), FIRST)
     back_first_b = swap(sums(sum_first[1], passed_b, after=[sum_own]), FIRST)
@@ -339,7 +356,10 @@
         P("expert", None, None),
         P("expert", None, None),
     )
-    body = on_four_chips if mesh.shape["expert"] == 8 else dispatched
+    def body(tokens, *others):
+        here = mesh.shape["expert"] == 8 and tokens.shape[0] == LANES
+        return (on_four_chips if here else dispatched)(tokens, *others)
+
     return jax.shard_map(
         body, mesh=mesh, in_specs=placed, out_specs=P(("dp", "expert"), None), check_vma=False
     )

time: 50.2 us -> 49.3 us (0.982)
  waiting for transfers between devices: 12.4 us -> 11.5 us
    ppermute x12, waiting for transfers between devices: 12.4 us -> 11.5 us  [swap(): lax.ppermute(value, 'expert', [(i, i ^ offsets[i % 2]) for i in range(siz...]
  transfers between devices with their start and end apart: 12 -> 12, of which waited for: 6 -> 6; matrix products, arithmetic and copies ran while one was open for 0% -> 0% of each run, Pallas kernels for 39% -> 40%
where the time goes in v5:
time: 49.3 us; the launch traced here: 49.1 us
  Pallas kernels  20.8 us (42%)
  starting transfers between devices  16.6 us (34%)
  waiting for transfers between devices  11.5 us (23%)
    ppermute x12, starting transfers between devices, swap(): lax.ppermute(value, 'expert', [(i, i ^ offsets[i % 2]) for i in range(siz...  16.6 us
    pallas_call x7, Pallas kernels, run_expert(): pl.pallas_call(functools.partial(expert_kernel, experts, other, len(added...  12.8 us
    ppermute x12, waiting for transfers between devices, swap(): lax.ppermute(value, 'expert', [(i, i ^ offsets[i % 2]) for i in range(siz...  11.5 us
    pallas_call x1, Pallas kernels, own_hidden(): pl.pallas_call(functools.partial(own_hidden_kernel, experts), out_shape=[...  4.2 us
    pallas_call x1, Pallas kernels, own_answer(): pl.pallas_call(functools.partial(own_answer_kernel, experts), out_shape=[...  2.55 us
  transfers between devices with their start and end apart: 12, of which 6 were waited for; matrix products, arithmetic and copies ran while one was open for 0% of the time, Pallas kernels for 40%

profile of v5, /device:TPU:0, one launch (start us, length us, event | category | flops | bytes accessed | tf_op | source)
XLA Modules:
  0.0 49.1 jit_solution(2011626397027053687)
XLA Ops:
  0.0 0.5 collective-permute-start
  0.5 0.1 collective-permute-start.1
  0.5 0.5 collective-permute-start.2
  1.0 2.5 %collective-permute-start.4 = (bf16[128,2560]{1,0:T(8,128)(2,1)}, bf16[128,2560]{1,0:T(8,128)(2,1)S(1)}, u32[]{:S(2)}, u32[]{:S(2)}) collective-permute-start(bf16[128,2560]{1,0:T(8,128)(2,1)} %tokens_hbm.1), channel_id=1, source_target_pairs={{0,2},{1,5},{2,0},{3,7},{4,6},{5,1},{6,4},{7,3},{8,10},{9,13},{10,... | collective-permute-start | bytes 1966088 | tf_op jit(solution)/shard_map/ppermute | solution.py:35
  3.5 4.2 %own_hidden.1 = (bf16[2592,128]{1,0:T(8,128)(2,1)S(1)}, bf16[32,128]{1,0:T(8,128)(2,1)S(1)}, bf16[128,768]{1,0:T(8,128)(2,1)S(1)}, bf16[2560,768]{1,0:T(8,128)(2,1)S(1)}, bf16[2560,768]{1,0:T(8,128)(2,1)S(1)}) custom-call(bf16[128,2560]{1,0:T(8,128)(2,1)} %tokens_hbm.1, s32[6,128]{1,0:T(8,128)} %bitcast.11, f32[6,128]{1,0:T(8,128)} %bitcast.12, ...), custom_call_target="tpu_custom_call" | custom-call | flops 1509949440 | bytes 1310720 | tf_op jit(solution)/shard_map/own_hidden/pallas_call | solution.py:119
  7.7 2.3 %collective-permute-start.3 = (bf16[2592,128]{1,0:T(8,128)(2,1)S(1)}, bf16[2592,128]{1,0:T(8,128)(2,1)S(1)}, u32[]{:S(2)}, u32[]{:S(2)}) collective-permute-start(bf16[2592,128]{1,0:T(8,128)(2,1)S(1)} %held.1.refs_3_), channel_id=1, source_target_pairs={{0,4},{1,3},{2,6},{3,1},{4,0},{5,7},{6,2},{7,5},{8,12},{9,11},{10,... | collective-permute-start | bytes 1990664 | tf_op jit(solution)/shard_map/ppermute | solution.py:35
  10.0 1.5 %collective-permute-start.5 = (bf16[32,128]{1,0:T(8,128)(2,1)S(1)}, bf16[32,128]{1,0:T(8,128)(2,1)S(1)}, u32[]{:S(2)}, u32[]{:S(2)}) collective-permute-start(bf16[32,128]{1,0:T(8,128)(2,1)S(1)} %get-tuple-element.22.terms_ref), channel_id=1, source_target_pairs={{0,2},{1,5},{2,0},{3,7},{4,6},{5,1},{6,4},{7,3},{8,10},{9,13},{10,... | collective-permute-start | bytes 24584 | tf_op jit(solution)/shard_map/ppermute | solution.py:35
  11.5 2.6 %own_answer.1 = (f32[128,2560]{1,0:T(8,128)S(1)}, bf16[768,2560]{1,0:T(8,128)(2,1)S(1)}) custom-call(bf16[128,768]{1,0:T(8,128)(2,1)S(1)} %get-tuple-element.21.hidden_ref, bf16[32,128]{1,0:T(8,128)(2,1)S(1)} %get-tuple-element.22.terms_ref, bf16[768,2560]{1,0:T(8,128)(2,1)} %bitcast.10), custom_call_target="tpu_custom_call" | custom-call | flops 503316480 | bytes 1310720 | tf_op jit(solution)/shard_map/own_answer/pallas_call | solution.py:161
  14.0 0.0 collective-permute-done.5.terms_ref
  14.1 0.1 append.1.refs_3_
  14.2 2.0 %collective-permute-start.7 = (bf16[2592,128]{1,0:T(8,128)(2,1)S(1)}, bf16[2592,128]{1,0:T(8,128)(2,1)S(1)}, u32[]{:S(2)}, u32[]{:S(2)}) collective-permute-start(bf16[2592,128]{1,0:T(8,128)(2,1)S(1)} %append.1.refs_3_), channel_id=1, source_target_pairs={{0,4},{1,3},{2,6},{3,1},{4,0},{5,7},{6,2},{7,5},{8,12},{9,11},{10,... | collective-permute-start | bytes 1990664 | tf_op jit(solution)/shard_map/ppermute | solution.py:35
  16.1 1.8 %expert.7 = (f32[64,2560]{1,0:T(8,128)S(1)}, f32[64,2560]{1,0:T(8,128)S(1)}) custom-call(bf16[2560,768]{1,0:T(8,128)(2,1)S(1)} %get-tuple-element.24.refs_0_, bf16[2560,768]{1,0:T(8,128)(2,1)S(1)} %get-tuple-element.25.refs_1_, bf16[768,2560]{1,0:T(8,128)(2,1)S(1)} %get-tuple-element.26.refs_2_, bf16[2592,128]{1,0:T(8,128)(2,1)S(1)} %append.1.refs_3_, ...), custom_call_target="tpu_custom_call" | custom-call | flops 1509949440 | bytes 1310720 | tf_op jit(solution)/shard_map/expert/pallas_call | solution.py:241
  18.0 1.3 %collective-permute-done.3.refs_3_ = bf16[2592,128]{1,0:T(8,128)(2,1)S(1)} collective-permute-done((bf16[2592,128]{1,0:T(8,128)(2,1)S(1)}, bf16[2592,128]{1,0:T(8,128)(2,1)S(1)}, u32[]{:S(2)}, u32[]{:S(2)}) %collective-permute-start.3) | collective-permute-done | bytes 663584 | tf_op jit(solution)/shard_map/ppermute | solution.py:35
  19.3 1.8 %expert.8.refs_4_ = f32[128,2560]{1,0:T(8,128)S(1)} custom-call(bf16[2560,768]{1,0:T(8,128)(2,1)S(1)} %get-tuple-element.24.refs_0_, bf16[2560,768]{1,0:T(8,128)(2,1)S(1)} %get-tuple-element.25.refs_1_, bf16[768,2560]{1,0:T(8,128)(2,1)S(1)} %get-tuple-element.26.refs_2_, bf16[2592,128]{1,0:T(8,128)(2,1)S(1)} %collective-permute-done.3.refs_3_, ...), custom_call_target="tpu_custom_call" | custom-call | flops 1509949440 | bytes 1310720 | tf_op jit(solution)/shard_map/expert/pallas_call | solution.py:241
  21.1 1.8 %expert.9.refs_4_ = bf16[128,2560]{1,0:T(8,128)(2,1)S(1)} custom-call(bf16[2560,768]{1,0:T(8,128)(2,1)S(1)} %collective-permute-done.refs_1_.refs_0_, bf16[2560,768]{1,0:T(8,128)(2,1)S(1)} %collective-permute-done.1.refs_1_, bf16[768,2560]{1,0:T(8,128)(2,1)S(1)} %collective-permute-done.2.refs_2_, bf16[2592,128]{1,0:T(8,128)(2,1)S(1)} %collective-permute-done.3.refs_3_, ...), custom_call_target="tpu_custom_call" | custom-call | flops 1509949440 | bytes 1310720 | tf_op jit(solution)/shard_map/expert/pallas_call | solution.py:241
  22.8 1.8 %collective-permute-start.6 = (bf16[128,2560]{1,0:T(8,128)(2,1)S(1)}, bf16[128,2560]{1,0:T(8,128)(2,1)S(1)}, u32[]{:S(2)}, u32[]{:S(2)}) collective-permute-start(bf16[128,2560]{1,0:T(8,128)(2,1)S(1)} %expert.9.refs_4_), channel_id=1, source_target_pairs={{0,4},{1,3},{2,6},{3,1},{4,0},{5,7},{6,2},{7,5},{8,12},{9,11},{10,... | collective-permute-start | bytes 1966088 | tf_op jit(solution)/shard_map/ppermute | solution.py:35
  24.7 1.7 %collective-permute-done.7.refs_3_ = bf16[2592,128]{1,0:T(8,128)(2,1)S(1)} collective-permute-done((bf16[2592,128]{1,0:T(8,128)(2,1)S(1)}, bf16[2592,128]{1,0:T(8,128)(2,1)S(1)}, u32[]{:S(2)}, u32[]{:S(2)}) %collective-permute-start.7) | collective-permute-done | bytes 663584 | tf_op jit(solution)/shard_map/ppermute | solution.py:35
  26.4 1.8 %expert.10 = (f32[64,2560]{1,0:T(8,128)S(1)}, f32[64,2560]{1,0:T(8,128)S(1)}) custom-call(bf16[2560,768]{1,0:T(8,128)(2,1)S(1)} %get-tuple-element.24.refs_0_, bf16[2560,768]{1,0:T(8,128)(2,1)S(1)} %get-tuple-element.25.refs_1_, bf16[768,2560]{1,0:T(8,128)(2,1)S(1)} %get-tuple-element.26.refs_2_, bf16[2592,128]{1,0:T(8,128)(2,1)S(1)} %collective-permute-done.7.refs_3_, ...), custom_call_target="tpu_custom_call" | custom-call | flops 1509949440 | bytes 1310720 | tf_op jit(solution)/shard_map/expert/pallas_call | solution.py:241
  28.2 1.8 %expert.11 = (bf16[64,2560]{1,0:T(8,128)(2,1)S(1)}, bf16[64,2560]{1,0:T(8,128)(2,1)S(1)}) custom-call(bf16[2560,768]{1,0:T(8,128)(2,1)S(1)} %collective-permute-done.refs_1_.refs_0_, bf16[2560,768]{1,0:T(8,128)(2,1)S(1)} %collective-permute-done.1.refs_1_, bf16[768,2560]{1,0:T(8,128)(2,1)S(1)} %collective-permute-done.2.refs_2_, ...), custom_call_target="tpu_custom_call" | custom-call | flops 1509949440 | bytes 1310720 | tf_op jit(solution)/shard_map/expert/pallas_call | solution.py:241
  29.9 1.8 %collective-permute-start.10 = (bf16[64,2560]{1,0:T(8,128)(2,1)S(1)}, bf16[64,2560]{1,0:T(8,128)(2,1)S(1)}, u32[]{:S(2)}, u32[]{:S(2)}) collective-permute-start(bf16[64,2560]{1,0:T(8,128)(2,1)S(1)} %get-tuple-element.32.refs_7_), channel_id=1, source_target_pairs={{0,4},{1,3},{2,6},{3,1},{4,0},{5,7},{6,2},{7,5},{8,12},{9,11},{10,... | collective-permute-start | bytes 983048 | tf_op jit(solution)/shard_map/ppermute | solution.py:35
  31.7 0.3 collective-permute-start.8
  32.0 2.0 %expert.12 = (f32[64,2560]{1,0:T(8,128)S(1)}, f32[64,2560]{1,0:T(8,128)S(1)}) custom-call(bf16[2560,768]{1,0:T(8,128)(2,1)S(1)} %collective-permute-done.refs_1_.refs_0_, bf16[2560,768]{1,0:T(8,128)(2,1)S(1)} %collective-permute-done.1.refs_1_, bf16[768,2560]{1,0:T(8,128)(2,1)S(1)} %collective-permute-done.2.refs_2_, bf16[2592,128]{1,0:T(8,128)(2,1)S(1)} %append.1.refs_3_, ...), custom_call_target="tpu_custom_call" | custom-call | flops 1509949440 | bytes 1310720 | tf_op jit(solution)/shard_map/expert/pallas_call | solution.py:241
  34.1 1.9 %expert.13.refs_0_.whole_ref = f32[128,2560]{1,0:T(8,128)S(1)} custom-call(bf16[2560,768]{1,0:T(8,128)(2,1)S(1)} %collective-permute-done.refs_1_.refs_0_, bf16[2560,768]{1,0:T(8,128)(2,1)S(1)} %collective-permute-done.1.refs_1_, bf16[768,2560]{1,0:T(8,128)(2,1)S(1)} %collective-permute-done.2.refs_2_, bf16[2592,128]{1,0:T(8,128)(2,1)S(1)} %held.1.refs_3_, ...), custom_call_target="tpu_custom_call" | custom-call | flops 1509949440 | bytes 1310720 | tf_op jit(solution)/shard_map/expert/pallas_call | solution.py:241
  36.0 1.1 %collective-permute-done.10.second_ref = bf16[64,2560]{1,0:T(8,128)(2,1)S(1)} collective-permute-done((bf16[64,2560]{1,0:T(8,128)(2,1)S(1)}, bf16[64,2560]{1,0:T(8,128)(2,1)S(1)}, u32[]{:S(2)}, u32[]{:S(2)}) %collective-permute-start.10) | collective-permute-done | bytes 327712 | tf_op jit(solution)/shard_map/ppermute | solution.py:35
  37.1 0.1 sums.3
  37.1 1.8 %collective-permute-start.11 = (bf16[64,2560]{1,0:T(8,128)(2,1)S(1)}, bf16[64,2560]{1,0:T(8,128)(2,1)S(1)}, u32[]{:S(2)}, u32[]{:S(2)}) collective-permute-start(bf16[64,2560]{1,0:T(8,128)(2,1)S(1)} %sums.3), channel_id=1, source_target_pairs={{0,2},{1,5},{2,0},{3,7},{4,6},{5,1},{6,4},{7,3},{8,10},{9,13},{10,... | collective-permute-start | bytes 983048 | tf_op jit(solution)/shard_map/ppermute | solution.py:35
  38.9 2.0 %collective-permute-done.8.second_ref = bf16[64,2560]{1,0:T(8,128)(2,1)S(1)} collective-permute-done((bf16[64,2560]{1,0:T(8,128)(2,1)S(1)}, bf16[64,2560]{1,0:T(8,128)(2,1)S(1)}, u32[]{:S(2)}, u32[]{:S(2)}) %collective-permute-start.8) | collective-permute-done | bytes 327712 | tf_op jit(solution)/shard_map/ppermute | solution.py:35
  40.9 0.1 sums.2
  41.0 1.8 %collective-permute-start.9 = (bf16[64,2560]{1,0:T(8,128)(2,1)S(1)}, bf16[64,2560]{1,0:T(8,128)(2,1)S(1)}, u32[]{:S(2)}, u32[]{:S(2)}) collective-permute-start(bf16[64,2560]{1,0:T(8,128)(2,1)S(1)} %sums.2), channel_id=1, source_target_pairs={{0,2},{1,5},{2,0},{3,7},{4,6},{5,1},{6,4},{7,3},{8,10},{9,13},{10,... | collective-permute-start | bytes 983048 | tf_op jit(solution)/shard_map/ppermute | solution.py:35
  42.7 1.6 %collective-permute-done.11.lower_ref = bf16[64,2560]{1,0:T(8,128)(2,1)S(1)} collective-permute-done((bf16[64,2560]{1,0:T(8,128)(2,1)S(1)}, bf16[64,2560]{1,0:T(8,128)(2,1)S(1)}, u32[]{:S(2)}, u32[]{:S(2)}) %collective-permute-start.11) | collective-permute-done | bytes 327712 | tf_op jit(solution)/shard_map/ppermute | solution.py:35
  44.3 3.8 %collective-permute-done.9.upper_ref = bf16[64,2560]{1,0:T(8,128)(2,1)S(1)} collective-permute-done((bf16[64,2560]{1,0:T(8,128)(2,1)S(1)}, bf16[64,2560]{1,0:T(8,128)(2,1)S(1)}, u32[]{:S(2)}, u32[]{:S(2)}) %collective-permute-start.9) | collective-permute-done | bytes 327712 | tf_op jit(solution)/shard_map/ppermute | solution.py:35
  48.1 1.0 %finish.1 = bf16[128,2560]{1,0:T(8,128)(2,1)} custom-call(f32[128,2560]{1,0:T(8,128)S(1)} %expert.13.refs_0_.whole_ref, bf16[64,2560]{1,0:T(8,128)(2,1)S(1)} %collective-permute-done.9.upper_ref, bf16[64,2560]{1,0:T(8,128)(2,1)S(1)} %collective-permute-done.11.lower_ref), custom_call_target="tpu_custom_call" | custom-call | tf_op jit(solution)/shard_map/finish/pallas_call | solution.py:275
  (6 shorter events, 0.0 us)
Async XLA Ops:
  0.0 7.7 %collective-permute-start = (bf16[2560,768]{1,0:T(8,128)(2,1)}, bf16[2560,768]{1,0:T(8,128)(2,1)S(1)}, u32[]{:S(2)}, u32[]{:S(2)}) collective-permute-start(bf16[2560,768]{1,0:T(8,128)(2,1)} %bitcast.5), channel_id=1, source_target_pairs={{0,1},{1,0},{2,3},{3,2},{4,5},{5,4},{6,7},{7,6},{8,9},{9,8},{10,11... | collective-permute-start | bytes 11796488 | tf_op jit(solution)/shard_map/ppermute | solution.py:35
  0.5 20.6 %collective-permute-start.1 = (bf16[2560,768]{1,0:T(8,128)(2,1)}, bf16[2560,768]{1,0:T(8,128)(2,1)S(1)}, u32[]{:S(2)}, u32[]{:S(2)}) collective-permute-start(bf16[2560,768]{1,0:T(8,128)(2,1)} %bitcast.7), channel_id=1, source_target_pairs={{0,1},{1,0},{2,3},{3,2},{4,5},{5,4},{6,7},{7,6},{8,9},{9,8},{10,11... | collective-permute-start | bytes 11796488 | tf_op jit(solution)/shard_map/ppermute | solution.py:35
  0.5 20.5 %collective-permute-start.2 = (bf16[768,2560]{1,0:T(8,128)(2,1)}, bf16[768,2560]{1,0:T(8,128)(2,1)S(1)}, u32[]{:S(2)}, u32[]{:S(2)}) collective-permute-start(bf16[768,2560]{1,0:T(8,128)(2,1)} %bitcast.9), channel_id=1, source_target_pairs={{0,1},{1,0},{2,3},{3,2},{4,5},{5,4},{6,7},{7,6},{8,9},{9,8},{10,11... | collective-permute-start | bytes 11796488 | tf_op jit(solution)/shard_map/ppermute | solution.py:35
  1.0 13.1 %collective-permute-start.4 = (bf16[128,2560]{1,0:T(8,128)(2,1)}, bf16[128,2560]{1,0:T(8,128)(2,1)S(1)}, u32[]{:S(2)}, u32[]{:S(2)}) collective-permute-start(bf16[128,2560]{1,0:T(8,128)(2,1)} %tokens_hbm.1), channel_id=1, source_target_pairs={{0,2},{1,5},{2,0},{3,7},{4,6},{5,1},{6,4},{7,3},{8,10},{9,13},{10,... | collective-permute-start | bytes 1966088 | tf_op jit(solution)/shard_map/ppermute | solution.py:35
  7.7 11.6 %collective-permute-start.3 = (bf16[2592,128]{1,0:T(8,128)(2,1)S(1)}, bf16[2592,128]{1,0:T(8,128)(2,1)S(1)}, u32[]{:S(2)}, u32[]{:S(2)}) collective-permute-start(bf16[2592,128]{1,0:T(8,128)(2,1)S(1)} %held.1.refs_3_), channel_id=1, source_target_pairs={{0,4},{1,3},{2,6},{3,1},{4,0},{5,7},{6,2},{7,5},{8,12},{9,11},{10,... | collective-permute-start | bytes 1990664 | tf_op jit(solution)/shard_map/ppermute | solution.py:35
  10.0 4.1 %collective-permute-start.5 = (bf16[32,128]{1,0:T(8,128)(2,1)S(1)}, bf16[32,128]{1,0:T(8,128)(2,1)S(1)}, u32[]{:S(2)}, u32[]{:S(2)}) collective-permute-start(bf16[32,128]{1,0:T(8,128)(2,1)S(1)} %get-tuple-element.22.terms_ref), channel_id=1, source_target_pairs={{0,2},{1,5},{2,0},{3,7},{4,6},{5,1},{6,4},{7,3},{8,10},{9,13},{10,... | collective-permute-start | bytes 24584 | tf_op jit(solution)/shard_map/ppermute | solution.py:35
  14.2 12.2 %collective-permute-start.7 = (bf16[2592,128]{1,0:T(8,128)(2,1)S(1)}, bf16[2592,128]{1,0:T(8,128)(2,1)S(1)}, u32[]{:S(2)}, u32[]{:S(2)}) collective-permute-start(bf16[2592,128]{1,0:T(8,128)(2,1)S(1)} %append.1.refs_3_), channel_id=1, source_target_pairs={{0,4},{1,3},{2,6},{3,1},{4,0},{5,7},{6,2},{7,5},{8,12},{9,11},{10,... | collective-permute-start | bytes 1990664 | tf_op jit(solution)/shard_map/ppermute | solution.py:35
  22.8 11.2 %collective-permute-start.6 = (bf16[128,2560]{1,0:T(8,128)(2,1)S(1)}, bf16[128,2560]{1,0:T(8,128)(2,1)S(1)}, u32[]{:S(2)}, u32[]{:S(2)}) collective-permute-start(bf16[128,2560]{1,0:T(8,128)(2,1)S(1)} %expert.9.refs_4_), channel_id=1, source_target_pairs={{0,4},{1,3},{2,6},{3,1},{4,0},{5,7},{6,2},{7,5},{8,12},{9,11},{10,... | collective-permute-start | bytes 1966088 | tf_op jit(solution)/shard_map/ppermute | solution.py:35
  29.9 7.1 %collective-permute-start.10 = (bf16[64,2560]{1,0:T(8,128)(2,1)S(1)}, bf16[64,2560]{1,0:T(8,128)(2,1)S(1)}, u32[]{:S(2)}, u32[]{:S(2)}) collective-permute-start(bf16[64,2560]{1,0:T(8,128)(2,1)S(1)} %get-tuple-element.32.refs_7_), channel_id=1, source_target_pairs={{0,4},{1,3},{2,6},{3,1},{4,0},{5,7},{6,2},{7,5},{8,12},{9,11},{10,... | collective-permute-start | bytes 983048 | tf_op jit(solution)/shard_map/ppermute | solution.py:35
  31.7 9.2 %collective-permute-start.8 = (bf16[64,2560]{1,0:T(8,128)(2,1)S(1)}, bf16[64,2560]{1,0:T(8,128)(2,1)S(1)}, u32[]{:S(2)}, u32[]{:S(2)}) collective-permute-start(bf16[64,2560]{1,0:T(8,128)(2,1)S(1)} %get-tuple-element.31.refs_6_), channel_id=1, source_target_pairs={{0,4},{1,3},{2,6},{3,1},{4,0},{5,7},{6,2},{7,5},{8,12},{9,11},{10,... | collective-permute-start | bytes 983048 | tf_op jit(solution)/shard_map/ppermute | solution.py:35
  37.1 7.1 %collective-permute-start.11 = (bf16[64,2560]{1,0:T(8,128)(2,1)S(1)}, bf16[64,2560]{1,0:T(8,128)(2,1)S(1)}, u32[]{:S(2)}, u32[]{:S(2)}) collective-permute-start(bf16[64,2560]{1,0:T(8,128)(2,1)S(1)} %sums.3), channel_id=1, source_target_pairs={{0,2},{1,5},{2,0},{3,7},{4,6},{5,1},{6,4},{7,3},{8,10},{9,13},{10,... | collective-permute-start | bytes 983048 | tf_op jit(solution)/shard_map/ppermute | solution.py:35
  41.0 7.1 %collective-permute-start.9 = (bf16[64,2560]{1,0:T(8,128)(2,1)S(1)}, bf16[64,2560]{1,0:T(8,128)(2,1)S(1)}, u32[]{:S(2)}, u32[]{:S(2)}) collective-permute-start(bf16[64,2560]{1,0:T(8,128)(2,1)S(1)} %sums.2), channel_id=1, source_target_pairs={{0,2},{1,5},{2,0},{3,7},{4,6},{5,1},{6,4},{7,3},{8,10},{9,13},{10,... | collective-permute-start | bytes 983048 | tf_op jit(solution)/shard_map/ppermute | solution.py:35

commit v6 on v5

--- a/solution.py
+++ b/solution.py
@@ -134,7 +134,7 @@
             pltpu.SemaphoreType.DMA((3 + 2 * (width // STEP),)),
         ],
         compiler_params=pltpu.CompilerParams(vmem_limit_bytes=16 * MIB),
-        cost_estimate=expert_cost(count, features, width),
+        cost_estimate=expert_cost(36 * count, features, width),
         name="own_hidden",
     )(*[in_hbm(v) for v in (tokens, ids, gates, gate, up)])
 
@@ -289,8 +289,8 @@
     far = tuple(swap(w, (CORE, CORE)) for w in weights)
     first = swap(tokens, FIRST)
     own, terms, hidden, near_gate, near_up = own_hidden(tokens, expert_ids, gate_values, *weights[:2], experts)
-    own, = held(own, after=far[:1])
     second = swap(own, SECOND)
+    terms, = held(terms, after=far[:1])
     near_own, near_down = own_answer(hidden, terms, weights[2], experts)
     first = append(first, swap(terms, FIRST), near_own)
     third = swap(first, SECOND)

time: 49.3 us -> 48.7 us (0.988)
  starting transfers between devices: 16.6 us -> 16 us
    ppermute x12, starting transfers between devices: 16.6 us -> 16 us  [swap(): lax.ppermute(value, 'expert', [(i, i ^ offsets[i % 2]) for i in range(siz...]
  transfers between devices with their start and end apart: 12 -> 12, of which waited for: 6 -> 8; matrix products, arithmetic and copies ran while one was open for 0% -> 0% of each run, Pallas kernels for 40% -> 41%
where the time goes in v6:
time: 48.7 us; the launch traced here: 48.6 us
  Pallas kernels  20.8 us (43%)
  starting transfers between devices  16 us (33%)
  waiting for transfers between devices  11.7 us (24%)
    ppermute x12, starting transfers between devices, swap(): lax.ppermute(value, 'expert', [(i, i ^ offsets[i % 2]) for i in range(siz...  16 us
    pallas_call x7, Pallas kernels, run_expert(): pl.pallas_call(functools.partial(expert_kernel, experts, other, len(added...  12.8 us
    ppermute x12, waiting for transfers between devices, swap(): lax.ppermute(value, 'expert', [(i, i ^ offsets[i % 2]) for i in range(siz...  11.7 us
    pallas_call x1, Pallas kernels, own_hidden(): pl.pallas_call(functools.partial(own_hidden_kernel, experts), out_shape=[...  4.2 us
    pallas_call x1, Pallas kernels, own_answer(): pl.pallas_call(functools.partial(own_answer_kernel, experts), out_shape=[...  2.55 us
    pallas_call x1, Pallas kernels, finish(): pl.pallas_call(finish_kernel, out_shape=jax.ShapeDtypeStruct(whole_part.s...  0.98 us
  transfers between devices with their start and end apart: 12, of which 8 were waited for; matrix products, arithmetic and copies ran while one was open for 0% of the time, Pallas kernels for 41%

profile of v6, /device:TPU:0, one launch (start us, length us, event | category | flops | bytes accessed | tf_op | source)
XLA Modules:
  0.0 48.6 jit_solution(7395182756132804991)
XLA Ops:
  0.0 0.5 collective-permute-start
  0.5 2.5 %collective-permute-start.4 = (bf16[128,2560]{1,0:T(8,128)(2,1)}, bf16[128,2560]{1,0:T(8,128)(2,1)S(1)}, u32[]{:S(2)}, u32[]{:S(2)}) collective-permute-start(bf16[128,2560]{1,0:T(8,128)(2,1)} %tokens_hbm.1), channel_id=1, source_target_pairs={{0,2},{1,5},{2,0},{3,7},{4,6},{5,1},{6,4},{7,3},{8,10},{9,13},{10,... | collective-permute-start | bytes 1966088 | tf_op jit(solution)/shard_map/ppermute | solution.py:35
  2.9 0.3 collective-permute-start.1
  3.2 0.3 collective-permute-start.2
  3.5 4.2 %own_hidden.1 = (bf16[2592,128]{1,0:T(8,128)(2,1)S(1)}, bf16[32,128]{1,0:T(8,128)(2,1)S(1)}, bf16[128,768]{1,0:T(8,128)(2,1)S(1)}, bf16[2560,768]{1,0:T(8,128)(2,1)S(1)}, bf16[2560,768]{1,0:T(8,128)(2,1)S(1)}) custom-call(bf16[128,2560]{1,0:T(8,128)(2,1)} %tokens_hbm.1, s32[6,128]{1,0:T(8,128)} %bitcast.11, f32[6,128]{1,0:T(8,128)} %bitcast.12, ...), custom_call_target="tpu_custom_call" | custom-call | flops 54358179840 | bytes 47185920 | tf_op jit(solution)/shard_map/own_hidden/pallas_call | solution.py:119
  7.7 1.6 %collective-permute-start.3 = (bf16[2592,128]{1,0:T(8,128)(2,1)S(1)}, bf16[2592,128]{1,0:T(8,128)(2,1)S(1)}, u32[]{:S(2)}, u32[]{:S(2)}) collective-permute-start(bf16[2592,128]{1,0:T(8,128)(2,1)S(1)} %get-tuple-element.20.refs_3_), channel_id=1, source_target_pairs={{0,4},{1,3},{2,6},{3,1},{4,0},{5,7},{6,2},{7,5},{8,12},{9,11},{10,... | collective-permute-start | bytes 1990664 | tf_op jit(solution)/shard_map/ppermute | solution.py:35
  9.3 0.7 %collective-permute-start.5 = (bf16[32,128]{1,0:T(8,128)(2,1)S(1)}, bf16[32,128]{1,0:T(8,128)(2,1)S(1)}, u32[]{:S(2)}, u32[]{:S(2)}) collective-permute-start(bf16[32,128]{1,0:T(8,128)(2,1)S(1)} %held.1.terms_ref), channel_id=1, source_target_pairs={{0,2},{1,5},{2,0},{3,7},{4,6},{5,1},{6,4},{7,3},{8,10},{9,13},{10,... | collective-permute-start | bytes 24584 | tf_op jit(solution)/shard_map/ppermute | solution.py:35
  9.9 2.6 %own_answer.1 = (f32[128,2560]{1,0:T(8,128)S(1)}, bf16[768,2560]{1,0:T(8,128)(2,1)S(1)}) custom-call(bf16[128,768]{1,0:T(8,128)(2,1)S(1)} %get-tuple-element.21.hidden_ref, bf16[32,128]{1,0:T(8,128)(2,1)S(1)} %held.1.terms_ref, bf16[768,2560]{1,0:T(8,128)(2,1)} %bitcast.6), custom_call_target="tpu_custom_call" | custom-call | flops 503316480 | bytes 1310720 | tf_op jit(solution)/shard_map/own_answer/pallas_call | solution.py:161
  12.5 0.5 collective-permute-done.4.rows_ref
  13.0 0.1 collective-permute-done.5.terms_ref
  13.1 0.1 append.1.refs_3_
  13.2 2.8 %collective-permute-start.7 = (bf16[2592,128]{1,0:T(8,128)(2,1)S(1)}, bf16[2592,128]{1,0:T(8,128)(2,1)S(1)}, u32[]{:S(2)}, u32[]{:S(2)}) collective-permute-start(bf16[2592,128]{1,0:T(8,128)(2,1)S(1)} %append.1.refs_3_), channel_id=1, source_target_pairs={{0,4},{1,3},{2,6},{3,1},{4,0},{5,7},{6,2},{7,5},{8,12},{9,11},{10,... | collective-permute-start | bytes 1990664 | tf_op jit(solution)/shard_map/ppermute | solution.py:35
  15.9 1.8 %expert.7 = (f32[64,2560]{1,0:T(8,128)S(1)}, f32[64,2560]{1,0:T(8,128)S(1)}) custom-call(bf16[2560,768]{1,0:T(8,128)(2,1)S(1)} %get-tuple-element.24.refs_0_, bf16[2560,768]{1,0:T(8,128)(2,1)S(1)} %get-tuple-element.25.refs_1_, bf16[768,2560]{1,0:T(8,128)(2,1)S(1)} %get-tuple-element.26.refs_2_, bf16[2592,128]{1,0:T(8,128)(2,1)S(1)} %append.1.refs_3_, ...), custom_call_target="tpu_custom_call" | custom-call | flops 1509949440 | bytes 1310720 | tf_op jit(solution)/shard_map/expert/pallas_call | solution.py:241
  17.8 1.0 %collective-permute-done.3.refs_3_ = bf16[2592,128]{1,0:T(8,128)(2,1)S(1)} collective-permute-done((bf16[2592,128]{1,0:T(8,128)(2,1)S(1)}, bf16[2592,128]{1,0:T(8,128)(2,1)S(1)}, u32[]{:S(2)}, u32[]{:S(2)}) %collective-permute-start.3) | collective-permute-done | bytes 663584 | tf_op jit(solution)/shard_map/ppermute | solution.py:35
  18.8 1.8 %expert.8.refs_4_ = f32[128,2560]{1,0:T(8,128)S(1)} custom-call(bf16[2560,768]{1,0:T(8,128)(2,1)S(1)} %get-tuple-element.24.refs_0_, bf16[2560,768]{1,0:T(8,128)(2,1)S(1)} %get-tuple-element.25.refs_1_, bf16[768,2560]{1,0:T(8,128)(2,1)S(1)} %get-tuple-element.26.refs_2_, bf16[2592,128]{1,0:T(8,128)(2,1)S(1)} %collective-permute-done.3.refs_3_, ...), custom_call_target="tpu_custom_call" | custom-call | flops 1509949440 | bytes 1310720 | tf_op jit(solution)/shard_map/expert/pallas_call | solution.py:241
  20.6 1.8 %expert.9.refs_4_ = bf16[128,2560]{1,0:T(8,128)(2,1)S(1)} custom-call(bf16[2560,768]{1,0:T(8,128)(2,1)S(1)} %collective-permute-done.refs_1_.refs_0_, bf16[2560,768]{1,0:T(8,128)(2,1)S(1)} %collective-permute-done.1.refs_1_, bf16[768,2560]{1,0:T(8,128)(2,1)S(1)} %collective-permute-done.2.refs_2_, bf16[2592,128]{1,0:T(8,128)(2,1)S(1)} %collective-permute-done.3.refs_3_, ...), custom_call_target="tpu_custom_call" | custom-call | flops 1509949440 | bytes 1310720 | tf_op jit(solution)/shard_map/expert/pallas_call | solution.py:241
  22.3 1.8 %collective-permute-start.6 = (bf16[128,2560]{1,0:T(8,128)(2,1)S(1)}, bf16[128,2560]{1,0:T(8,128)(2,1)S(1)}, u32[]{:S(2)}, u32[]{:S(2)}) collective-permute-start(bf16[128,2560]{1,0:T(8,128)(2,1)S(1)} %expert.9.refs_4_), channel_id=1, source_target_pairs={{0,4},{1,3},{2,6},{3,1},{4,0},{5,7},{6,2},{7,5},{8,12},{9,11},{10,... | collective-permute-start | bytes 1966088 | tf_op jit(solution)/shard_map/ppermute | solution.py:35
  24.1 1.7 %collective-permute-done.7.refs_3_ = bf16[2592,128]{1,0:T(8,128)(2,1)S(1)} collective-permute-done((bf16[2592,128]{1,0:T(8,128)(2,1)S(1)}, bf16[2592,128]{1,0:T(8,128)(2,1)S(1)}, u32[]{:S(2)}, u32[]{:S(2)}) %collective-permute-start.7) | collective-permute-done | bytes 663584 | tf_op jit(solution)/shard_map/ppermute | solution.py:35
  25.9 1.8 %expert.10 = (f32[64,2560]{1,0:T(8,128)S(1)}, f32[64,2560]{1,0:T(8,128)S(1)}) custom-call(bf16[2560,768]{1,0:T(8,128)(2,1)S(1)} %get-tuple-element.24.refs_0_, bf16[2560,768]{1,0:T(8,128)(2,1)S(1)} %get-tuple-element.25.refs_1_, bf16[768,2560]{1,0:T(8,128)(2,1)S(1)} %get-tuple-element.26.refs_2_, bf16[2592,128]{1,0:T(8,128)(2,1)S(1)} %collective-permute-done.7.refs_3_, ...), custom_call_target="tpu_custom_call" | custom-call | flops 1509949440 | bytes 1310720 | tf_op jit(solution)/shard_map/expert/pallas_call | solution.py:241
  27.6 1.8 %expert.11 = (bf16[64,2560]{1,0:T(8,128)(2,1)S(1)}, bf16[64,2560]{1,0:T(8,128)(2,1)S(1)}) custom-call(bf16[2560,768]{1,0:T(8,128)(2,1)S(1)} %collective-permute-done.refs_1_.refs_0_, bf16[2560,768]{1,0:T(8,128)(2,1)S(1)} %collective-permute-done.1.refs_1_, bf16[768,2560]{1,0:T(8,128)(2,1)S(1)} %collective-permute-done.2.refs_2_, ...), custom_call_target="tpu_custom_call" | custom-call | flops 1509949440 | bytes 1310720 | tf_op jit(solution)/shard_map/expert/pallas_call | solution.py:241
  29.4 1.8 %collective-permute-start.10 = (bf16[64,2560]{1,0:T(8,128)(2,1)S(1)}, bf16[64,2560]{1,0:T(8,128)(2,1)S(1)}, u32[]{:S(2)}, u32[]{:S(2)}) collective-permute-start(bf16[64,2560]{1,0:T(8,128)(2,1)S(1)} %get-tuple-element.32.refs_7_), channel_id=1, source_target_pairs={{0,4},{1,3},{2,6},{3,1},{4,0},{5,7},{6,2},{7,5},{8,12},{9,11},{10,... | collective-permute-start | bytes 983048 | tf_op jit(solution)/shard_map/ppermute | solution.py:35
  31.2 0.3 collective-permute-start.8
  31.5 2.0 %expert.12 = (f32[64,2560]{1,0:T(8,128)S(1)}, f32[64,2560]{1,0:T(8,128)S(1)}) custom-call(bf16[2560,768]{1,0:T(8,128)(2,1)S(1)} %collective-permute-done.refs_1_.refs_0_, bf16[2560,768]{1,0:T(8,128)(2,1)S(1)} %collective-permute-done.1.refs_1_, bf16[768,2560]{1,0:T(8,128)(2,1)S(1)} %collective-permute-done.2.refs_2_, bf16[2592,128]{1,0:T(8,128)(2,1)S(1)} %append.1.refs_3_, ...), custom_call_target="tpu_custom_call" | custom-call | flops 1509949440 | bytes 1310720 | tf_op jit(solution)/shard_map/expert/pallas_call | solution.py:241
  33.6 1.9 %expert.13.refs_0_.whole_ref = f32[128,2560]{1,0:T(8,128)S(1)} custom-call(bf16[2560,768]{1,0:T(8,128)(2,1)S(1)} %collective-permute-done.refs_1_.refs_0_, bf16[2560,768]{1,0:T(8,128)(2,1)S(1)} %collective-permute-done.1.refs_1_, bf16[768,2560]{1,0:T(8,128)(2,1)S(1)} %collective-permute-done.2.refs_2_, bf16[2592,128]{1,0:T(8,128)(2,1)S(1)} %get-tuple-element.20.refs_3_, ...), custom_call_target="tpu_custom_call" | custom-call | flops 1509949440 | bytes 1310720 | tf_op jit(solution)/shard_map/expert/pallas_call | solution.py:241
  35.4 1.1 %collective-permute-done.10.second_ref = bf16[64,2560]{1,0:T(8,128)(2,1)S(1)} collective-permute-done((bf16[64,2560]{1,0:T(8,128)(2,1)S(1)}, bf16[64,2560]{1,0:T(8,128)(2,1)S(1)}, u32[]{:S(2)}, u32[]{:S(2)}) %collective-permute-start.10) | collective-permute-done | bytes 327712 | tf_op jit(solution)/shard_map/ppermute | solution.py:35
  36.6 0.1 sums.3
  36.6 1.8 %collective-permute-start.11 = (bf16[64,2560]{1,0:T(8,128)(2,1)S(1)}, bf16[64,2560]{1,0:T(8,128)(2,1)S(1)}, u32[]{:S(2)}, u32[]{:S(2)}) collective-permute-start(bf16[64,2560]{1,0:T(8,128)(2,1)S(1)} %sums.3), channel_id=1, source_target_pairs={{0,2},{1,5},{2,0},{3,7},{4,6},{5,1},{6,4},{7,3},{8,10},{9,13},{10,... | collective-permute-start | bytes 983048 | tf_op jit(solution)/shard_map/ppermute | solution.py:35
  38.4 2.0 %collective-permute-done.8.second_ref = bf16[64,2560]{1,0:T(8,128)(2,1)S(1)} collective-permute-done((bf16[64,2560]{1,0:T(8,128)(2,1)S(1)}, bf16[64,2560]{1,0:T(8,128)(2,1)S(1)}, u32[]{:S(2)}, u32[]{:S(2)}) %collective-permute-start.8) | collective-permute-done | bytes 327712 | tf_op jit(solution)/shard_map/ppermute | solution.py:35
  40.4 1.8 %collective-permute-start.9 = (bf16[64,2560]{1,0:T(8,128)(2,1)S(1)}, bf16[64,2560]{1,0:T(8,128)(2,1)S(1)}, u32[]{:S(2)}, u32[]{:S(2)}) collective-permute-start(bf16[64,2560]{1,0:T(8,128)(2,1)S(1)} %sums.2), channel_id=1, source_target_pairs={{0,2},{1,5},{2,0},{3,7},{4,6},{5,1},{6,4},{7,3},{8,10},{9,13},{10,... | collective-permute-start | bytes 983048 | tf_op jit(solution)/shard_map/ppermute | solution.py:35
  42.2 1.5 %collective-permute-done.11.lower_ref = bf16[64,2560]{1,0:T(8,128)(2,1)S(1)} collective-permute-done((bf16[64,2560]{1,0:T(8,128)(2,1)S(1)}, bf16[64,2560]{1,0:T(8,128)(2,1)S(1)}, u32[]{:S(2)}, u32[]{:S(2)}) %collective-permute-start.11) | collective-permute-done | bytes 327712 | tf_op jit(solution)/shard_map/ppermute | solution.py:35
  43.8 3.8 %collective-permute-done.9.upper_ref = bf16[64,2560]{1,0:T(8,128)(2,1)S(1)} collective-permute-done((bf16[64,2560]{1,0:T(8,128)(2,1)S(1)}, bf16[64,2560]{1,0:T(8,128)(2,1)S(1)}, u32[]{:S(2)}, u32[]{:S(2)}) %collective-permute-start.9) | collective-permute-done | bytes 327712 | tf_op jit(solution)/shard_map/ppermute | solution.py:35
  47.6 1.0 %finish.1 = bf16[128,2560]{1,0:T(8,128)(2,1)} custom-call(f32[128,2560]{1,0:T(8,128)S(1)} %expert.13.refs_0_.whole_ref, bf16[64,2560]{1,0:T(8,128)(2,1)S(1)} %collective-permute-done.9.upper_ref, bf16[64,2560]{1,0:T(8,128)(2,1)S(1)} %collective-permute-done.11.lower_ref), custom_call_target="tpu_custom_call" | custom-call | tf_op jit(solution)/shard_map/finish/pallas_call | solution.py:275
  (6 shorter events, 0.1 us)
Async XLA Ops:
  0.0 9.3 %collective-permute-start = (bf16[2560,768]{1,0:T(8,128)(2,1)}, bf16[2560,768]{1,0:T(8,128)(2,1)S(1)}, u32[]{:S(2)}, u32[]{:S(2)}) collective-permute-start(bf16[2560,768]{1,0:T(8,128)(2,1)} %bitcast.7), channel_id=1, source_target_pairs={{0,1},{1,0},{2,3},{3,2},{4,5},{5,4},{6,7},{7,6},{8,9},{9,8},{10,11... | collective-permute-start | bytes 11796488 | tf_op jit(solution)/shard_map/ppermute | solution.py:35
  0.5 12.5 %collective-permute-start.4 = (bf16[128,2560]{1,0:T(8,128)(2,1)}, bf16[128,2560]{1,0:T(8,128)(2,1)S(1)}, u32[]{:S(2)}, u32[]{:S(2)}) collective-permute-start(bf16[128,2560]{1,0:T(8,128)(2,1)} %tokens_hbm.1), channel_id=1, source_target_pairs={{0,2},{1,5},{2,0},{3,7},{4,6},{5,1},{6,4},{7,3},{8,10},{9,13},{10,... | collective-permute-start | bytes 1966088 | tf_op jit(solution)/shard_map/ppermute | solution.py:35
  2.9 17.6 %collective-permute-start.1 = (bf16[2560,768]{1,0:T(8,128)(2,1)}, bf16[2560,768]{1,0:T(8,128)(2,1)S(1)}, u32[]{:S(2)}, u32[]{:S(2)}) collective-permute-start(bf16[2560,768]{1,0:T(8,128)(2,1)} %bitcast.9), channel_id=1, source_target_pairs={{0,1},{1,0},{2,3},{3,2},{4,5},{5,4},{6,7},{7,6},{8,9},{9,8},{10,11... | collective-permute-start | bytes 11796488 | tf_op jit(solution)/shard_map/ppermute | solution.py:35
  3.2 17.3 %collective-permute-start.2 = (bf16[768,2560]{1,0:T(8,128)(2,1)}, bf16[768,2560]{1,0:T(8,128)(2,1)S(1)}, u32[]{:S(2)}, u32[]{:S(2)}) collective-permute-start(bf16[768,2560]{1,0:T(8,128)(2,1)} %bitcast.5), channel_id=1, source_target_pairs={{0,1},{1,0},{2,3},{3,2},{4,5},{5,4},{6,7},{7,6},{8,9},{9,8},{10,11... | collective-permute-start | bytes 11796488 | tf_op jit(solution)/shard_map/ppermute | solution.py:35
  7.7 11.1 %collective-permute-start.3 = (bf16[2592,128]{1,0:T(8,128)(2,1)S(1)}, bf16[2592,128]{1,0:T(8,128)(2,1)S(1)}, u32[]{:S(2)}, u32[]{:S(2)}) collective-permute-start(bf16[2592,128]{1,0:T(8,128)(2,1)S(1)} %get-tuple-element.20.refs_3_), channel_id=1, source_target_pairs={{0,4},{1,3},{2,6},{3,1},{4,0},{5,7},{6,2},{7,5},{8,12},{9,11},{10,... | collective-permute-start | bytes 1990664 | tf_op jit(solution)/shard_map/ppermute | solution.py:35
  9.3 3.8 %collective-permute-start.5 = (bf16[32,128]{1,0:T(8,128)(2,1)S(1)}, bf16[32,128]{1,0:T(8,128)(2,1)S(1)}, u32[]{:S(2)}, u32[]{:S(2)}) collective-permute-start(bf16[32,128]{1,0:T(8,128)(2,1)S(1)} %held.1.terms_ref), channel_id=1, source_target_pairs={{0,2},{1,5},{2,0},{3,7},{4,6},{5,1},{6,4},{7,3},{8,10},{9,13},{10,... | collective-permute-start | bytes 24584 | tf_op jit(solution)/shard_map/ppermute | solution.py:35
  13.2 12.7 %collective-permute-start.7 = (bf16[2592,128]{1,0:T(8,128)(2,1)S(1)}, bf16[2592,128]{1,0:T(8,128)(2,1)S(1)}, u32[]{:S(2)}, u32[]{:S(2)}) collective-permute-start(bf16[2592,128]{1,0:T(8,128)(2,1)S(1)} %append.1.refs_3_), channel_id=1, source_target_pairs={{0,4},{1,3},{2,6},{3,1},{4,0},{5,7},{6,2},{7,5},{8,12},{9,11},{10,... | collective-permute-start | bytes 1990664 | tf_op jit(solution)/shard_map/ppermute | solution.py:35
  22.3 11.2 %collective-permute-start.6 = (bf16[128,2560]{1,0:T(8,128)(2,1)S(1)}, bf16[128,2560]{1,0:T(8,128)(2,1)S(1)}, u32[]{:S(2)}, u32[]{:S(2)}) collective-permute-start(bf16[128,2560]{1,0:T(8,128)(2,1)S(1)} %expert.9.refs_4_), channel_id=1, source_target_pairs={{0,4},{1,3},{2,6},{3,1},{4,0},{5,7},{6,2},{7,5},{8,12},{9,11},{10,... | collective-permute-start | bytes 1966088 | tf_op jit(solution)/shard_map/ppermute | solution.py:35
  29.4 7.1 %collective-permute-start.10 = (bf16[64,2560]{1,0:T(8,128)(2,1)S(1)}, bf16[64,2560]{1,0:T(8,128)(2,1)S(1)}, u32[]{:S(2)}, u32[]{:S(2)}) collective-permute-start(bf16[64,2560]{1,0:T(8,128)(2,1)S(1)} %get-tuple-element.32.refs_7_), channel_id=1, source_target_pairs={{0,4},{1,3},{2,6},{3,1},{4,0},{5,7},{6,2},{7,5},{8,12},{9,11},{10,... | collective-permute-start | bytes 983048 | tf_op jit(solution)/shard_map/ppermute | solution.py:35
  31.2 9.1 %collective-permute-start.8 = (bf16[64,2560]{1,0:T(8,128)(2,1)S(1)}, bf16[64,2560]{1,0:T(8,128)(2,1)S(1)}, u32[]{:S(2)}, u32[]{:S(2)}) collective-permute-start(bf16[64,2560]{1,0:T(8,128)(2,1)S(1)} %get-tuple-element.31.refs_6_), channel_id=1, source_target_pairs={{0,4},{1,3},{2,6},{3,1},{4,0},{5,7},{6,2},{7,5},{8,12},{9,11},{10,... | collective-permute-start | bytes 983048 | tf_op jit(solution)/shard_map/ppermute | solution.py:35
  36.6 7.1 %collective-permute-start.11 = (bf16[64,2560]{1,0:T(8,128)(2,1)S(1)}, bf16[64,2560]{1,0:T(8,128)(2,1)S(1)}, u32[]{:S(2)}, u32[]{:S(2)}) collective-permute-start(bf16[64,2560]{1,0:T(8,128)(2,1)S(1)} %sums.3), channel_id=1, source_target_pairs={{0,2},{1,5},{2,0},{3,7},{4,6},{5,1},{6,4},{7,3},{8,10},{9,13},{10,... | collective-permute-start | bytes 983048 | tf_op jit(solution)/shard_map/ppermute | solution.py:35
  40.4 7.1 %collective-permute-start.9 = (bf16[64,2560]{1,0:T(8,128)(2,1)S(1)}, bf16[64,2560]{1,0:T(8,128)(2,1)S(1)}, u32[]{:S(2)}, u32[]{:S(2)}) collective-permute-start(bf16[64,2560]{1,0:T(8,128)(2,1)S(1)} %sums.2), channel_id=1, source_target_pairs={{0,2},{1,5},{2,0},{3,7},{4,6},{5,1},{6,4},{7,3},{8,10},{9,13},{10,... | collective-permute-start | bytes 983048 | tf_op jit(solution)/shard_map/ppermute | solution.py:35

commit v7 on v6

--- a/solution.py
+++ b/solution.py
@@ -265,21 +265,33 @@
     )(in_vmem(first), in_vmem(second), *after)
 
 
-def finish_kernel(whole_ref, upper_ref, lower_ref, out_ref):
+def finish_kernel(pieces, total_ref, upper_ref, lower_ref, out_hbm, out, done):
+    count = total_ref.shape[0] // pieces
     half = upper_ref.shape[0]
-    out_ref[:half] = (whole_ref[:half] + upper_ref[...].astype(jnp.float32)).astype(out_ref.dtype)
-    out_ref[half:] = (whole_ref[half:] + lower_ref[...].astype(jnp.float32)).astype(out_ref.dtype)
-
-
-def finish(whole_part, upper, lower):
-    return pl.pallas_call(
-        finish_kernel,
-        out_shape=jax.ShapeDtypeStruct(whole_part.shape, jnp.bfloat16),
+    copies = []
+    for i in range(pieces):
+        start = i * count
+        ref, at = (upper_ref, start) if start < half else (lower_ref, start - half)
+        part = total_ref[start : start + count] + ref[at : at + count].astype(jnp.float32)
+        out[start : start + count] = part.astype(out.dtype)
+        rows = pl.ds(start, count)
+        copies.append(pltpu.make_async_copy(out.at[rows], out_hbm.at[rows], done.at[i]))
+        copies[-1].start()
+    for copy in copies:
+        copy.wait()
+
+
+def finish(total, upper, lower, pieces=4):
+    return pl.pallas_call(
+        functools.partial(finish_kernel, pieces),
+        out_shape=jax.ShapeDtypeStruct(total.shape, upper.dtype),
         in_specs=[whole()] * 3,
-        out_specs=whole(),
-        compiler_params=pltpu.CompilerParams(vmem_limit_bytes=16 * MIB),
+        out_specs=anywhere(),
+        scratch_shapes=[pltpu.VMEM(total.shape, upper.dtype), pltpu.SemaphoreType.DMA((pieces,))],
+        compiler_params=pltpu.CompilerParams(vmem_limit_bytes=16 * MIB),
+        cost_estimate=pl.CostEstimate(flops=0, bytes_accessed=4 * total.size, transcendentals=0),
         name="finish",
-    )(in_vmem(whole_part), in_vmem(upper), in_vmem(lower))
+    )(in_vmem(total), in_vmem(upper), in_vmem(lower))
 
 
 def on_four_chips(tokens, expert_ids, gate_values, w_gate, w_up, w_down):

time: 48.7 us -> 48.8 us (level)
  no operation moved by 1% of the time
where the time goes in v7:
time: 48.8 us; the launch traced here: 48.7 us
  Pallas kernels  20.7 us (42%)
  starting transfers between devices  16 us (33%)
  waiting for transfers between devices  11.7 us (24%)
    ppermute x12, starting transfers between devices, swap(): lax.ppermute(value, 'expert', [(i, i ^ offsets[i % 2]) for i in range(siz...  16 us
    pallas_call x7, Pallas kernels, run_expert(): pl.pallas_call(functools.partial(expert_kernel, experts, other, len(added...  12.8 us
    ppermute x12, waiting for transfers between devices, swap(): lax.ppermute(value, 'expert', [(i, i ^ offsets[i % 2]) for i in range(siz...  11.7 us
    pallas_call x1, Pallas kernels, own_hidden(): pl.pallas_call(functools.partial(own_hidden_kernel, experts), out_shape=[...  4.2 us
    pallas_call x1, Pallas kernels, own_answer(): pl.pallas_call(functools.partial(own_answer_kernel, experts), out_shape=[...  2.55 us
  transfers between devices with their start and end apart: 12, of which 8 were waited for; matrix products, arithmetic and copies ran while one was open for 0% of the time, Pallas kernels for 41%

profile of v7, /device:TPU:0, one launch (start us, length us, event | category | flops | bytes accessed | tf_op | source)
XLA Modules:
  0.0 48.7 jit_solution(15126664979728741657)
XLA Ops:
  0.0 0.5 collective-permute-start
  0.5 2.5 %collective-permute-start.4 = (bf16[128,2560]{1,0:T(8,128)(2,1)}, bf16[128,2560]{1,0:T(8,128)(2,1)S(1)}, u32[]{:S(2)}, u32[]{:S(2)}) collective-permute-start(bf16[128,2560]{1,0:T(8,128)(2,1)} %tokens_hbm.1), channel_id=1, source_target_pairs={{0,2},{1,5},{2,0},{3,7},{4,6},{5,1},{6,4},{7,3},{8,10},{9,13},{10,... | collective-permute-start | bytes 1966088 | tf_op jit(solution)/shard_map/ppermute | solution.py:35
  2.9 0.3 collective-permute-start.1
  3.2 0.3 collective-permute-start.2
  3.5 4.2 %own_hidden.1 = (bf16[2592,128]{1,0:T(8,128)(2,1)S(1)}, bf16[32,128]{1,0:T(8,128)(2,1)S(1)}, bf16[128,768]{1,0:T(8,128)(2,1)S(1)}, bf16[2560,768]{1,0:T(8,128)(2,1)S(1)}, bf16[2560,768]{1,0:T(8,128)(2,1)S(1)}) custom-call(bf16[128,2560]{1,0:T(8,128)(2,1)} %tokens_hbm.1, s32[6,128]{1,0:T(8,128)} %bitcast.11, f32[6,128]{1,0:T(8,128)} %bitcast.12, ...), custom_call_target="tpu_custom_call" | custom-call | flops 54358179840 | bytes 47185920 | tf_op jit(solution)/shard_map/own_hidden/pallas_call | solution.py:119
  7.7 1.6 %collective-permute-start.3 = (bf16[2592,128]{1,0:T(8,128)(2,1)S(1)}, bf16[2592,128]{1,0:T(8,128)(2,1)S(1)}, u32[]{:S(2)}, u32[]{:S(2)}) collective-permute-start(bf16[2592,128]{1,0:T(8,128)(2,1)S(1)} %get-tuple-element.20.refs_3_), channel_id=1, source_target_pairs={{0,4},{1,3},{2,6},{3,1},{4,0},{5,7},{6,2},{7,5},{8,12},{9,11},{10,... | collective-permute-start | bytes 1990664 | tf_op jit(solution)/shard_map/ppermute | solution.py:35
  9.3 0.7 %collective-permute-start.5 = (bf16[32,128]{1,0:T(8,128)(2,1)S(1)}, bf16[32,128]{1,0:T(8,128)(2,1)S(1)}, u32[]{:S(2)}, u32[]{:S(2)}) collective-permute-start(bf16[32,128]{1,0:T(8,128)(2,1)S(1)} %held.1.terms_ref), channel_id=1, source_target_pairs={{0,2},{1,5},{2,0},{3,7},{4,6},{5,1},{6,4},{7,3},{8,10},{9,13},{10,... | collective-permute-start | bytes 24584 | tf_op jit(solution)/shard_map/ppermute | solution.py:35
  9.9 2.6 %own_answer.1 = (f32[128,2560]{1,0:T(8,128)S(1)}, bf16[768,2560]{1,0:T(8,128)(2,1)S(1)}) custom-call(bf16[128,768]{1,0:T(8,128)(2,1)S(1)} %get-tuple-element.21.hidden_ref, bf16[32,128]{1,0:T(8,128)(2,1)S(1)} %held.1.terms_ref, bf16[768,2560]{1,0:T(8,128)(2,1)} %bitcast.6), custom_call_target="tpu_custom_call" | custom-call | flops 503316480 | bytes 1310720 | tf_op jit(solution)/shard_map/own_answer/pallas_call | solution.py:161
  12.5 0.5 collective-permute-done.4.rows_ref
  13.0 0.1 collective-permute-done.5.terms_ref
  13.1 0.1 append.1.refs_3_
  13.2 2.8 %collective-permute-start.7 = (bf16[2592,128]{1,0:T(8,128)(2,1)S(1)}, bf16[2592,128]{1,0:T(8,128)(2,1)S(1)}, u32[]{:S(2)}, u32[]{:S(2)}) collective-permute-start(bf16[2592,128]{1,0:T(8,128)(2,1)S(1)} %append.1.refs_3_), channel_id=1, source_target_pairs={{0,4},{1,3},{2,6},{3,1},{4,0},{5,7},{6,2},{7,5},{8,12},{9,11},{10,... | collective-permute-start | bytes 1990664 | tf_op jit(solution)/shard_map/ppermute | solution.py:35
  15.9 1.8 %expert.7 = (f32[64,2560]{1,0:T(8,128)S(1)}, f32[64,2560]{1,0:T(8,128)S(1)}) custom-call(bf16[2560,768]{1,0:T(8,128)(2,1)S(1)} %get-tuple-element.24.refs_0_, bf16[2560,768]{1,0:T(8,128)(2,1)S(1)} %get-tuple-element.25.refs_1_, bf16[768,2560]{1,0:T(8,128)(2,1)S(1)} %get-tuple-element.26.refs_2_, bf16[2592,128]{1,0:T(8,128)(2,1)S(1)} %append.1.refs_3_, ...), custom_call_target="tpu_custom_call" | custom-call | flops 1509949440 | bytes 1310720 | tf_op jit(solution)/shard_map/expert/pallas_call | solution.py:241
  17.8 1.0 %collective-permute-done.3.refs_3_ = bf16[2592,128]{1,0:T(8,128)(2,1)S(1)} collective-permute-done((bf16[2592,128]{1,0:T(8,128)(2,1)S(1)}, bf16[2592,128]{1,0:T(8,128)(2,1)S(1)}, u32[]{:S(2)}, u32[]{:S(2)}) %collective-permute-start.3) | collective-permute-done | bytes 663584 | tf_op jit(solution)/shard_map/ppermute | solution.py:35
  18.8 1.8 %expert.8.refs_4_ = f32[128,2560]{1,0:T(8,128)S(1)} custom-call(bf16[2560,768]{1,0:T(8,128)(2,1)S(1)} %get-tuple-element.24.refs_0_, bf16[2560,768]{1,0:T(8,128)(2,1)S(1)} %get-tuple-element.25.refs_1_, bf16[768,2560]{1,0:T(8,128)(2,1)S(1)} %get-tuple-element.26.refs_2_, bf16[2592,128]{1,0:T(8,128)(2,1)S(1)} %collective-permute-done.3.refs_3_, ...), custom_call_target="tpu_custom_call" | custom-call | flops 1509949440 | bytes 1310720 | tf_op jit(solution)/shard_map/expert/pallas_call | solution.py:241
  20.6 1.8 %expert.9.refs_4_ = bf16[128,2560]{1,0:T(8,128)(2,1)S(1)} custom-call(bf16[2560,768]{1,0:T(8,128)(2,1)S(1)} %collective-permute-done.refs_1_.refs_0_, bf16[2560,768]{1,0:T(8,128)(2,1)S(1)} %collective-permute-done.1.refs_1_, bf16[768,2560]{1,0:T(8,128)(2,1)S(1)} %collective-permute-done.2.refs_2_, bf16[2592,128]{1,0:T(8,128)(2,1)S(1)} %collective-permute-done.3.refs_3_, ...), custom_call_target="tpu_custom_call" | custom-call | flops 1509949440 | bytes 1310720 | tf_op jit(solution)/shard_map/expert/pallas_call | solution.py:241
  22.3 1.8 %collective-permute-start.6 = (bf16[128,2560]{1,0:T(8,128)(2,1)S(1)}, bf16[128,2560]{1,0:T(8,128)(2,1)S(1)}, u32[]{:S(2)}, u32[]{:S(2)}) collective-permute-start(bf16[128,2560]{1,0:T(8,128)(2,1)S(1)} %expert.9.refs_4_), channel_id=1, source_target_pairs={{0,4},{1,3},{2,6},{3,1},{4,0},{5,7},{6,2},{7,5},{8,12},{9,11},{10,... | collective-permute-start | bytes 1966088 | tf_op jit(solution)/shard_map/ppermute | solution.py:35
  24.1 1.7 %collective-permute-done.7.refs_3_ = bf16[2592,128]{1,0:T(8,128)(2,1)S(1)} collective-permute-done((bf16[2592,128]{1,0:T(8,128)(2,1)S(1)}, bf16[2592,128]{1,0:T(8,128)(2,1)S(1)}, u32[]{:S(2)}, u32[]{:S(2)}) %collective-permute-start.7) | collective-permute-done | bytes 663584 | tf_op jit(solution)/shard_map/ppermute | solution.py:35
  25.9 1.8 %expert.10 = (f32[64,2560]{1,0:T(8,128)S(1)}, f32[64,2560]{1,0:T(8,128)S(1)}) custom-call(bf16[2560,768]{1,0:T(8,128)(2,1)S(1)} %get-tuple-element.24.refs_0_, bf16[2560,768]{1,0:T(8,128)(2,1)S(1)} %get-tuple-element.25.refs_1_, bf16[768,2560]{1,0:T(8,128)(2,1)S(1)} %get-tuple-element.26.refs_2_, bf16[2592,128]{1,0:T(8,128)(2,1)S(1)} %collective-permute-done.7.refs_3_, ...), custom_call_target="tpu_custom_call" | custom-call | flops 1509949440 | bytes 1310720 | tf_op jit(solution)/shard_map/expert/pallas_call | solution.py:241
  27.6 1.8 %expert.11 = (bf16[64,2560]{1,0:T(8,128)(2,1)S(1)}, bf16[64,2560]{1,0:T(8,128)(2,1)S(1)}) custom-call(bf16[2560,768]{1,0:T(8,128)(2,1)S(1)} %collective-permute-done.refs_1_.refs_0_, bf16[2560,768]{1,0:T(8,128)(2,1)S(1)} %collective-permute-done.1.refs_1_, bf16[768,2560]{1,0:T(8,128)(2,1)S(1)} %collective-permute-done.2.refs_2_, ...), custom_call_target="tpu_custom_call" | custom-call | flops 1509949440 | bytes 1310720 | tf_op jit(solution)/shard_map/expert/pallas_call | solution.py:241
  29.4 1.8 %collective-permute-start.10 = (bf16[64,2560]{1,0:T(8,128)(2,1)S(1)}, bf16[64,2560]{1,0:T(8,128)(2,1)S(1)}, u32[]{:S(2)}, u32[]{:S(2)}) collective-permute-start(bf16[64,2560]{1,0:T(8,128)(2,1)S(1)} %get-tuple-element.32.refs_7_), channel_id=1, source_target_pairs={{0,4},{1,3},{2,6},{3,1},{4,0},{5,7},{6,2},{7,5},{8,12},{9,11},{10,... | collective-permute-start | bytes 983048 | tf_op jit(solution)/shard_map/ppermute | solution.py:35
  31.2 0.3 collective-permute-start.8
  31.5 2.0 %expert.12 = (f32[64,2560]{1,0:T(8,128)S(1)}, f32[64,2560]{1,0:T(8,128)S(1)}) custom-call(bf16[2560,768]{1,0:T(8,128)(2,1)S(1)} %collective-permute-done.refs_1_.refs_0_, bf16[2560,768]{1,0:T(8,128)(2,1)S(1)} %collective-permute-done.1.refs_1_, bf16[768,2560]{1,0:T(8,128)(2,1)S(1)} %collective-permute-done.2.refs_2_, bf16[2592,128]{1,0:T(8,128)(2,1)S(1)} %append.1.refs_3_, ...), custom_call_target="tpu_custom_call" | custom-call | flops 1509949440 | bytes 1310720 | tf_op jit(solution)/shard_map/expert/pallas_call | solution.py:241
  33.6 1.9 %expert.13.refs_0_.total_ref = f32[128,2560]{1,0:T(8,128)S(1)} custom-call(bf16[2560,768]{1,0:T(8,128)(2,1)S(1)} %collective-permute-done.refs_1_.refs_0_, bf16[2560,768]{1,0:T(8,128)(2,1)S(1)} %collective-permute-done.1.refs_1_, bf16[768,2560]{1,0:T(8,128)(2,1)S(1)} %collective-permute-done.2.refs_2_, bf16[2592,128]{1,0:T(8,128)(2,1)S(1)} %get-tuple-element.20.refs_3_, ...), custom_call_target="tpu_custom_call" | custom-call | flops 1509949440 | bytes 1310720 | tf_op jit(solution)/shard_map/expert/pallas_call | solution.py:241
  35.4 1.1 %collective-permute-done.10.second_ref = bf16[64,2560]{1,0:T(8,128)(2,1)S(1)} collective-permute-done((bf16[64,2560]{1,0:T(8,128)(2,1)S(1)}, bf16[64,2560]{1,0:T(8,128)(2,1)S(1)}, u32[]{:S(2)}, u32[]{:S(2)}) %collective-permute-start.10) | collective-permute-done | bytes 327712 | tf_op jit(solution)/shard_map/ppermute | solution.py:35
  36.6 0.1 sums.3
  36.6 1.8 %collective-permute-start.11 = (bf16[64,2560]{1,0:T(8,128)(2,1)S(1)}, bf16[64,2560]{1,0:T(8,128)(2,1)S(1)}, u32[]{:S(2)}, u32[]{:S(2)}) collective-permute-start(bf16[64,2560]{1,0:T(8,128)(2,1)S(1)} %sums.3), channel_id=1, source_target_pairs={{0,2},{1,5},{2,0},{3,7},{4,6},{5,1},{6,4},{7,3},{8,10},{9,13},{10,... | collective-permute-start | bytes 983048 | tf_op jit(solution)/shard_map/ppermute | solution.py:35
  38.4 2.0 %collective-permute-done.8.second_ref = bf16[64,2560]{1,0:T(8,128)(2,1)S(1)} collective-permute-done((bf16[64,2560]{1,0:T(8,128)(2,1)S(1)}, bf16[64,2560]{1,0:T(8,128)(2,1)S(1)}, u32[]{:S(2)}, u32[]{:S(2)}) %collective-permute-start.8) | collective-permute-done | bytes 327712 | tf_op jit(solution)/shard_map/ppermute | solution.py:35
  40.4 1.8 %collective-permute-start.9 = (bf16[64,2560]{1,0:T(8,128)(2,1)S(1)}, bf16[64,2560]{1,0:T(8,128)(2,1)S(1)}, u32[]{:S(2)}, u32[]{:S(2)}) collective-permute-start(bf16[64,2560]{1,0:T(8,128)(2,1)S(1)} %sums.2), channel_id=1, source_target_pairs={{0,2},{1,5},{2,0},{3,7},{4,6},{5,1},{6,4},{7,3},{8,10},{9,13},{10,... | collective-permute-start | bytes 983048 | tf_op jit(solution)/shard_map/ppermute | solution.py:35
  42.2 1.5 %collective-permute-done.11.lower_ref = bf16[64,2560]{1,0:T(8,128)(2,1)S(1)} collective-permute-done((bf16[64,2560]{1,0:T(8,128)(2,1)S(1)}, bf16[64,2560]{1,0:T(8,128)(2,1)S(1)}, u32[]{:S(2)}, u32[]{:S(2)}) %collective-permute-start.11) | collective-permute-done | bytes 327712 | tf_op jit(solution)/shard_map/ppermute | solution.py:35
  43.8 3.8 %collective-permute-done.9.upper_ref = bf16[64,2560]{1,0:T(8,128)(2,1)S(1)} collective-permute-done((bf16[64,2560]{1,0:T(8,128)(2,1)S(1)}, bf16[64,2560]{1,0:T(8,128)(2,1)S(1)}, u32[]{:S(2)}, u32[]{:S(2)}) %collective-permute-start.9) | collective-permute-done | bytes 327712 | tf_op jit(solution)/shard_map/ppermute | solution.py:35
  47.6 0.9 %finish.1 = bf16[128,2560]{1,0:T(8,128)(2,1)} custom-call(f32[128,2560]{1,0:T(8,128)S(1)} %expert.13.refs_0_.total_ref, bf16[64,2560]{1,0:T(8,128)(2,1)S(1)} %collective-permute-done.9.upper_ref, bf16[64,2560]{1,0:T(8,128)(2,1)S(1)} %collective-permute-done.11.lower_ref), custom_call_target="tpu_custom_call" | custom-call | bytes 1310720 | tf_op jit(solution)/shard_map/finish/pallas_call | solution.py:285
  (6 shorter events, 0.1 us)
Async XLA Ops:
  0.0 9.3 %collective-permute-start = (bf16[2560,768]{1,0:T(8,128)(2,1)}, bf16[2560,768]{1,0:T(8,128)(2,1)S(1)}, u32[]{:S(2)}, u32[]{:S(2)}) collective-permute-start(bf16[2560,768]{1,0:T(8,128)(2,1)} %bitcast.7), channel_id=1, source_target_pairs={{0,1},{1,0},{2,3},{3,2},{4,5},{5,4},{6,7},{7,6},{8,9},{9,8},{10,11... | collective-permute-start | bytes 11796488 | tf_op jit(solution)/shard_map/ppermute | solution.py:35
  0.5 12.5 %collective-permute-start.4 = (bf16[128,2560]{1,0:T(8,128)(2,1)}, bf16[128,2560]{1,0:T(8,128)(2,1)S(1)}, u32[]{:S(2)}, u32[]{:S(2)}) collective-permute-start(bf16[128,2560]{1,0:T(8,128)(2,1)} %tokens_hbm.1), channel_id=1, source_target_pairs={{0,2},{1,5},{2,0},{3,7},{4,6},{5,1},{6,4},{7,3},{8,10},{9,13},{10,... | collective-permute-start | bytes 1966088 | tf_op jit(solution)/shard_map/ppermute | solution.py:35
  2.9 17.6 %collective-permute-start.1 = (bf16[2560,768]{1,0:T(8,128)(2,1)}, bf16[2560,768]{1,0:T(8,128)(2,1)S(1)}, u32[]{:S(2)}, u32[]{:S(2)}) collective-permute-start(bf16[2560,768]{1,0:T(8,128)(2,1)} %bitcast.9), channel_id=1, source_target_pairs={{0,1},{1,0},{2,3},{3,2},{4,5},{5,4},{6,7},{7,6},{8,9},{9,8},{10,11... | collective-permute-start | bytes 11796488 | tf_op jit(solution)/shard_map/ppermute | solution.py:35
  3.2 17.3 %collective-permute-start.2 = (bf16[768,2560]{1,0:T(8,128)(2,1)}, bf16[768,2560]{1,0:T(8,128)(2,1)S(1)}, u32[]{:S(2)}, u32[]{:S(2)}) collective-permute-start(bf16[768,2560]{1,0:T(8,128)(2,1)} %bitcast.5), channel_id=1, source_target_pairs={{0,1},{1,0},{2,3},{3,2},{4,5},{5,4},{6,7},{7,6},{8,9},{9,8},{10,11... | collective-permute-start | bytes 11796488 | tf_op jit(solution)/shard_map/ppermute | solution.py:35
  7.7 11.1 %collective-permute-start.3 = (bf16[2592,128]{1,0:T(8,128)(2,1)S(1)}, bf16[2592,128]{1,0:T(8,128)(2,1)S(1)}, u32[]{:S(2)}, u32[]{:S(2)}) collective-permute-start(bf16[2592,128]{1,0:T(8,128)(2,1)S(1)} %get-tuple-element.20.refs_3_), channel_id=1, source_target_pairs={{0,4},{1,3},{2,6},{3,1},{4,0},{5,7},{6,2},{7,5},{8,12},{9,11},{10,... | collective-permute-start | bytes 1990664 | tf_op jit(solution)/shard_map/ppermute | solution.py:35
  9.3 3.8 %collective-permute-start.5 = (bf16[32,128]{1,0:T(8,128)(2,1)S(1)}, bf16[32,128]{1,0:T(8,128)(2,1)S(1)}, u32[]{:S(2)}, u32[]{:S(2)}) collective-permute-start(bf16[32,128]{1,0:T(8,128)(2,1)S(1)} %held.1.terms_ref), channel_id=1, source_target_pairs={{0,2},{1,5},{2,0},{3,7},{4,6},{5,1},{6,4},{7,3},{8,10},{9,13},{10,... | collective-permute-start | bytes 24584 | tf_op jit(solution)/shard_map/ppermute | solution.py:35
  13.2 12.7 %collective-permute-start.7 = (bf16[2592,128]{1,0:T(8,128)(2,1)S(1)}, bf16[2592,128]{1,0:T(8,128)(2,1)S(1)}, u32[]{:S(2)}, u32[]{:S(2)}) collective-permute-start(bf16[2592,128]{1,0:T(8,128)(2,1)S(1)} %append.1.refs_3_), channel_id=1, source_target_pairs={{0,4},{1,3},{2,6},{3,1},{4,0},{5,7},{6,2},{7,5},{8,12},{9,11},{10,... | collective-permute-start | bytes 1990664 | tf_op jit(solution)/shard_map/ppermute | solution.py:35
  22.3 11.2 %collective-permute-start.6 = (bf16[128,2560]{1,0:T(8,128)(2,1)S(1)}, bf16[128,2560]{1,0:T(8,128)(2,1)S(1)}, u32[]{:S(2)}, u32[]{:S(2)}) collective-permute-start(bf16[128,2560]{1,0:T(8,128)(2,1)S(1)} %expert.9.refs_4_), channel_id=1, source_target_pairs={{0,4},{1,3},{2,6},{3,1},{4,0},{5,7},{6,2},{7,5},{8,12},{9,11},{10,... | collective-permute-start | bytes 1966088 | tf_op jit(solution)/shard_map/ppermute | solution.py:35
  29.4 7.1 %collective-permute-start.10 = (bf16[64,2560]{1,0:T(8,128)(2,1)S(1)}, bf16[64,2560]{1,0:T(8,128)(2,1)S(1)}, u32[]{:S(2)}, u32[]{:S(2)}) collective-permute-start(bf16[64,2560]{1,0:T(8,128)(2,1)S(1)} %get-tuple-element.32.refs_7_), channel_id=1, source_target_pairs={{0,4},{1,3},{2,6},{3,1},{4,0},{5,7},{6,2},{7,5},{8,12},{9,11},{10,... | collective-permute-start | bytes 983048 | tf_op jit(solution)/shard_map/ppermute | solution.py:35
  31.2 9.1 %collective-permute-start.8 = (bf16[64,2560]{1,0:T(8,128)(2,1)S(1)}, bf16[64,2560]{1,0:T(8,128)(2,1)S(1)}, u32[]{:S(2)}, u32[]{:S(2)}) collective-permute-start(bf16[64,2560]{1,0:T(8,128)(2,1)S(1)} %get-tuple-element.31.refs_6_), channel_id=1, source_target_pairs={{0,4},{1,3},{2,6},{3,1},{4,0},{5,7},{6,2},{7,5},{8,12},{9,11},{10,... | collective-permute-start | bytes 983048 | tf_op jit(solution)/shard_map/ppermute | solution.py:35
  36.6 7.1 %collective-permute-start.11 = (bf16[64,2560]{1,0:T(8,128)(2,1)S(1)}, bf16[64,2560]{1,0:T(8,128)(2,1)S(1)}, u32[]{:S(2)}, u32[]{:S(2)}) collective-permute-start(bf16[64,2560]{1,0:T(8,128)(2,1)S(1)} %sums.3), channel_id=1, source_target_pairs={{0,2},{1,5},{2,0},{3,7},{4,6},{5,1},{6,4},{7,3},{8,10},{9,13},{10,... | collective-permute-start | bytes 983048 | tf_op jit(solution)/shard_map/ppermute | solution.py:35
  40.4 7.1 %collective-permute-start.9 = (bf16[64,2560]{1,0:T(8,128)(2,1)S(1)}, bf16[64,2560]{1,0:T(8,128)(2,1)S(1)}, u32[]{:S(2)}, u32[]{:S(2)}) collective-permute-start(bf16[64,2560]{1,0:T(8,128)(2,1)S(1)} %sums.2), channel_id=1, source_target_pairs={{0,2},{1,5},{2,0},{3,7},{4,6},{5,1},{6,4},{7,3},{8,10},{9,13},{10,... | collective-permute-start | bytes 983048 | tf_op jit(solution)/shard_map/ppermute | solution.py:35

commit v8 on v7

--- a/solution.py
+++ b/solution.py
@@ -10,6 +10,8 @@
 CORE, X, Y = 1, 2, 4
 FIRST, SECOND = (X, Y), (Y, X)
 LANES = 128
+TERMS = 16
+HERE, THERE = 0, 2
 STEP = 256
 MIB = 2**20
 
@@ -35,12 +37,14 @@
     return lax.ppermute(value, "expert", [(i, i ^ offsets[i % 2]) for i in range(size)])
 
 
-def row_terms(ids, gates, experts):
+def row_terms(ids, gates, pairs):
     topk, rows = ids.shape
-    line = lax.broadcasted_iota(jnp.int32, (4 * experts, rows), 0)
-    expert = line
+    line = lax.broadcasted_iota(jnp.int32, (TERMS, rows), 0)
+    slot = line
     for _ in range(3):
-        expert = jnp.where(expert >= experts, expert - experts, expert)
+        slot = jnp.where(slot >= 4, slot - 4, slot)
+    apart = jnp.where(slot >= 2, pairs[1], pairs[0]) ^ jnp.where((slot == 1) | (slot == 3), CORE, 0)
+    expert = apart ^ lax.axis_index("expert")
     weight = jnp.zeros(line.shape, jnp.float32)
     for k in range(topk):
         weight += jnp.where(expert == ids[k : k + 1, :], gates[k : k + 1, :], 0.0)
@@ -48,15 +52,14 @@
     rest = weight - high
     middle = rest.astype(jnp.bfloat16).astype(jnp.float32)
     low = rest - middle
-    terms = jnp.where(line < experts, high, jnp.where(line < 2 * experts, middle, low))
-    return jnp.where(line < 3 * experts, terms, 0.0).astype(jnp.bfloat16)
-
-
-def row_weights(terms, experts, other):
+    terms = jnp.where(line < 4, high, jnp.where(line < 8, middle, low))
+    return jnp.where(line < 12, terms, 0.0).astype(jnp.bfloat16)
+
+
+def row_weights(terms, slot):
     count = terms.shape[1]
     line = lax.broadcasted_iota(jnp.int32, terms.shape, 0)
-    own = lax.axis_index("expert") ^ other
-    chosen = (line == own) | (line == own + experts) | (line == own + 2 * experts)
+    chosen = (line == slot) | (line == slot + 4) | (line == slot + 8)
     weights = jnp.sum(jnp.where(chosen, terms.astype(jnp.float32), 0.0), axis=0, keepdims=True)
     square = (count, count)
     same = lax.broadcasted_iota(jnp.int32, square, 0) == lax.broadcasted_iota(jnp.int32, square, 1)
@@ -86,7 +89,7 @@
 
 
 def own_hidden_kernel(
-    experts, tokens_hbm, ids_hbm, gates_hbm, gate_hbm, up_hbm, blocks_ref, terms_ref, hidden_ref, gate_ref, up_ref, ids, gates, tokens, done
+    tokens_hbm, ids_hbm, gates_hbm, gate_hbm, up_hbm, blocks_ref, terms_ref, hidden_ref, gate_ref, up_ref, ids, gates, tokens, done
 ):
     width = gate_ref.shape[1]
     pairs = [(ids_hbm, ids), (gates_hbm, gates), (tokens_hbm, tokens)]
@@ -99,8 +102,10 @@
         copy.start()
     copies[0].wait()
     copies[1].wait()
-    terms = row_terms(ids, gates, experts)
-    terms_ref[...] = terms
+    on_first = lax.axis_index("expert") % 2 == 0
+    first, second = jnp.where(on_first, X, Y), jnp.where(on_first, Y, X)
+    terms_ref[...] = row_terms(ids, gates, (first, X ^ Y))
+    terms = row_terms(ids, gates, (0, second))
     copies[2].wait()
     rows = tokens[...]
     put_blocks(rows, terms, blocks_ref)
@@ -112,15 +117,15 @@
         hidden_ref[:, columns] = hidden_columns(rows, gate_ref, up_ref, columns)
 
 
-def own_hidden(tokens, ids, gates, gate, up, experts):
+def own_hidden(tokens, ids, gates, gate, up):
     count, features = tokens.shape
     width = gate.shape[1]
     ids, gates = ids.T, gates.T
     return pl.pallas_call(
-        functools.partial(own_hidden_kernel, experts),
+        own_hidden_kernel,
         out_shape=[
-            jax.ShapeDtypeStruct((features + 4 * experts, LANES), tokens.dtype),
-            jax.ShapeDtypeStruct((4 * experts, LANES), tokens.dtype),
+            jax.ShapeDtypeStruct((features + TERMS, LANES), tokens.dtype),
+            jax.ShapeDtypeStruct((TERMS, LANES), tokens.dtype),
             jax.ShapeDtypeStruct((count, width), tokens.dtype),
             jax.ShapeDtypeStruct(gate.shape, gate.dtype),
             jax.ShapeDtypeStruct(up.shape, up.dtype),
@@ -139,7 +144,7 @@
     )(*[in_hbm(v) for v in (tokens, ids, gates, gate, up)])
 
 
-def own_answer_kernel(experts, hidden_ref, terms_ref, down_hbm, out_ref, down_ref, done):
+def own_answer_kernel(hidden_ref, blocks_ref, down_hbm, out_ref, down_ref, done):
     features = down_ref.shape[1]
     copies = []
     for i, at in enumerate(range(0, features, 2 * STEP)):
@@ -147,7 +152,7 @@
         copies.append(pltpu.make_async_copy(down_hbm.at[:, columns], down_ref.at[:, columns], done.at[i]))
     for copy in copies:
         copy.start()
-    weight = row_weights(terms_ref[...], experts, 0)
+    weight = row_weights(terms_of(blocks_ref, features), HERE)
     hidden = hidden_ref[...]
     for i, at in enumerate(range(0, features, 2 * STEP)):
         copies[i].wait()
@@ -155,11 +160,11 @@
         out_ref[:, columns] = jnp.dot(hidden, down_ref[:, columns], preferred_element_type=jnp.float32) * weight
 
 
-def own_answer(hidden, terms, down, experts):
+def own_answer(hidden, blocks, down):
     count, width = hidden.shape
     features = down.shape[1]
     return pl.pallas_call(
-        functools.partial(own_answer_kernel, experts),
+        own_answer_kernel,
         out_shape=[jax.ShapeDtypeStruct((count, features), jnp.float32), jax.ShapeDtypeStruct(down.shape, down.dtype)],
         in_specs=[whole()] * 2 + [anywhere()],
         out_specs=[whole()] * 2,
@@ -167,7 +172,7 @@
         compiler_params=pltpu.CompilerParams(vmem_limit_bytes=16 * MIB),
         cost_estimate=expert_cost(count, features, width // 3),
         name="own_answer",
-    )(in_vmem(hidden), in_vmem(terms), in_hbm(down))
+    )(in_vmem(hidden), in_vmem(blocks), in_hbm(down))
 
 
 def nothing(*refs):
@@ -210,14 +215,14 @@
     )
 
 
-def expert_kernel(experts, other, added, after, parts, *refs):
+def expert_kernel(slot, added, after, parts, *refs):
     gate_ref, up_ref, down_ref, blocks_ref = refs[:4]
     added_refs = refs[4 : 4 + added * parts]
     out_refs = refs[4 + added * parts + after : -1]
     hidden_ref = refs[-1]
     features, width = gate_ref.shape
     rows = rows_of(blocks_ref, features)
-    weight = row_weights(terms_of(blocks_ref, features), experts, other)
+    weight = row_weights(terms_of(blocks_ref, features), slot)
     for at in range(0, width, STEP):
         columns = slice(at, at + STEP)
         hidden_ref[:, columns] = hidden_columns(rows, gate_ref, up_ref, columns)
@@ -234,12 +239,12 @@
             start += out_ref.shape[0]
 
 
-def run_expert(weights, other, experts, blocks, kind, *added, parts=1, after=()):
+def run_expert(weights, slot, blocks, kind, *added, parts=1, after=()):
     features, width = weights[0].shape
     count = LANES
     operands = [in_vmem(v) for v in (*weights, blocks, *(v for group in added for v in group))]
     return pl.pallas_call(
-        functools.partial(expert_kernel, experts, other, len(added), len(after), parts),
+        functools.partial(expert_kernel, slot, len(added), len(after), parts),
         out_shape=[jax.ShapeDtypeStruct((count // parts, features), kind)] * parts,
         in_specs=[whole()] * len(operands) + [anywhere()] * len(after),
         out_specs=[whole()] * parts,
@@ -295,30 +300,34 @@
 
 
 def on_four_chips(tokens, expert_ids, gate_values, w_gate, w_up, w_down):
-    experts = lax.axis_size("expert")
     weights = (w_gate[0], w_up[0], w_down[0])
     wide, narrow = jnp.float32, jnp.bfloat16
     far = tuple(swap(w, (CORE, CORE)) for w in weights)
     first = swap(tokens, FIRST)
-    own, terms, hidden, near_gate, near_up = own_hidden(tokens, expert_ids, gate_values, *weights[:2], experts)
+    own, terms, hidden, near_gate, near_up = own_hidden(tokens, expert_ids, gate_values, *weights[:2])
     second = swap(own, SECOND)
     terms, = held(terms, after=far[:1])
-    near_own, near_down = own_answer(hidden, terms, weights[2], experts)
+    near_own, near_down = own_answer(hidden, own, weights[2])
     first = append(first, swap(terms, FIRST), near_own)
     third = swap(first, SECOND)
 
     near = (near_gate, near_up, near_down)
-    near_run = functools.partial(run_expert, near, 0, experts)
-    far_run = functools.partial(run_expert, far, CORE, experts)
-    near_first = near_run(first, wide, parts=2, after=[near_own])
-    near_second = near_run(second, wide, after=near_first)
-    sum_second = far_run(second, narrow, near_second)
+
+    def near_run(chip, *given, **options):
+        return run_expert(near, chip, *given, **options)
+
+    def far_run(chip, *given, **options):
+        return run_expert(far, chip + CORE, *given, **options)
+
+    near_first = near_run(HERE, first, wide, parts=2, after=[near_own])
+    near_second = near_run(THERE, second, wide, after=near_first)
+    sum_second = far_run(THERE, second, narrow, near_second)
     back_second = swap(sum_second[0], SECOND)
-    near_third = near_run(third, wide, parts=2, after=sum_second)
-    sum_third = far_run(third, narrow, near_third, parts=2)
+    near_third = near_run(THERE, third, wide, parts=2, after=sum_second)
+    sum_third = far_run(THERE, third, narrow, near_third, parts=2)
     passed_a, passed_b = swap(sum_third[0], SECOND), swap(sum_third[1], SECOND)
-    sum_first = far_run(first, wide, near_first, parts=2, after=sum_third)
-    sum_own = far_run(own, wide, [near_own], [back_second], after=sum_first)[0]
+    sum_first = far_run(HERE, first, wide, near_first, parts=2, after=sum_third)
+    sum_own = far_run(HERE, own, wide, [near_own], [back_second], after=sum_first)[0]
     back_first_a = swap(sums(sum_first[0], passed_a, after=[sum_own]), FIRST)
     back_first_b = swap(sums(sum_first[1], passed_b, after=[sum_own]), FIRST)
     return finish(sum_own, back_first_a, back_first_b)

time: 48.8 us -> 48.9 us (level)
  transfers between devices with their start and end apart: 12 -> 12, of which waited for: 8 -> 7; matrix products, arithmetic and copies ran while one was open for 0% -> 0% of each run, Pallas kernels for 41% -> 41%
where the time goes in v8:
time: 48.9 us; the launch traced here: 48.7 us
  Pallas kernels  20.7 us (42%)
  starting transfers between devices  16 us (33%)
  waiting for transfers between devices  11.7 us (24%)
    ppermute x12, starting transfers between devices, swap(): lax.ppermute(value, 'expert', [(i, i ^ offsets[i % 2]) for i in range(siz...  16 us
    pallas_call x7, Pallas kernels, run_expert(): pl.pallas_call(functools.partial(expert_kernel, slot, len(added), len(aft...  12.8 us
    ppermute x12, waiting for transfers between devices, swap(): lax.ppermute(value, 'expert', [(i, i ^ offsets[i % 2]) for i in range(siz...  11.7 us
    pallas_call x1, Pallas kernels, own_hidden(): pl.pallas_call(own_hidden_kernel, out_shape=[jax.ShapeDtypeStruct((featur...  4.19 us
    pallas_call x1, Pallas kernels, own_answer(): pl.pallas_call(own_answer_kernel, out_shape=[jax.ShapeDtypeStruct((count,...  2.55 us
  transfers between devices with their start and end apart: 12, of which 7 were waited for; matrix products, arithmetic and copies ran while one was open for 0% of the time, Pallas kernels for 41%

profile of v8, /device:TPU:0, one launch (start us, length us, event | category | flops | bytes accessed | tf_op | source)
XLA Modules:
  0.0 48.7 jit_solution(9183539545023685506)
XLA Ops:
  0.0 0.5 collective-permute-start
  0.5 2.5 %collective-permute-start.4 = (bf16[128,2560]{1,0:T(8,128)(2,1)}, bf16[128,2560]{1,0:T(8,128)(2,1)S(1)}, u32[]{:S(2)}, u32[]{:S(2)}) collective-permute-start(bf16[128,2560]{1,0:T(8,128)(2,1)} %tokens_hbm.1), channel_id=1, source_target_pairs={{0,2},{1,5},{2,0},{3,7},{4,6},{5,1},{6,4},{7,3},{8,10},{9,13},{10,... | collective-permute-start | bytes 1966088 | tf_op jit(solution)/shard_map/ppermute | solution.py:37
  2.9 0.3 collective-permute-start.1
  3.2 0.3 collective-permute-start.2
  3.5 4.2 %own_hidden.1 = (bf16[2576,128]{1,0:T(8,128)(2,1)S(1)}, bf16[16,128]{1,0:T(8,128)(2,1)S(1)}, bf16[128,768]{1,0:T(8,128)(2,1)S(1)}, bf16[2560,768]{1,0:T(8,128)(2,1)S(1)}, bf16[2560,768]{1,0:T(8,128)(2,1)S(1)}) custom-call(bf16[128,2560]{1,0:T(8,128)(2,1)} %tokens_hbm.1, s32[6,128]{1,0:T(8,128)} %bitcast.11, f32[6,128]{1,0:T(8,128)} %bitcast.12, ...), custom_call_target="tpu_custom_call" | custom-call | flops 54358179840 | bytes 47185920 | tf_op jit(solution)/shard_map/own_hidden/pallas_call | solution.py:124
  7.7 1.6 %collective-permute-start.3 = (bf16[2576,128]{1,0:T(8,128)(2,1)S(1)}, bf16[2576,128]{1,0:T(8,128)(2,1)S(1)}, u32[]{:S(2)}, u32[]{:S(2)}) collective-permute-start(bf16[2576,128]{1,0:T(8,128)(2,1)S(1)} %get-tuple-element.20.blocks_ref.refs_3_), channel_id=1, source_target_pairs={{0,4},{1,3},{2,6},{3,1},{4,0},{5,7},{6,2},{7,5},{8,12},{9,11},{10,... | collective-permute-start | bytes 1978376 | tf_op jit(solution)/shard_map/ppermute | solution.py:37
  9.2 0.7 %collective-permute-start.5 = (bf16[16,128]{1,0:T(8,128)(2,1)S(1)}, bf16[16,128]{1,0:T(8,128)(2,1)S(1)}, u32[]{:S(2)}, u32[]{:S(2)}) collective-permute-start(bf16[16,128]{1,0:T(8,128)(2,1)S(1)} %held.1), channel_id=1, source_target_pairs={{0,2},{1,5},{2,0},{3,7},{4,6},{5,1},{6,4},{7,3},{8,10},{9,13},{10,... | collective-permute-start | bytes 12296 | tf_op jit(solution)/shard_map/ppermute | solution.py:37
  9.9 2.6 %own_answer.1 = (f32[128,2560]{1,0:T(8,128)S(1)}, bf16[768,2560]{1,0:T(8,128)(2,1)S(1)}) custom-call(bf16[128,768]{1,0:T(8,128)(2,1)S(1)} %get-tuple-element.21.hidden_ref, bf16[2576,128]{1,0:T(8,128)(2,1)S(1)} %get-tuple-element.20.blocks_ref.refs_3_, bf16[768,2560]{1,0:T(8,128)(2,1)} %bitcast.6), custom_call_target="tpu_custom_call" | custom-call | flops 503316480 | bytes 1310720 | tf_op jit(solution)/shard_map/own_answer/pallas_call | solution.py:166
  12.5 0.5 collective-permute-done.4.rows_ref
  13.0 0.1 append.1.refs_3_
  13.1 2.8 %collective-permute-start.7 = (bf16[2576,128]{1,0:T(8,128)(2,1)S(1)}, bf16[2576,128]{1,0:T(8,128)(2,1)S(1)}, u32[]{:S(2)}, u32[]{:S(2)}) collective-permute-start(bf16[2576,128]{1,0:T(8,128)(2,1)S(1)} %append.1.refs_3_), channel_id=1, source_target_pairs={{0,4},{1,3},{2,6},{3,1},{4,0},{5,7},{6,2},{7,5},{8,12},{9,11},{10,... | collective-permute-start | bytes 1978376 | tf_op jit(solution)/shard_map/ppermute | solution.py:37
  15.9 1.8 %expert.7 = (f32[64,2560]{1,0:T(8,128)S(1)}, f32[64,2560]{1,0:T(8,128)S(1)}) custom-call(bf16[2560,768]{1,0:T(8,128)(2,1)S(1)} %get-tuple-element.23.refs_0_, bf16[2560,768]{1,0:T(8,128)(2,1)S(1)} %get-tuple-element.24.refs_1_, bf16[768,2560]{1,0:T(8,128)(2,1)S(1)} %get-tuple-element.25.refs_2_, bf16[2576,128]{1,0:T(8,128)(2,1)S(1)} %append.1.refs_3_, ...), custom_call_target="tpu_custom_call" | custom-call | flops 1509949440 | bytes 1310720 | tf_op jit(solution)/shard_map/expert/pallas_call | solution.py:246
  17.7 1.0 %collective-permute-done.3.refs_3_ = bf16[2576,128]{1,0:T(8,128)(2,1)S(1)} collective-permute-done((bf16[2576,128]{1,0:T(8,128)(2,1)S(1)}, bf16[2576,128]{1,0:T(8,128)(2,1)S(1)}, u32[]{:S(2)}, u32[]{:S(2)}) %collective-permute-start.3) | collective-permute-done | bytes 659488 | tf_op jit(solution)/shard_map/ppermute | solution.py:37
  18.7 1.8 %expert.8.refs_4_ = f32[128,2560]{1,0:T(8,128)S(1)} custom-call(bf16[2560,768]{1,0:T(8,128)(2,1)S(1)} %get-tuple-element.23.refs_0_, bf16[2560,768]{1,0:T(8,128)(2,1)S(1)} %get-tuple-element.24.refs_1_, bf16[768,2560]{1,0:T(8,128)(2,1)S(1)} %get-tuple-element.25.refs_2_, bf16[2576,128]{1,0:T(8,128)(2,1)S(1)} %collective-permute-done.3.refs_3_, ...), custom_call_target="tpu_custom_call" | custom-call | flops 1509949440 | bytes 1310720 | tf_op jit(solution)/shard_map/expert/pallas_call | solution.py:246
  20.5 1.8 %expert.9.refs_4_ = bf16[128,2560]{1,0:T(8,128)(2,1)S(1)} custom-call(bf16[2560,768]{1,0:T(8,128)(2,1)S(1)} %collective-permute-done.refs_1_.refs_0_, bf16[2560,768]{1,0:T(8,128)(2,1)S(1)} %collective-permute-done.1.refs_1_, bf16[768,2560]{1,0:T(8,128)(2,1)S(1)} %collective-permute-done.2.refs_2_, bf16[2576,128]{1,0:T(8,128)(2,1)S(1)} %collective-permute-done.3.refs_3_, ...), custom_call_target="tpu_custom_call" | custom-call | flops 1509949440 | bytes 1310720 | tf_op jit(solution)/shard_map/expert/pallas_call | solution.py:246
  22.3 1.8 %collective-permute-start.6 = (bf16[128,2560]{1,0:T(8,128)(2,1)S(1)}, bf16[128,2560]{1,0:T(8,128)(2,1)S(1)}, u32[]{:S(2)}, u32[]{:S(2)}) collective-permute-start(bf16[128,2560]{1,0:T(8,128)(2,1)S(1)} %expert.9.refs_4_), channel_id=1, source_target_pairs={{0,4},{1,3},{2,6},{3,1},{4,0},{5,7},{6,2},{7,5},{8,12},{9,11},{10,... | collective-permute-start | bytes 1966088 | tf_op jit(solution)/shard_map/ppermute | solution.py:37
  24.1 1.7 %collective-permute-done.7.refs_3_ = bf16[2576,128]{1,0:T(8,128)(2,1)S(1)} collective-permute-done((bf16[2576,128]{1,0:T(8,128)(2,1)S(1)}, bf16[2576,128]{1,0:T(8,128)(2,1)S(1)}, u32[]{:S(2)}, u32[]{:S(2)}) %collective-permute-start.7) | collective-permute-done | bytes 659488 | tf_op jit(solution)/shard_map/ppermute | solution.py:37
  25.7 1.8 %expert.10 = (f32[64,2560]{1,0:T(8,128)S(1)}, f32[64,2560]{1,0:T(8,128)S(1)}) custom-call(bf16[2560,768]{1,0:T(8,128)(2,1)S(1)} %get-tuple-element.23.refs_0_, bf16[2560,768]{1,0:T(8,128)(2,1)S(1)} %get-tuple-element.24.refs_1_, bf16[768,2560]{1,0:T(8,128)(2,1)S(1)} %get-tuple-element.25.refs_2_, bf16[2576,128]{1,0:T(8,128)(2,1)S(1)} %collective-permute-done.7.refs_3_, ...), custom_call_target="tpu_custom_call" | custom-call | flops 1509949440 | bytes 1310720 | tf_op jit(solution)/shard_map/expert/pallas_call | solution.py:246
  27.6 1.8 %expert.11 = (bf16[64,2560]{1,0:T(8,128)(2,1)S(1)}, bf16[64,2560]{1,0:T(8,128)(2,1)S(1)}) custom-call(bf16[2560,768]{1,0:T(8,128)(2,1)S(1)} %collective-permute-done.refs_1_.refs_0_, bf16[2560,768]{1,0:T(8,128)(2,1)S(1)} %collective-permute-done.1.refs_1_, bf16[768,2560]{1,0:T(8,128)(2,1)S(1)} %collective-permute-done.2.refs_2_, ...), custom_call_target="tpu_custom_call" | custom-call | flops 1509949440 | bytes 1310720 | tf_op jit(solution)/shard_map/expert/pallas_call | solution.py:246
  29.4 1.8 %collective-permute-start.10 = (bf16[64,2560]{1,0:T(8,128)(2,1)S(1)}, bf16[64,2560]{1,0:T(8,128)(2,1)S(1)}, u32[]{:S(2)}, u32[]{:S(2)}) collective-permute-start(bf16[64,2560]{1,0:T(8,128)(2,1)S(1)} %get-tuple-element.32.refs_7_), channel_id=1, source_target_pairs={{0,4},{1,3},{2,6},{3,1},{4,0},{5,7},{6,2},{7,5},{8,12},{9,11},{10,... | collective-permute-start | bytes 983048 | tf_op jit(solution)/shard_map/ppermute | solution.py:37
  31.2 0.3 collective-permute-start.8
  31.5 2.0 %expert.12 = (f32[64,2560]{1,0:T(8,128)S(1)}, f32[64,2560]{1,0:T(8,128)S(1)}) custom-call(bf16[2560,768]{1,0:T(8,128)(2,1)S(1)} %collective-permute-done.refs_1_.refs_0_, bf16[2560,768]{1,0:T(8,128)(2,1)S(1)} %collective-permute-done.1.refs_1_, bf16[768,2560]{1,0:T(8,128)(2,1)S(1)} %collective-permute-done.2.refs_2_, bf16[2576,128]{1,0:T(8,128)(2,1)S(1)} %append.1.refs_3_, ...), custom_call_target="tpu_custom_call" | custom-call | flops 1509949440 | bytes 1310720 | tf_op jit(solution)/shard_map/expert/pallas_call | solution.py:246
  33.5 1.8 %expert.13.refs_0_.total_ref = f32[128,2560]{1,0:T(8,128)S(1)} custom-call(bf16[2560,768]{1,0:T(8,128)(2,1)S(1)} %collective-permute-done.refs_1_.refs_0_, bf16[2560,768]{1,0:T(8,128)(2,1)S(1)} %collective-permute-done.1.refs_1_, bf16[768,2560]{1,0:T(8,128)(2,1)S(1)} %collective-permute-done.2.refs_2_, ...), custom_call_target="tpu_custom_call" | custom-call | flops 1509949440 | bytes 1310720 | tf_op jit(solution)/shard_map/expert/pallas_call | solution.py:246
  35.3 1.2 %collective-permute-done.10.second_ref = bf16[64,2560]{1,0:T(8,128)(2,1)S(1)} collective-permute-done((bf16[64,2560]{1,0:T(8,128)(2,1)S(1)}, bf16[64,2560]{1,0:T(8,128)(2,1)S(1)}, u32[]{:S(2)}, u32[]{:S(2)}) %collective-permute-start.10) | collective-permute-done | bytes 327712 | tf_op jit(solution)/shard_map/ppermute | solution.py:37
  36.5 0.1 sums.3
  36.6 1.8 %collective-permute-start.11 = (bf16[64,2560]{1,0:T(8,128)(2,1)S(1)}, bf16[64,2560]{1,0:T(8,128)(2,1)S(1)}, u32[]{:S(2)}, u32[]{:S(2)}) collective-permute-start(bf16[64,2560]{1,0:T(8,128)(2,1)S(1)} %sums.3), channel_id=1, source_target_pairs={{0,2},{1,5},{2,0},{3,7},{4,6},{5,1},{6,4},{7,3},{8,10},{9,13},{10,... | collective-permute-start | bytes 983048 | tf_op jit(solution)/shard_map/ppermute | solution.py:37
  38.4 2.1 %collective-permute-done.8.second_ref = bf16[64,2560]{1,0:T(8,128)(2,1)S(1)} collective-permute-done((bf16[64,2560]{1,0:T(8,128)(2,1)S(1)}, bf16[64,2560]{1,0:T(8,128)(2,1)S(1)}, u32[]{:S(2)}, u32[]{:S(2)}) %collective-permute-start.8) | collective-permute-done | bytes 327712 | tf_op jit(solution)/shard_map/ppermute | solution.py:37
  40.4 0.1 sums.2
  40.5 1.8 %collective-permute-start.9 = (bf16[64,2560]{1,0:T(8,128)(2,1)S(1)}, bf16[64,2560]{1,0:T(8,128)(2,1)S(1)}, u32[]{:S(2)}, u32[]{:S(2)}) collective-permute-start(bf16[64,2560]{1,0:T(8,128)(2,1)S(1)} %sums.2), channel_id=1, source_target_pairs={{0,2},{1,5},{2,0},{3,7},{4,6},{5,1},{6,4},{7,3},{8,10},{9,13},{10,... | collective-permute-start | bytes 983048 | tf_op jit(solution)/shard_map/ppermute | solution.py:37
  42.3 1.4 %collective-permute-done.11.lower_ref = bf16[64,2560]{1,0:T(8,128)(2,1)S(1)} collective-permute-done((bf16[64,2560]{1,0:T(8,128)(2,1)S(1)}, bf16[64,2560]{1,0:T(8,128)(2,1)S(1)}, u32[]{:S(2)}, u32[]{:S(2)}) %collective-permute-start.11) | collective-permute-done | bytes 327712 | tf_op jit(solution)/shard_map/ppermute | solution.py:37
  43.7 3.9 %collective-permute-done.9.upper_ref = bf16[64,2560]{1,0:T(8,128)(2,1)S(1)} collective-permute-done((bf16[64,2560]{1,0:T(8,128)(2,1)S(1)}, bf16[64,2560]{1,0:T(8,128)(2,1)S(1)}, u32[]{:S(2)}, u32[]{:S(2)}) %collective-permute-start.9) | collective-permute-done | bytes 327712 | tf_op jit(solution)/shard_map/ppermute | solution.py:37
  47.6 0.9 %finish.1 = bf16[128,2560]{1,0:T(8,128)(2,1)} custom-call(f32[128,2560]{1,0:T(8,128)S(1)} %expert.13.refs_0_.total_ref, bf16[64,2560]{1,0:T(8,128)(2,1)S(1)} %collective-permute-done.9.upper_ref, bf16[64,2560]{1,0:T(8,128)(2,1)S(1)} %collective-permute-done.11.lower_ref), custom_call_target="tpu_custom_call" | custom-call | bytes 1310720 | tf_op jit(solution)/shard_map/finish/pallas_call | solution.py:290
  (6 shorter events, 0.0 us)
Async XLA Ops:
  0.0 9.2 %collective-permute-start = (bf16[2560,768]{1,0:T(8,128)(2,1)}, bf16[2560,768]{1,0:T(8,128)(2,1)S(1)}, u32[]{:S(2)}, u32[]{:S(2)}) collective-permute-start(bf16[2560,768]{1,0:T(8,128)(2,1)} %bitcast.7), channel_id=1, source_target_pairs={{0,1},{1,0},{2,3},{3,2},{4,5},{5,4},{6,7},{7,6},{8,9},{9,8},{10,11... | collective-permute-start | bytes 11796488 | tf_op jit(solution)/shard_map/ppermute | solution.py:37
  0.5 12.5 %collective-permute-start.4 = (bf16[128,2560]{1,0:T(8,128)(2,1)}, bf16[128,2560]{1,0:T(8,128)(2,1)S(1)}, u32[]{:S(2)}, u32[]{:S(2)}) collective-permute-start(bf16[128,2560]{1,0:T(8,128)(2,1)} %tokens_hbm.1), channel_id=1, source_target_pairs={{0,2},{1,5},{2,0},{3,7},{4,6},{5,1},{6,4},{7,3},{8,10},{9,13},{10,... | collective-permute-start | bytes 1966088 | tf_op jit(solution)/shard_map/ppermute | solution.py:37
  2.9 17.5 %collective-permute-start.1 = (bf16[2560,768]{1,0:T(8,128)(2,1)}, bf16[2560,768]{1,0:T(8,128)(2,1)S(1)}, u32[]{:S(2)}, u32[]{:S(2)}) collective-permute-start(bf16[2560,768]{1,0:T(8,128)(2,1)} %bitcast.9), channel_id=1, source_target_pairs={{0,1},{1,0},{2,3},{3,2},{4,5},{5,4},{6,7},{7,6},{8,9},{9,8},{10,11... | collective-permute-start | bytes 11796488 | tf_op jit(solution)/shard_map/ppermute | solution.py:37
  3.2 17.3 %collective-permute-start.2 = (bf16[768,2560]{1,0:T(8,128)(2,1)}, bf16[768,2560]{1,0:T(8,128)(2,1)S(1)}, u32[]{:S(2)}, u32[]{:S(2)}) collective-permute-start(bf16[768,2560]{1,0:T(8,128)(2,1)} %bitcast.5), channel_id=1, source_target_pairs={{0,1},{1,0},{2,3},{3,2},{4,5},{5,4},{6,7},{7,6},{8,9},{9,8},{10,11... | collective-permute-start | bytes 11796488 | tf_op jit(solution)/shard_map/ppermute | solution.py:37
  7.7 11.0 %collective-permute-start.3 = (bf16[2576,128]{1,0:T(8,128)(2,1)S(1)}, bf16[2576,128]{1,0:T(8,128)(2,1)S(1)}, u32[]{:S(2)}, u32[]{:S(2)}) collective-permute-start(bf16[2576,128]{1,0:T(8,128)(2,1)S(1)} %get-tuple-element.20.blocks_ref.refs_3_), channel_id=1, source_target_pairs={{0,4},{1,3},{2,6},{3,1},{4,0},{5,7},{6,2},{7,5},{8,12},{9,11},{10,... | collective-permute-start | bytes 1978376 | tf_op jit(solution)/shard_map/ppermute | solution.py:37
  9.2 3.7 %collective-permute-start.5 = (bf16[16,128]{1,0:T(8,128)(2,1)S(1)}, bf16[16,128]{1,0:T(8,128)(2,1)S(1)}, u32[]{:S(2)}, u32[]{:S(2)}) collective-permute-start(bf16[16,128]{1,0:T(8,128)(2,1)S(1)} %held.1), channel_id=1, source_target_pairs={{0,2},{1,5},{2,0},{3,7},{4,6},{5,1},{6,4},{7,3},{8,10},{9,13},{10,... | collective-permute-start | bytes 12296 | tf_op jit(solution)/shard_map/ppermute | solution.py:37
  13.1 12.7 %collective-permute-start.7 = (bf16[2576,128]{1,0:T(8,128)(2,1)S(1)}, bf16[2576,128]{1,0:T(8,128)(2,1)S(1)}, u32[]{:S(2)}, u32[]{:S(2)}) collective-permute-start(bf16[2576,128]{1,0:T(8,128)(2,1)S(1)} %append.1.refs_3_), channel_id=1, source_target_pairs={{0,4},{1,3},{2,6},{3,1},{4,0},{5,7},{6,2},{7,5},{8,12},{9,11},{10,... | collective-permute-start | bytes 1978376 | tf_op jit(solution)/shard_map/ppermute | solution.py:37
  22.3 11.2 %collective-permute-start.6 = (bf16[128,2560]{1,0:T(8,128)(2,1)S(1)}, bf16[128,2560]{1,0:T(8,128)(2,1)S(1)}, u32[]{:S(2)}, u32[]{:S(2)}) collective-permute-start(bf16[128,2560]{1,0:T(8,128)(2,1)S(1)} %expert.9.refs_4_), channel_id=1, source_target_pairs={{0,4},{1,3},{2,6},{3,1},{4,0},{5,7},{6,2},{7,5},{8,12},{9,11},{10,... | collective-permute-start | bytes 1966088 | tf_op jit(solution)/shard_map/ppermute | solution.py:37
  29.4 7.1 %collective-permute-start.10 = (bf16[64,2560]{1,0:T(8,128)(2,1)S(1)}, bf16[64,2560]{1,0:T(8,128)(2,1)S(1)}, u32[]{:S(2)}, u32[]{:S(2)}) collective-permute-start(bf16[64,2560]{1,0:T(8,128)(2,1)S(1)} %get-tuple-element.32.refs_7_), channel_id=1, source_target_pairs={{0,4},{1,3},{2,6},{3,1},{4,0},{5,7},{6,2},{7,5},{8,12},{9,11},{10,... | collective-permute-start | bytes 983048 | tf_op jit(solution)/shard_map/ppermute | solution.py:37
  31.2 9.2 %collective-permute-start.8 = (bf16[64,2560]{1,0:T(8,128)(2,1)S(1)}, bf16[64,2560]{1,0:T(8,128)(2,1)S(1)}, u32[]{:S(2)}, u32[]{:S(2)}) collective-permute-start(bf16[64,2560]{1,0:T(8,128)(2,1)S(1)} %get-tuple-element.31.refs_6_), channel_id=1, source_target_pairs={{0,4},{1,3},{2,6},{3,1},{4,0},{5,7},{6,2},{7,5},{8,12},{9,11},{10,... | collective-permute-start | bytes 983048 | tf_op jit(solution)/shard_map/ppermute | solution.py:37
  36.6 7.1 %collective-permute-start.11 = (bf16[64,2560]{1,0:T(8,128)(2,1)S(1)}, bf16[64,2560]{1,0:T(8,128)(2,1)S(1)}, u32[]{:S(2)}, u32[]{:S(2)}) collective-permute-start(bf16[64,2560]{1,0:T(8,128)(2,1)S(1)} %sums.3), channel_id=1, source_target_pairs={{0,2},{1,5},{2,0},{3,7},{4,6},{5,1},{6,4},{7,3},{8,10},{9,13},{10,... | collective-permute-start | bytes 983048 | tf_op jit(solution)/shard_map/ppermute | solution.py:37
  40.5 7.1 %collective-permute-start.9 = (bf16[64,2560]{1,0:T(8,128)(2,1)S(1)}, bf16[64,2560]{1,0:T(8,128)(2,1)S(1)}, u32[]{:S(2)}, u32[]{:S(2)}) collective-permute-start(bf16[64,2560]{1,0:T(8,128)(2,1)S(1)} %sums.2), channel_id=1, source_target_pairs={{0,2},{1,5},{2,0},{3,7},{4,6},{5,1},{6,4},{7,3},{8,10},{9,13},{10,... | collective-permute-start | bytes 983048 | tf_op jit(solution)/shard_map/ppermute | solution.py:37

commit v9 on v7

--- a/solution.py
+++ b/solution.py
@@ -319,8 +319,8 @@
     passed_a, passed_b = swap(sum_third[0], SECOND), swap(sum_third[1], SECOND)
     sum_first = far_run(first, wide, near_first, parts=2, after=sum_third)
     sum_own = far_run(own, wide, [near_own], [back_second], after=sum_first)[0]
-    back_first_a = swap(sums(sum_first[0], passed_a, after=[sum_own]), FIRST)
-    back_first_b = swap(sums(sum_first[1], passed_b, after=[sum_own]), FIRST)
+    back_first_a = swap(sums(sum_first[0], passed_a), FIRST)
+    back_first_b = swap(sums(sum_first[1], passed_b), FIRST)
     return finish(sum_own, back_first_a, back_first_b)
 
 

time: 48.8 us -> 48.8 us (level)
  transfers between devices with their start and end apart: 12 -> 12, of which waited for: 8 -> 7; matrix products, arithmetic and copies ran while one was open for 0% -> 0% of each run, Pallas kernels for 41% -> 41%
where the time goes in v9:
time: 48.8 us; the launch traced here: 48.7 us
  Pallas kernels  20.7 us (42%)
  starting transfers between devices  16 us (33%)
  waiting for transfers between devices  11.7 us (24%)
    ppermute x12, starting transfers between devices, swap(): lax.ppermute(value, 'expert', [(i, i ^ offsets[i % 2]) for i in range(siz...  16 us
    pallas_call x7, Pallas kernels, run_expert(): pl.pallas_call(functools.partial(expert_kernel, experts, other, len(added...  12.8 us
    ppermute x12, waiting for transfers between devices, swap(): lax.ppermute(value, 'expert', [(i, i ^ offsets[i % 2]) for i in range(siz...  11.7 us
    pallas_call x1, Pallas kernels, own_hidden(): pl.pallas_call(functools.partial(own_hidden_kernel, experts), out_shape=[...  4.2 us
    pallas_call x1, Pallas kernels, own_answer(): pl.pallas_call(functools.partial(own_answer_kernel, experts), out_shape=[...  2.55 us
  transfers between devices with their start and end apart: 12, of which 7 were waited for; matrix products, arithmetic and copies ran while one was open for 0% of the time, Pallas kernels for 41%

profile of v9, /device:TPU:0, one launch (start us, length us, event | category | flops | bytes accessed | tf_op | source)
XLA Modules:
  0.0 48.7 jit_solution(3652145330362198936)
XLA Ops:
  0.0 0.5 collective-permute-start
  0.5 2.5 %collective-permute-start.4 = (bf16[128,2560]{1,0:T(8,128)(2,1)}, bf16[128,2560]{1,0:T(8,128)(2,1)S(1)}, u32[]{:S(2)}, u32[]{:S(2)}) collective-permute-start(bf16[128,2560]{1,0:T(8,128)(2,1)} %tokens_hbm.1), channel_id=1, source_target_pairs={{0,2},{1,5},{2,0},{3,7},{4,6},{5,1},{6,4},{7,3},{8,10},{9,13},{10,... | collective-permute-start | bytes 1966088 | tf_op jit(solution)/shard_map/ppermute | solution.py:35
  2.9 0.3 collective-permute-start.1
  3.2 0.3 collective-permute-start.2
  3.5 4.2 %own_hidden.1 = (bf16[2592,128]{1,0:T(8,128)(2,1)S(1)}, bf16[32,128]{1,0:T(8,128)(2,1)S(1)}, bf16[128,768]{1,0:T(8,128)(2,1)S(1)}, bf16[2560,768]{1,0:T(8,128)(2,1)S(1)}, bf16[2560,768]{1,0:T(8,128)(2,1)S(1)}) custom-call(bf16[128,2560]{1,0:T(8,128)(2,1)} %tokens_hbm.1, s32[6,128]{1,0:T(8,128)} %bitcast.11, f32[6,128]{1,0:T(8,128)} %bitcast.12, ...), custom_call_target="tpu_custom_call" | custom-call | flops 54358179840 | bytes 47185920 | tf_op jit(solution)/shard_map/own_hidden/pallas_call | solution.py:119
  7.7 1.6 %collective-permute-start.3 = (bf16[2592,128]{1,0:T(8,128)(2,1)S(1)}, bf16[2592,128]{1,0:T(8,128)(2,1)S(1)}, u32[]{:S(2)}, u32[]{:S(2)}) collective-permute-start(bf16[2592,128]{1,0:T(8,128)(2,1)S(1)} %get-tuple-element.20.refs_3_), channel_id=1, source_target_pairs={{0,4},{1,3},{2,6},{3,1},{4,0},{5,7},{6,2},{7,5},{8,12},{9,11},{10,... | collective-permute-start | bytes 1990664 | tf_op jit(solution)/shard_map/ppermute | solution.py:35
  9.3 0.7 %collective-permute-start.5 = (bf16[32,128]{1,0:T(8,128)(2,1)S(1)}, bf16[32,128]{1,0:T(8,128)(2,1)S(1)}, u32[]{:S(2)}, u32[]{:S(2)}) collective-permute-start(bf16[32,128]{1,0:T(8,128)(2,1)S(1)} %held.1.terms_ref), channel_id=1, source_target_pairs={{0,2},{1,5},{2,0},{3,7},{4,6},{5,1},{6,4},{7,3},{8,10},{9,13},{10,... | collective-permute-start | bytes 24584 | tf_op jit(solution)/shard_map/ppermute | solution.py:35
  9.9 2.6 %own_answer.1 = (f32[128,2560]{1,0:T(8,128)S(1)}, bf16[768,2560]{1,0:T(8,128)(2,1)S(1)}) custom-call(bf16[128,768]{1,0:T(8,128)(2,1)S(1)} %get-tuple-element.21.hidden_ref, bf16[32,128]{1,0:T(8,128)(2,1)S(1)} %held.1.terms_ref, bf16[768,2560]{1,0:T(8,128)(2,1)} %bitcast.6), custom_call_target="tpu_custom_call" | custom-call | flops 503316480 | bytes 1310720 | tf_op jit(solution)/shard_map/own_answer/pallas_call | solution.py:161
  12.5 0.5 collective-permute-done.4.rows_ref
  13.0 0.1 collective-permute-done.5.terms_ref
  13.1 0.1 append.1.refs_3_
  13.2 2.8 %collective-permute-start.7 = (bf16[2592,128]{1,0:T(8,128)(2,1)S(1)}, bf16[2592,128]{1,0:T(8,128)(2,1)S(1)}, u32[]{:S(2)}, u32[]{:S(2)}) collective-permute-start(bf16[2592,128]{1,0:T(8,128)(2,1)S(1)} %append.1.refs_3_), channel_id=1, source_target_pairs={{0,4},{1,3},{2,6},{3,1},{4,0},{5,7},{6,2},{7,5},{8,12},{9,11},{10,... | collective-permute-start | bytes 1990664 | tf_op jit(solution)/shard_map/ppermute | solution.py:35
  15.9 1.8 %expert.7 = (f32[64,2560]{1,0:T(8,128)S(1)}, f32[64,2560]{1,0:T(8,128)S(1)}) custom-call(bf16[2560,768]{1,0:T(8,128)(2,1)S(1)} %get-tuple-element.24.refs_0_, bf16[2560,768]{1,0:T(8,128)(2,1)S(1)} %get-tuple-element.25.refs_1_, bf16[768,2560]{1,0:T(8,128)(2,1)S(1)} %get-tuple-element.26.refs_2_, bf16[2592,128]{1,0:T(8,128)(2,1)S(1)} %append.1.refs_3_, ...), custom_call_target="tpu_custom_call" | custom-call | flops 1509949440 | bytes 1310720 | tf_op jit(solution)/shard_map/expert/pallas_call | solution.py:241
  17.8 1.0 %collective-permute-done.3.refs_3_ = bf16[2592,128]{1,0:T(8,128)(2,1)S(1)} collective-permute-done((bf16[2592,128]{1,0:T(8,128)(2,1)S(1)}, bf16[2592,128]{1,0:T(8,128)(2,1)S(1)}, u32[]{:S(2)}, u32[]{:S(2)}) %collective-permute-start.3) | collective-permute-done | bytes 663584 | tf_op jit(solution)/shard_map/ppermute | solution.py:35
  18.8 1.8 %expert.8.refs_4_ = f32[128,2560]{1,0:T(8,128)S(1)} custom-call(bf16[2560,768]{1,0:T(8,128)(2,1)S(1)} %get-tuple-element.24.refs_0_, bf16[2560,768]{1,0:T(8,128)(2,1)S(1)} %get-tuple-element.25.refs_1_, bf16[768,2560]{1,0:T(8,128)(2,1)S(1)} %get-tuple-element.26.refs_2_, bf16[2592,128]{1,0:T(8,128)(2,1)S(1)} %collective-permute-done.3.refs_3_, ...), custom_call_target="tpu_custom_call" | custom-call | flops 1509949440 | bytes 1310720 | tf_op jit(solution)/shard_map/expert/pallas_call | solution.py:241
  20.6 1.8 %expert.9.refs_4_ = bf16[128,2560]{1,0:T(8,128)(2,1)S(1)} custom-call(bf16[2560,768]{1,0:T(8,128)(2,1)S(1)} %collective-permute-done.refs_1_.refs_0_, bf16[2560,768]{1,0:T(8,128)(2,1)S(1)} %collective-permute-done.1.refs_1_, bf16[768,2560]{1,0:T(8,128)(2,1)S(1)} %collective-permute-done.2.refs_2_, bf16[2592,128]{1,0:T(8,128)(2,1)S(1)} %collective-permute-done.3.refs_3_, ...), custom_call_target="tpu_custom_call" | custom-call | flops 1509949440 | bytes 1310720 | tf_op jit(solution)/shard_map/expert/pallas_call | solution.py:241
  22.3 1.8 %collective-permute-start.6 = (bf16[128,2560]{1,0:T(8,128)(2,1)S(1)}, bf16[128,2560]{1,0:T(8,128)(2,1)S(1)}, u32[]{:S(2)}, u32[]{:S(2)}) collective-permute-start(bf16[128,2560]{1,0:T(8,128)(2,1)S(1)} %expert.9.refs_4_), channel_id=1, source_target_pairs={{0,4},{1,3},{2,6},{3,1},{4,0},{5,7},{6,2},{7,5},{8,12},{9,11},{10,... | collective-permute-start | bytes 1966088 | tf_op jit(solution)/shard_map/ppermute | solution.py:35
  24.1 1.7 %collective-permute-done.7.refs_3_ = bf16[2592,128]{1,0:T(8,128)(2,1)S(1)} collective-permute-done((bf16[2592,128]{1,0:T(8,128)(2,1)S(1)}, bf16[2592,128]{1,0:T(8,128)(2,1)S(1)}, u32[]{:S(2)}, u32[]{:S(2)}) %collective-permute-start.7) | collective-permute-done | bytes 663584 | tf_op jit(solution)/shard_map/ppermute | solution.py:35
  25.9 1.8 %expert.10 = (f32[64,2560]{1,0:T(8,128)S(1)}, f32[64,2560]{1,0:T(8,128)S(1)}) custom-call(bf16[2560,768]{1,0:T(8,128)(2,1)S(1)} %get-tuple-element.24.refs_0_, bf16[2560,768]{1,0:T(8,128)(2,1)S(1)} %get-tuple-element.25.refs_1_, bf16[768,2560]{1,0:T(8,128)(2,1)S(1)} %get-tuple-element.26.refs_2_, bf16[2592,128]{1,0:T(8,128)(2,1)S(1)} %collective-permute-done.7.refs_3_, ...), custom_call_target="tpu_custom_call" | custom-call | flops 1509949440 | bytes 1310720 | tf_op jit(solution)/shard_map/expert/pallas_call | solution.py:241
  27.6 1.8 %expert.11 = (bf16[64,2560]{1,0:T(8,128)(2,1)S(1)}, bf16[64,2560]{1,0:T(8,128)(2,1)S(1)}) custom-call(bf16[2560,768]{1,0:T(8,128)(2,1)S(1)} %collective-permute-done.refs_1_.refs_0_, bf16[2560,768]{1,0:T(8,128)(2,1)S(1)} %collective-permute-done.1.refs_1_, bf16[768,2560]{1,0:T(8,128)(2,1)S(1)} %collective-permute-done.2.refs_2_, ...), custom_call_target="tpu_custom_call" | custom-call | flops 1509949440 | bytes 1310720 | tf_op jit(solution)/shard_map/expert/pallas_call | solution.py:241
  29.4 1.8 %collective-permute-start.10 = (bf16[64,2560]{1,0:T(8,128)(2,1)S(1)}, bf16[64,2560]{1,0:T(8,128)(2,1)S(1)}, u32[]{:S(2)}, u32[]{:S(2)}) collective-permute-start(bf16[64,2560]{1,0:T(8,128)(2,1)S(1)} %get-tuple-element.32.refs_7_), channel_id=1, source_target_pairs={{0,4},{1,3},{2,6},{3,1},{4,0},{5,7},{6,2},{7,5},{8,12},{9,11},{10,... | collective-permute-start | bytes 983048 | tf_op jit(solution)/shard_map/ppermute | solution.py:35
  31.2 0.3 collective-permute-start.8
  31.5 2.0 %expert.12 = (f32[64,2560]{1,0:T(8,128)S(1)}, f32[64,2560]{1,0:T(8,128)S(1)}) custom-call(bf16[2560,768]{1,0:T(8,128)(2,1)S(1)} %collective-permute-done.refs_1_.refs_0_, bf16[2560,768]{1,0:T(8,128)(2,1)S(1)} %collective-permute-done.1.refs_1_, bf16[768,2560]{1,0:T(8,128)(2,1)S(1)} %collective-permute-done.2.refs_2_, bf16[2592,128]{1,0:T(8,128)(2,1)S(1)} %append.1.refs_3_, ...), custom_call_target="tpu_custom_call" | custom-call | flops 1509949440 | bytes 1310720 | tf_op jit(solution)/shard_map/expert/pallas_call | solution.py:241
  33.6 3.0 %collective-permute-done.10.second_ref = bf16[64,2560]{1,0:T(8,128)(2,1)S(1)} collective-permute-done((bf16[64,2560]{1,0:T(8,128)(2,1)S(1)}, bf16[64,2560]{1,0:T(8,128)(2,1)S(1)}, u32[]{:S(2)}, u32[]{:S(2)}) %collective-permute-start.10) | collective-permute-done | bytes 327712 | tf_op jit(solution)/shard_map/ppermute | solution.py:35
  36.6 0.1 sums.3
  36.6 1.8 %collective-permute-start.11 = (bf16[64,2560]{1,0:T(8,128)(2,1)S(1)}, bf16[64,2560]{1,0:T(8,128)(2,1)S(1)}, u32[]{:S(2)}, u32[]{:S(2)}) collective-permute-start(bf16[64,2560]{1,0:T(8,128)(2,1)S(1)} %sums.3), channel_id=1, source_target_pairs={{0,2},{1,5},{2,0},{3,7},{4,6},{5,1},{6,4},{7,3},{8,10},{9,13},{10,... | collective-permute-start | bytes 983048 | tf_op jit(solution)/shard_map/ppermute | solution.py:35
  38.4 2.0 %collective-permute-done.8.second_ref = bf16[64,2560]{1,0:T(8,128)(2,1)S(1)} collective-permute-done((bf16[64,2560]{1,0:T(8,128)(2,1)S(1)}, bf16[64,2560]{1,0:T(8,128)(2,1)S(1)}, u32[]{:S(2)}, u32[]{:S(2)}) %collective-permute-start.8) | collective-permute-done | bytes 327712 | tf_op jit(solution)/shard_map/ppermute | solution.py:35
  40.4 0.1 sums.2
  40.5 1.8 %collective-permute-start.9 = (bf16[64,2560]{1,0:T(8,128)(2,1)S(1)}, bf16[64,2560]{1,0:T(8,128)(2,1)S(1)}, u32[]{:S(2)}, u32[]{:S(2)}) collective-permute-start(bf16[64,2560]{1,0:T(8,128)(2,1)S(1)} %sums.2), channel_id=1, source_target_pairs={{0,2},{1,5},{2,0},{3,7},{4,6},{5,1},{6,4},{7,3},{8,10},{9,13},{10,... | collective-permute-start | bytes 983048 | tf_op jit(solution)/shard_map/ppermute | solution.py:35
  42.2 1.8 %expert.13.total_ref = f32[128,2560]{1,0:T(8,128)S(1)} custom-call(bf16[2560,768]{1,0:T(8,128)(2,1)S(1)} %collective-permute-done.refs_1_.refs_0_, bf16[2560,768]{1,0:T(8,128)(2,1)S(1)} %collective-permute-done.1.refs_1_, bf16[768,2560]{1,0:T(8,128)(2,1)S(1)} %collective-permute-done.2.refs_2_, bf16[2592,128]{1,0:T(8,128)(2,1)S(1)} %get-tuple-element.20.refs_3_, ...), custom_call_target="tpu_custom_call" | custom-call | flops 1509949440 | bytes 1310720 | tf_op jit(solution)/shard_map/expert/pallas_call | solution.py:241
  44.1 3.5 %collective-permute-done.9.upper_ref = bf16[64,2560]{1,0:T(8,128)(2,1)S(1)} collective-permute-done((bf16[64,2560]{1,0:T(8,128)(2,1)S(1)}, bf16[64,2560]{1,0:T(8,128)(2,1)S(1)}, u32[]{:S(2)}, u32[]{:S(2)}) %collective-permute-start.9) | collective-permute-done | bytes 327712 | tf_op jit(solution)/shard_map/ppermute | solution.py:35
  47.6 0.9 %finish.1 = bf16[128,2560]{1,0:T(8,128)(2,1)} custom-call(f32[128,2560]{1,0:T(8,128)S(1)} %expert.13.total_ref, bf16[64,2560]{1,0:T(8,128)(2,1)S(1)} %collective-permute-done.9.upper_ref, bf16[64,2560]{1,0:T(8,128)(2,1)S(1)} %collective-permute-done.11.lower_ref), custom_call_target="tpu_custom_call" | custom-call | bytes 1310720 | tf_op jit(solution)/shard_map/finish/pallas_call | solution.py:285
  (6 shorter events, 0.0 us)
Async XLA Ops:
  0.0 9.3 %collective-permute-start = (bf16[2560,768]{1,0:T(8,128)(2,1)}, bf16[2560,768]{1,0:T(8,128)(2,1)S(1)}, u32[]{:S(2)}, u32[]{:S(2)}) collective-permute-start(bf16[2560,768]{1,0:T(8,128)(2,1)} %bitcast.7), channel_id=1, source_target_pairs={{0,1},{1,0},{2,3},{3,2},{4,5},{5,4},{6,7},{7,6},{8,9},{9,8},{10,11... | collective-permute-start | bytes 11796488 | tf_op jit(solution)/shard_map/ppermute | solution.py:35
  0.5 12.5 %collective-permute-start.4 = (bf16[128,2560]{1,0:T(8,128)(2,1)}, bf16[128,2560]{1,0:T(8,128)(2,1)S(1)}, u32[]{:S(2)}, u32[]{:S(2)}) collective-permute-start(bf16[128,2560]{1,0:T(8,128)(2,1)} %tokens_hbm.1), channel_id=1, source_target_pairs={{0,2},{1,5},{2,0},{3,7},{4,6},{5,1},{6,4},{7,3},{8,10},{9,13},{10,... | collective-permute-start | bytes 1966088 | tf_op jit(solution)/shard_map/ppermute | solution.py:35
  2.9 17.6 %collective-permute-start.1 = (bf16[2560,768]{1,0:T(8,128)(2,1)}, bf16[2560,768]{1,0:T(8,128)(2,1)S(1)}, u32[]{:S(2)}, u32[]{:S(2)}) collective-permute-start(bf16[2560,768]{1,0:T(8,128)(2,1)} %bitcast.9), channel_id=1, source_target_pairs={{0,1},{1,0},{2,3},{3,2},{4,5},{5,4},{6,7},{7,6},{8,9},{9,8},{10,11... | collective-permute-start | bytes 11796488 | tf_op jit(solution)/shard_map/ppermute | solution.py:35
  3.2 17.3 %collective-permute-start.2 = (bf16[768,2560]{1,0:T(8,128)(2,1)}, bf16[768,2560]{1,0:T(8,128)(2,1)S(1)}, u32[]{:S(2)}, u32[]{:S(2)}) collective-permute-start(bf16[768,2560]{1,0:T(8,128)(2,1)} %bitcast.5), channel_id=1, source_target_pairs={{0,1},{1,0},{2,3},{3,2},{4,5},{5,4},{6,7},{7,6},{8,9},{9,8},{10,11... | collective-permute-start | bytes 11796488 | tf_op jit(solution)/shard_map/ppermute | solution.py:35
  7.7 11.1 %collective-permute-start.3 = (bf16[2592,128]{1,0:T(8,128)(2,1)S(1)}, bf16[2592,128]{1,0:T(8,128)(2,1)S(1)}, u32[]{:S(2)}, u32[]{:S(2)}) collective-permute-start(bf16[2592,128]{1,0:T(8,128)(2,1)S(1)} %get-tuple-element.20.refs_3_), channel_id=1, source_target_pairs={{0,4},{1,3},{2,6},{3,1},{4,0},{5,7},{6,2},{7,5},{8,12},{9,11},{10,... | collective-permute-start | bytes 1990664 | tf_op jit(solution)/shard_map/ppermute | solution.py:35
  9.3 3.8 %collective-permute-start.5 = (bf16[32,128]{1,0:T(8,128)(2,1)S(1)}, bf16[32,128]{1,0:T(8,128)(2,1)S(1)}, u32[]{:S(2)}, u32[]{:S(2)}) collective-permute-start(bf16[32,128]{1,0:T(8,128)(2,1)S(1)} %held.1.terms_ref), channel_id=1, source_target_pairs={{0,2},{1,5},{2,0},{3,7},{4,6},{5,1},{6,4},{7,3},{8,10},{9,13},{10,... | collective-permute-start | bytes 24584 | tf_op jit(solution)/shard_map/ppermute | solution.py:35
  13.2 12.7 %collective-permute-start.7 = (bf16[2592,128]{1,0:T(8,128)(2,1)S(1)}, bf16[2592,128]{1,0:T(8,128)(2,1)S(1)}, u32[]{:S(2)}, u32[]{:S(2)}) collective-permute-start(bf16[2592,128]{1,0:T(8,128)(2,1)S(1)} %append.1.refs_3_), channel_id=1, source_target_pairs={{0,4},{1,3},{2,6},{3,1},{4,0},{5,7},{6,2},{7,5},{8,12},{9,11},{10,... | collective-permute-start | bytes 1990664 | tf_op jit(solution)/shard_map/ppermute | solution.py:35
  22.3 19.9 %collective-permute-start.6 = (bf16[128,2560]{1,0:T(8,128)(2,1)S(1)}, bf16[128,2560]{1,0:T(8,128)(2,1)S(1)}, u32[]{:S(2)}, u32[]{:S(2)}) collective-permute-start(bf16[128,2560]{1,0:T(8,128)(2,1)S(1)} %expert.9.refs_4_), channel_id=1, source_target_pairs={{0,4},{1,3},{2,6},{3,1},{4,0},{5,7},{6,2},{7,5},{8,12},{9,11},{10,... | collective-permute-start | bytes 1966088 | tf_op jit(solution)/shard_map/ppermute | solution.py:35
  29.4 7.1 %collective-permute-start.10 = (bf16[64,2560]{1,0:T(8,128)(2,1)S(1)}, bf16[64,2560]{1,0:T(8,128)(2,1)S(1)}, u32[]{:S(2)}, u32[]{:S(2)}) collective-permute-start(bf16[64,2560]{1,0:T(8,128)(2,1)S(1)} %get-tuple-element.32.refs_7_), channel_id=1, source_target_pairs={{0,4},{1,3},{2,6},{3,1},{4,0},{5,7},{6,2},{7,5},{8,12},{9,11},{10,... | collective-permute-start | bytes 983048 | tf_op jit(solution)/shard_map/ppermute | solution.py:35
  31.2 9.1 %collective-permute-start.8 = (bf16[64,2560]{1,0:T(8,128)(2,1)S(1)}, bf16[64,2560]{1,0:T(8,128)(2,1)S(1)}, u32[]{:S(2)}, u32[]{:S(2)}) collective-permute-start(bf16[64,2560]{1,0:T(8,128)(2,1)S(1)} %get-tuple-element.31.refs_6_), channel_id=1, source_target_pairs={{0,4},{1,3},{2,6},{3,1},{4,0},{5,7},{6,2},{7,5},{8,12},{9,11},{10,... | collective-permute-start | bytes 983048 | tf_op jit(solution)/shard_map/ppermute | solution.py:35
  36.6 7.5 %collective-permute-start.11 = (bf16[64,2560]{1,0:T(8,128)(2,1)S(1)}, bf16[64,2560]{1,0:T(8,128)(2,1)S(1)}, u32[]{:S(2)}, u32[]{:S(2)}) collective-permute-start(bf16[64,2560]{1,0:T(8,128)(2,1)S(1)} %sums.3), channel_id=1, source_target_pairs={{0,2},{1,5},{2,0},{3,7},{4,6},{5,1},{6,4},{7,3},{8,10},{9,13},{10,... | collective-permute-start | bytes 983048 | tf_op jit(solution)/shard_map/ppermute | solution.py:35
  40.5 7.1 %collective-permute-start.9 = (bf16[64,2560]{1,0:T(8,128)(2,1)S(1)}, bf16[64,2560]{1,0:T(8,128)(2,1)S(1)}, u32[]{:S(2)}, u32[]{:S(2)}) collective-permute-start(bf16[64,2560]{1,0:T(8,128)(2,1)S(1)} %sums.2), channel_id=1, source_target_pairs={{0,2},{1,5},{2,0},{3,7},{4,6},{5,1},{6,4},{7,3},{8,10},{9,13},{10,... | collective-permute-start | bytes 983048 | tf_op jit(solution)/shard_map/ppermute | solution.py:35

commit v10 on v7

--- a/solution.py
+++ b/solution.py
@@ -8,7 +8,7 @@
 from jax.sharding import PartitionSpec as P
 
 CORE, X, Y = 1, 2, 4
-FIRST, SECOND = (X, Y), (Y, X)
+FIRST, SECOND = (Y, X), (X, Y)
 LANES = 128
 STEP = 256
 MIB = 2**20

time: 48.8 us -> 48.8 us (level)
  no operation moved by 1% of the time
where the time goes in v10:
time: 48.8 us; the launch traced here: 48.6 us
  Pallas kernels  20.7 us (42%)
  starting transfers between devices  16 us (33%)
  waiting for transfers between devices  11.6 us (24%)
    ppermute x12, starting transfers between devices, swap(): lax.ppermute(value, 'expert', [(i, i ^ offsets[i % 2]) for i in range(siz...  16 us
    pallas_call x7, Pallas kernels, run_expert(): pl.pallas_call(functools.partial(expert_kernel, experts, other, len(added...  12.8 us
    ppermute x12, waiting for transfers between devices, swap(): lax.ppermute(value, 'expert', [(i, i ^ offsets[i % 2]) for i in range(siz...  11.6 us
    pallas_call x1, Pallas kernels, own_hidden(): pl.pallas_call(functools.partial(own_hidden_kernel, experts), out_shape=[...  4.21 us
    pallas_call x1, Pallas kernels, own_answer(): pl.pallas_call(functools.partial(own_answer_kernel, experts), out_shape=[...  2.55 us
  transfers between devices with their start and end apart: 12, of which 8 were waited for; matrix products, arithmetic and copies ran while one was open for 0% of the time, Pallas kernels for 41%

profile of v10, /device:TPU:0, one launch (start us, length us, event | category | flops | bytes accessed | tf_op | source)
XLA Modules:
  0.0 48.6 jit_solution(2315309776072402937)
XLA Ops:
  0.0 0.5 collective-permute-start
  0.5 2.5 %collective-permute-start.4 = (bf16[128,2560]{1,0:T(8,128)(2,1)}, bf16[128,2560]{1,0:T(8,128)(2,1)S(1)}, u32[]{:S(2)}, u32[]{:S(2)}) collective-permute-start(bf16[128,2560]{1,0:T(8,128)(2,1)} %tokens_hbm.1), channel_id=1, source_target_pairs={{0,4},{1,3},{2,6},{3,1},{4,0},{5,7},{6,2},{7,5},{8,12},{9,11},{10,... | collective-permute-start | bytes 1966088 | tf_op jit(solution)/shard_map/ppermute | solution.py:35
  3.0 0.2 collective-permute-start.1
  3.2 0.3 collective-permute-start.2
  3.5 4.2 %own_hidden.1 = (bf16[2592,128]{1,0:T(8,128)(2,1)S(1)}, bf16[32,128]{1,0:T(8,128)(2,1)S(1)}, bf16[128,768]{1,0:T(8,128)(2,1)S(1)}, bf16[2560,768]{1,0:T(8,128)(2,1)S(1)}, bf16[2560,768]{1,0:T(8,128)(2,1)S(1)}) custom-call(bf16[128,2560]{1,0:T(8,128)(2,1)} %tokens_hbm.1, s32[6,128]{1,0:T(8,128)} %bitcast.11, f32[6,128]{1,0:T(8,128)} %bitcast.12, ...), custom_call_target="tpu_custom_call" | custom-call | flops 54358179840 | bytes 47185920 | tf_op jit(solution)/shard_map/own_hidden/pallas_call | solution.py:119
  7.7 1.5 %collective-permute-start.3 = (bf16[2592,128]{1,0:T(8,128)(2,1)S(1)}, bf16[2592,128]{1,0:T(8,128)(2,1)S(1)}, u32[]{:S(2)}, u32[]{:S(2)}) collective-permute-start(bf16[2592,128]{1,0:T(8,128)(2,1)S(1)} %get-tuple-element.20.refs_3_), channel_id=1, source_target_pairs={{0,2},{1,5},{2,0},{3,7},{4,6},{5,1},{6,4},{7,3},{8,10},{9,13},{10,... | collective-permute-start | bytes 1990664 | tf_op jit(solution)/shard_map/ppermute | solution.py:35
  9.3 0.7 %collective-permute-start.5 = (bf16[32,128]{1,0:T(8,128)(2,1)S(1)}, bf16[32,128]{1,0:T(8,128)(2,1)S(1)}, u32[]{:S(2)}, u32[]{:S(2)}) collective-permute-start(bf16[32,128]{1,0:T(8,128)(2,1)S(1)} %held.1.terms_ref), channel_id=1, source_target_pairs={{0,4},{1,3},{2,6},{3,1},{4,0},{5,7},{6,2},{7,5},{8,12},{9,11},{10,... | collective-permute-start | bytes 24584 | tf_op jit(solution)/shard_map/ppermute | solution.py:35
  10.0 2.5 %own_answer.1 = (f32[128,2560]{1,0:T(8,128)S(1)}, bf16[768,2560]{1,0:T(8,128)(2,1)S(1)}) custom-call(bf16[128,768]{1,0:T(8,128)(2,1)S(1)} %get-tuple-element.21.hidden_ref, bf16[32,128]{1,0:T(8,128)(2,1)S(1)} %held.1.terms_ref, bf16[768,2560]{1,0:T(8,128)(2,1)} %bitcast.6), custom_call_target="tpu_custom_call" | custom-call | flops 503316480 | bytes 1310720 | tf_op jit(solution)/shard_map/own_answer/pallas_call | solution.py:161
  12.5 0.5 %collective-permute-done.4.rows_ref = bf16[128,2560]{1,0:T(8,128)(2,1)S(1)} collective-permute-done((bf16[128,2560]{1,0:T(8,128)(2,1)}, bf16[128,2560]{1,0:T(8,128)(2,1)S(1)}, u32[]{:S(2)}, u32[]{:S(2)}) %collective-permute-start.4) | collective-permute-done | bytes 655392 | tf_op jit(solution)/shard_map/ppermute | solution.py:35
  13.0 0.1 collective-permute-done.5.terms_ref
  13.1 0.1 append.1.refs_3_
  13.2 2.7 %collective-permute-start.7 = (bf16[2592,128]{1,0:T(8,128)(2,1)S(1)}, bf16[2592,128]{1,0:T(8,128)(2,1)S(1)}, u32[]{:S(2)}, u32[]{:S(2)}) collective-permute-start(bf16[2592,128]{1,0:T(8,128)(2,1)S(1)} %append.1.refs_3_), channel_id=1, source_target_pairs={{0,2},{1,5},{2,0},{3,7},{4,6},{5,1},{6,4},{7,3},{8,10},{9,13},{10,... | collective-permute-start | bytes 1990664 | tf_op jit(solution)/shard_map/ppermute | solution.py:35
  15.9 1.8 %expert.7 = (f32[64,2560]{1,0:T(8,128)S(1)}, f32[64,2560]{1,0:T(8,128)S(1)}) custom-call(bf16[2560,768]{1,0:T(8,128)(2,1)S(1)} %get-tuple-element.24.refs_0_, bf16[2560,768]{1,0:T(8,128)(2,1)S(1)} %get-tuple-element.25.refs_1_, bf16[768,2560]{1,0:T(8,128)(2,1)S(1)} %get-tuple-element.26.refs_2_, bf16[2592,128]{1,0:T(8,128)(2,1)S(1)} %append.1.refs_3_, ...), custom_call_target="tpu_custom_call" | custom-call | flops 1509949440 | bytes 1310720 | tf_op jit(solution)/shard_map/expert/pallas_call | solution.py:241
  17.7 1.0 %collective-permute-done.3.refs_3_ = bf16[2592,128]{1,0:T(8,128)(2,1)S(1)} collective-permute-done((bf16[2592,128]{1,0:T(8,128)(2,1)S(1)}, bf16[2592,128]{1,0:T(8,128)(2,1)S(1)}, u32[]{:S(2)}, u32[]{:S(2)}) %collective-permute-start.3) | collective-permute-done | bytes 663584 | tf_op jit(solution)/shard_map/ppermute | solution.py:35
  18.7 1.8 %expert.8.refs_4_ = f32[128,2560]{1,0:T(8,128)S(1)} custom-call(bf16[2560,768]{1,0:T(8,128)(2,1)S(1)} %get-tuple-element.24.refs_0_, bf16[2560,768]{1,0:T(8,128)(2,1)S(1)} %get-tuple-element.25.refs_1_, bf16[768,2560]{1,0:T(8,128)(2,1)S(1)} %get-tuple-element.26.refs_2_, bf16[2592,128]{1,0:T(8,128)(2,1)S(1)} %collective-permute-done.3.refs_3_, ...), custom_call_target="tpu_custom_call" | custom-call | flops 1509949440 | bytes 1310720 | tf_op jit(solution)/shard_map/expert/pallas_call | solution.py:241
  20.5 1.8 %expert.9.refs_4_ = bf16[128,2560]{1,0:T(8,128)(2,1)S(1)} custom-call(bf16[2560,768]{1,0:T(8,128)(2,1)S(1)} %collective-permute-done.refs_1_.refs_0_, bf16[2560,768]{1,0:T(8,128)(2,1)S(1)} %collective-permute-done.1.refs_1_, bf16[768,2560]{1,0:T(8,128)(2,1)S(1)} %collective-permute-done.2.refs_2_, bf16[2592,128]{1,0:T(8,128)(2,1)S(1)} %collective-permute-done.3.refs_3_, ...), custom_call_target="tpu_custom_call" | custom-call | flops 1509949440 | bytes 1310720 | tf_op jit(solution)/shard_map/expert/pallas_call | solution.py:241
  22.3 1.8 %collective-permute-start.6 = (bf16[128,2560]{1,0:T(8,128)(2,1)S(1)}, bf16[128,2560]{1,0:T(8,128)(2,1)S(1)}, u32[]{:S(2)}, u32[]{:S(2)}) collective-permute-start(bf16[128,2560]{1,0:T(8,128)(2,1)S(1)} %expert.9.refs_4_), channel_id=1, source_target_pairs={{0,2},{1,5},{2,0},{3,7},{4,6},{5,1},{6,4},{7,3},{8,10},{9,13},{10,... | collective-permute-start | bytes 1966088 | tf_op jit(solution)/shard_map/ppermute | solution.py:35
  24.1 1.7 %collective-permute-done.7.refs_3_ = bf16[2592,128]{1,0:T(8,128)(2,1)S(1)} collective-permute-done((bf16[2592,128]{1,0:T(8,128)(2,1)S(1)}, bf16[2592,128]{1,0:T(8,128)(2,1)S(1)}, u32[]{:S(2)}, u32[]{:S(2)}) %collective-permute-start.7) | collective-permute-done | bytes 663584 | tf_op jit(solution)/shard_map/ppermute | solution.py:35
  25.8 1.8 %expert.10 = (f32[64,2560]{1,0:T(8,128)S(1)}, f32[64,2560]{1,0:T(8,128)S(1)}) custom-call(bf16[2560,768]{1,0:T(8,128)(2,1)S(1)} %get-tuple-element.24.refs_0_, bf16[2560,768]{1,0:T(8,128)(2,1)S(1)} %get-tuple-element.25.refs_1_, bf16[768,2560]{1,0:T(8,128)(2,1)S(1)} %get-tuple-element.26.refs_2_, bf16[2592,128]{1,0:T(8,128)(2,1)S(1)} %collective-permute-done.7.refs_3_, ...), custom_call_target="tpu_custom_call" | custom-call | flops 1509949440 | bytes 1310720 | tf_op jit(solution)/shard_map/expert/pallas_call | solution.py:241
  27.6 1.8 %expert.11 = (bf16[64,2560]{1,0:T(8,128)(2,1)S(1)}, bf16[64,2560]{1,0:T(8,128)(2,1)S(1)}) custom-call(bf16[2560,768]{1,0:T(8,128)(2,1)S(1)} %collective-permute-done.refs_1_.refs_0_, bf16[2560,768]{1,0:T(8,128)(2,1)S(1)} %collective-permute-done.1.refs_1_, bf16[768,2560]{1,0:T(8,128)(2,1)S(1)} %collective-permute-done.2.refs_2_, ...), custom_call_target="tpu_custom_call" | custom-call | flops 1509949440 | bytes 1310720 | tf_op jit(solution)/shard_map/expert/pallas_call | solution.py:241
  29.4 1.8 %collective-permute-start.10 = (bf16[64,2560]{1,0:T(8,128)(2,1)S(1)}, bf16[64,2560]{1,0:T(8,128)(2,1)S(1)}, u32[]{:S(2)}, u32[]{:S(2)}) collective-permute-start(bf16[64,2560]{1,0:T(8,128)(2,1)S(1)} %get-tuple-element.32.refs_7_), channel_id=1, source_target_pairs={{0,2},{1,5},{2,0},{3,7},{4,6},{5,1},{6,4},{7,3},{8,10},{9,13},{10,... | collective-permute-start | bytes 983048 | tf_op jit(solution)/shard_map/ppermute | solution.py:35
  31.2 0.3 collective-permute-start.8
  31.5 2.0 %expert.12 = (f32[64,2560]{1,0:T(8,128)S(1)}, f32[64,2560]{1,0:T(8,128)S(1)}) custom-call(bf16[2560,768]{1,0:T(8,128)(2,1)S(1)} %collective-permute-done.refs_1_.refs_0_, bf16[2560,768]{1,0:T(8,128)(2,1)S(1)} %collective-permute-done.1.refs_1_, bf16[768,2560]{1,0:T(8,128)(2,1)S(1)} %collective-permute-done.2.refs_2_, bf16[2592,128]{1,0:T(8,128)(2,1)S(1)} %append.1.refs_3_, ...), custom_call_target="tpu_custom_call" | custom-call | flops 1509949440 | bytes 1310720 | tf_op jit(solution)/shard_map/expert/pallas_call | solution.py:241
  33.6 1.9 %expert.13.refs_0_.total_ref = f32[128,2560]{1,0:T(8,128)S(1)} custom-call(bf16[2560,768]{1,0:T(8,128)(2,1)S(1)} %collective-permute-done.refs_1_.refs_0_, bf16[2560,768]{1,0:T(8,128)(2,1)S(1)} %collective-permute-done.1.refs_1_, bf16[768,2560]{1,0:T(8,128)(2,1)S(1)} %collective-permute-done.2.refs_2_, bf16[2592,128]{1,0:T(8,128)(2,1)S(1)} %get-tuple-element.20.refs_3_, ...), custom_call_target="tpu_custom_call" | custom-call | flops 1509949440 | bytes 1310720 | tf_op jit(solution)/shard_map/expert/pallas_call | solution.py:241
  35.4 1.1 %collective-permute-done.10.second_ref = bf16[64,2560]{1,0:T(8,128)(2,1)S(1)} collective-permute-done((bf16[64,2560]{1,0:T(8,128)(2,1)S(1)}, bf16[64,2560]{1,0:T(8,128)(2,1)S(1)}, u32[]{:S(2)}, u32[]{:S(2)}) %collective-permute-start.10) | collective-permute-done | bytes 327712 | tf_op jit(solution)/shard_map/ppermute | solution.py:35
  36.5 0.1 sums.3
  36.6 1.8 %collective-permute-start.11 = (bf16[64,2560]{1,0:T(8,128)(2,1)S(1)}, bf16[64,2560]{1,0:T(8,128)(2,1)S(1)}, u32[]{:S(2)}, u32[]{:S(2)}) collective-permute-start(bf16[64,2560]{1,0:T(8,128)(2,1)S(1)} %sums.3), channel_id=1, source_target_pairs={{0,4},{1,3},{2,6},{3,1},{4,0},{5,7},{6,2},{7,5},{8,12},{9,11},{10,... | collective-permute-start | bytes 983048 | tf_op jit(solution)/shard_map/ppermute | solution.py:35
  38.4 1.9 %collective-permute-done.8.second_ref = bf16[64,2560]{1,0:T(8,128)(2,1)S(1)} collective-permute-done((bf16[64,2560]{1,0:T(8,128)(2,1)S(1)}, bf16[64,2560]{1,0:T(8,128)(2,1)S(1)}, u32[]{:S(2)}, u32[]{:S(2)}) %collective-permute-start.8) | collective-permute-done | bytes 327712 | tf_op jit(solution)/shard_map/ppermute | solution.py:35
  40.4 1.8 %collective-permute-start.9 = (bf16[64,2560]{1,0:T(8,128)(2,1)S(1)}, bf16[64,2560]{1,0:T(8,128)(2,1)S(1)}, u32[]{:S(2)}, u32[]{:S(2)}) collective-permute-start(bf16[64,2560]{1,0:T(8,128)(2,1)S(1)} %sums.2), channel_id=1, source_target_pairs={{0,4},{1,3},{2,6},{3,1},{4,0},{5,7},{6,2},{7,5},{8,12},{9,11},{10,... | collective-permute-start | bytes 983048 | tf_op jit(solution)/shard_map/ppermute | solution.py:35
  42.3 1.5 %collective-permute-done.11.lower_ref = bf16[64,2560]{1,0:T(8,128)(2,1)S(1)} collective-permute-done((bf16[64,2560]{1,0:T(8,128)(2,1)S(1)}, bf16[64,2560]{1,0:T(8,128)(2,1)S(1)}, u32[]{:S(2)}, u32[]{:S(2)}) %collective-permute-start.11) | collective-permute-done | bytes 327712 | tf_op jit(solution)/shard_map/ppermute | solution.py:35
  43.7 3.8 %collective-permute-done.9.upper_ref = bf16[64,2560]{1,0:T(8,128)(2,1)S(1)} collective-permute-done((bf16[64,2560]{1,0:T(8,128)(2,1)S(1)}, bf16[64,2560]{1,0:T(8,128)(2,1)S(1)}, u32[]{:S(2)}, u32[]{:S(2)}) %collective-permute-start.9) | collective-permute-done | bytes 327712 | tf_op jit(solution)/shard_map/ppermute | solution.py:35
  47.6 0.9 %finish.1 = bf16[128,2560]{1,0:T(8,128)(2,1)} custom-call(f32[128,2560]{1,0:T(8,128)S(1)} %expert.13.refs_0_.total_ref, bf16[64,2560]{1,0:T(8,128)(2,1)S(1)} %collective-permute-done.9.upper_ref, bf16[64,2560]{1,0:T(8,128)(2,1)S(1)} %collective-permute-done.11.lower_ref), custom_call_target="tpu_custom_call" | custom-call | bytes 1310720 | tf_op jit(solution)/shard_map/finish/pallas_call | solution.py:285
  (6 shorter events, 0.1 us)
Async XLA Ops:
  0.0 9.3 %collective-permute-start = (bf16[2560,768]{1,0:T(8,128)(2,1)}, bf16[2560,768]{1,0:T(8,128)(2,1)S(1)}, u32[]{:S(2)}, u32[]{:S(2)}) collective-permute-start(bf16[2560,768]{1,0:T(8,128)(2,1)} %bitcast.7), channel_id=1, source_target_pairs={{0,1},{1,0},{2,3},{3,2},{4,5},{5,4},{6,7},{7,6},{8,9},{9,8},{10,11... | collective-permute-start | bytes 11796488 | tf_op jit(solution)/shard_map/ppermute | solution.py:35
  0.5 12.6 %collective-permute-start.4 = (bf16[128,2560]{1,0:T(8,128)(2,1)}, bf16[128,2560]{1,0:T(8,128)(2,1)S(1)}, u32[]{:S(2)}, u32[]{:S(2)}) collective-permute-start(bf16[128,2560]{1,0:T(8,128)(2,1)} %tokens_hbm.1), channel_id=1, source_target_pairs={{0,4},{1,3},{2,6},{3,1},{4,0},{5,7},{6,2},{7,5},{8,12},{9,11},{10,... | collective-permute-start | bytes 1966088 | tf_op jit(solution)/shard_map/ppermute | solution.py:35
  3.0 17.5 %collective-permute-start.1 = (bf16[2560,768]{1,0:T(8,128)(2,1)}, bf16[2560,768]{1,0:T(8,128)(2,1)S(1)}, u32[]{:S(2)}, u32[]{:S(2)}) collective-permute-start(bf16[2560,768]{1,0:T(8,128)(2,1)} %bitcast.9), channel_id=1, source_target_pairs={{0,1},{1,0},{2,3},{3,2},{4,5},{5,4},{6,7},{7,6},{8,9},{9,8},{10,11... | collective-permute-start | bytes 11796488 | tf_op jit(solution)/shard_map/ppermute | solution.py:35
  3.2 17.3 %collective-permute-start.2 = (bf16[768,2560]{1,0:T(8,128)(2,1)}, bf16[768,2560]{1,0:T(8,128)(2,1)S(1)}, u32[]{:S(2)}, u32[]{:S(2)}) collective-permute-start(bf16[768,2560]{1,0:T(8,128)(2,1)} %bitcast.5), channel_id=1, source_target_pairs={{0,1},{1,0},{2,3},{3,2},{4,5},{5,4},{6,7},{7,6},{8,9},{9,8},{10,11... | collective-permute-start | bytes 11796488 | tf_op jit(solution)/shard_map/ppermute | solution.py:35
  7.7 11.0 %collective-permute-start.3 = (bf16[2592,128]{1,0:T(8,128)(2,1)S(1)}, bf16[2592,128]{1,0:T(8,128)(2,1)S(1)}, u32[]{:S(2)}, u32[]{:S(2)}) collective-permute-start(bf16[2592,128]{1,0:T(8,128)(2,1)S(1)} %get-tuple-element.20.refs_3_), channel_id=1, source_target_pairs={{0,2},{1,5},{2,0},{3,7},{4,6},{5,1},{6,4},{7,3},{8,10},{9,13},{10,... | collective-permute-start | bytes 1990664 | tf_op jit(solution)/shard_map/ppermute | solution.py:35
  9.3 3.8 %collective-permute-start.5 = (bf16[32,128]{1,0:T(8,128)(2,1)S(1)}, bf16[32,128]{1,0:T(8,128)(2,1)S(1)}, u32[]{:S(2)}, u32[]{:S(2)}) collective-permute-start(bf16[32,128]{1,0:T(8,128)(2,1)S(1)} %held.1.terms_ref), channel_id=1, source_target_pairs={{0,4},{1,3},{2,6},{3,1},{4,0},{5,7},{6,2},{7,5},{8,12},{9,11},{10,... | collective-permute-start | bytes 24584 | tf_op jit(solution)/shard_map/ppermute | solution.py:35
  13.2 12.7 %collective-permute-start.7 = (bf16[2592,128]{1,0:T(8,128)(2,1)S(1)}, bf16[2592,128]{1,0:T(8,128)(2,1)S(1)}, u32[]{:S(2)}, u32[]{:S(2)}) collective-permute-start(bf16[2592,128]{1,0:T(8,128)(2,1)S(1)} %append.1.refs_3_), channel_id=1, source_target_pairs={{0,2},{1,5},{2,0},{3,7},{4,6},{5,1},{6,4},{7,3},{8,10},{9,13},{10,... | collective-permute-start | bytes 1990664 | tf_op jit(solution)/shard_map/ppermute | solution.py:35
  22.3 11.2 %collective-permute-start.6 = (bf16[128,2560]{1,0:T(8,128)(2,1)S(1)}, bf16[128,2560]{1,0:T(8,128)(2,1)S(1)}, u32[]{:S(2)}, u32[]{:S(2)}) collective-permute-start(bf16[128,2560]{1,0:T(8,128)(2,1)S(1)} %expert.9.refs_4_), channel_id=1, source_target_pairs={{0,2},{1,5},{2,0},{3,7},{4,6},{5,1},{6,4},{7,3},{8,10},{9,13},{10,... | collective-permute-start | bytes 1966088 | tf_op jit(solution)/shard_map/ppermute | solution.py:35
  29.4 7.1 %collective-permute-start.10 = (bf16[64,2560]{1,0:T(8,128)(2,1)S(1)}, bf16[64,2560]{1,0:T(8,128)(2,1)S(1)}, u32[]{:S(2)}, u32[]{:S(2)}) collective-permute-start(bf16[64,2560]{1,0:T(8,128)(2,1)S(1)} %get-tuple-element.32.refs_7_), channel_id=1, source_target_pairs={{0,2},{1,5},{2,0},{3,7},{4,6},{5,1},{6,4},{7,3},{8,10},{9,13},{10,... | collective-permute-start | bytes 983048 | tf_op jit(solution)/shard_map/ppermute | solution.py:35
  31.2 9.2 %collective-permute-start.8 = (bf16[64,2560]{1,0:T(8,128)(2,1)S(1)}, bf16[64,2560]{1,0:T(8,128)(2,1)S(1)}, u32[]{:S(2)}, u32[]{:S(2)}) collective-permute-start(bf16[64,2560]{1,0:T(8,128)(2,1)S(1)} %get-tuple-element.31.refs_6_), channel_id=1, source_target_pairs={{0,2},{1,5},{2,0},{3,7},{4,6},{5,1},{6,4},{7,3},{8,10},{9,13},{10,... | collective-permute-start | bytes 983048 | tf_op jit(solution)/shard_map/ppermute | solution.py:35
  36.6 7.1 %collective-permute-start.11 = (bf16[64,2560]{1,0:T(8,128)(2,1)S(1)}, bf16[64,2560]{1,0:T(8,128)(2,1)S(1)}, u32[]{:S(2)}, u32[]{:S(2)}) collective-permute-start(bf16[64,2560]{1,0:T(8,128)(2,1)S(1)} %sums.3), channel_id=1, source_target_pairs={{0,4},{1,3},{2,6},{3,1},{4,0},{5,7},{6,2},{7,5},{8,12},{9,11},{10,... | collective-permute-start | bytes 983048 | tf_op jit(solution)/shard_map/ppermute | solution.py:35
  40.4 7.1 %collective-permute-start.9 = (bf16[64,2560]{1,0:T(8,128)(2,1)S(1)}, bf16[64,2560]{1,0:T(8,128)(2,1)S(1)}, u32[]{:S(2)}, u32[]{:S(2)}) collective-permute-start(bf16[64,2560]{1,0:T(8,128)(2,1)S(1)} %sums.2), channel_id=1, source_target_pairs={{0,4},{1,3},{2,6},{3,1},{4,0},{5,7},{6,2},{7,5},{8,12},{9,11},{10,... | collective-permute-start | bytes 983048 | tf_op jit(solution)/shard_map/ppermute | solution.py:35

commit v11 on v9

--- a/solution.py
+++ b/solution.py
@@ -8,7 +8,7 @@
 from jax.sharding import PartitionSpec as P
 
 CORE, X, Y = 1, 2, 4
-FIRST, SECOND = (X, Y), (Y, X)
+FIRST, SECOND = (Y, X), (X, Y)
 LANES = 128
 STEP = 256
 MIB = 2**20

time: 48.8 us -> 48.8 us (level)
  no operation moved by 1% of the time
where the time goes in v11:
time: 48.8 us; the launch traced here: 48.6 us
  Pallas kernels  20.7 us (42%)
  starting transfers between devices  16 us (33%)
  waiting for transfers between devices  11.7 us (24%)
    ppermute x12, starting transfers between devices, swap(): lax.ppermute(value, 'expert', [(i, i ^ offsets[i % 2]) for i in range(siz...  16 us
    pallas_call x7, Pallas kernels, run_expert(): pl.pallas_call(functools.partial(expert_kernel, experts, other, len(added...  12.8 us
    ppermute x12, waiting for transfers between devices, swap(): lax.ppermute(value, 'expert', [(i, i ^ offsets[i % 2]) for i in range(siz...  11.7 us
    pallas_call x1, Pallas kernels, own_hidden(): pl.pallas_call(functools.partial(own_hidden_kernel, experts), out_shape=[...  4.21 us
    pallas_call x1, Pallas kernels, own_answer(): pl.pallas_call(functools.partial(own_answer_kernel, experts), out_shape=[...  2.55 us
  transfers between devices with their start and end apart: 12, of which 7 were waited for; matrix products, arithmetic and copies ran while one was open for 0% of the time, Pallas kernels for 41%

profile of v11, /device:TPU:0, one launch (start us, length us, event | category | flops | bytes accessed | tf_op | source)
XLA Modules:
  0.0 48.6 jit_solution(2904501723928925191)
XLA Ops:
  0.0 0.5 collective-permute-start
  0.5 2.5 %collective-permute-start.4 = (bf16[128,2560]{1,0:T(8,128)(2,1)}, bf16[128,2560]{1,0:T(8,128)(2,1)S(1)}, u32[]{:S(2)}, u32[]{:S(2)}) collective-permute-start(bf16[128,2560]{1,0:T(8,128)(2,1)} %tokens_hbm.1), channel_id=1, source_target_pairs={{0,4},{1,3},{2,6},{3,1},{4,0},{5,7},{6,2},{7,5},{8,12},{9,11},{10,... | collective-permute-start | bytes 1966088 | tf_op jit(solution)/shard_map/ppermute | solution.py:35
  3.0 0.2 collective-permute-start.1
  3.2 0.3 collective-permute-start.2
  3.5 4.2 %own_hidden.1 = (bf16[2592,128]{1,0:T(8,128)(2,1)S(1)}, bf16[32,128]{1,0:T(8,128)(2,1)S(1)}, bf16[128,768]{1,0:T(8,128)(2,1)S(1)}, bf16[2560,768]{1,0:T(8,128)(2,1)S(1)}, bf16[2560,768]{1,0:T(8,128)(2,1)S(1)}) custom-call(bf16[128,2560]{1,0:T(8,128)(2,1)} %tokens_hbm.1, s32[6,128]{1,0:T(8,128)} %bitcast.11, f32[6,128]{1,0:T(8,128)} %bitcast.12, ...), custom_call_target="tpu_custom_call" | custom-call | flops 54358179840 | bytes 47185920 | tf_op jit(solution)/shard_map/own_hidden/pallas_call | solution.py:119
  7.7 1.5 %collective-permute-start.3 = (bf16[2592,128]{1,0:T(8,128)(2,1)S(1)}, bf16[2592,128]{1,0:T(8,128)(2,1)S(1)}, u32[]{:S(2)}, u32[]{:S(2)}) collective-permute-start(bf16[2592,128]{1,0:T(8,128)(2,1)S(1)} %get-tuple-element.20.refs_3_), channel_id=1, source_target_pairs={{0,2},{1,5},{2,0},{3,7},{4,6},{5,1},{6,4},{7,3},{8,10},{9,13},{10,... | collective-permute-start | bytes 1990664 | tf_op jit(solution)/shard_map/ppermute | solution.py:35
  9.3 0.7 %collective-permute-start.5 = (bf16[32,128]{1,0:T(8,128)(2,1)S(1)}, bf16[32,128]{1,0:T(8,128)(2,1)S(1)}, u32[]{:S(2)}, u32[]{:S(2)}) collective-permute-start(bf16[32,128]{1,0:T(8,128)(2,1)S(1)} %held.1.terms_ref), channel_id=1, source_target_pairs={{0,4},{1,3},{2,6},{3,1},{4,0},{5,7},{6,2},{7,5},{8,12},{9,11},{10,... | collective-permute-start | bytes 24584 | tf_op jit(solution)/shard_map/ppermute | solution.py:35
  10.0 2.5 %own_answer.1 = (f32[128,2560]{1,0:T(8,128)S(1)}, bf16[768,2560]{1,0:T(8,128)(2,1)S(1)}) custom-call(bf16[128,768]{1,0:T(8,128)(2,1)S(1)} %get-tuple-element.21.hidden_ref, bf16[32,128]{1,0:T(8,128)(2,1)S(1)} %held.1.terms_ref, bf16[768,2560]{1,0:T(8,128)(2,1)} %bitcast.6), custom_call_target="tpu_custom_call" | custom-call | flops 503316480 | bytes 1310720 | tf_op jit(solution)/shard_map/own_answer/pallas_call | solution.py:161
  12.5 0.5 %collective-permute-done.4.rows_ref = bf16[128,2560]{1,0:T(8,128)(2,1)S(1)} collective-permute-done((bf16[128,2560]{1,0:T(8,128)(2,1)}, bf16[128,2560]{1,0:T(8,128)(2,1)S(1)}, u32[]{:S(2)}, u32[]{:S(2)}) %collective-permute-start.4) | collective-permute-done | bytes 655392 | tf_op jit(solution)/shard_map/ppermute | solution.py:35
  13.0 0.1 collective-permute-done.5.terms_ref
  13.1 0.1 append.1.refs_3_
  13.2 2.7 %collective-permute-start.7 = (bf16[2592,128]{1,0:T(8,128)(2,1)S(1)}, bf16[2592,128]{1,0:T(8,128)(2,1)S(1)}, u32[]{:S(2)}, u32[]{:S(2)}) collective-permute-start(bf16[2592,128]{1,0:T(8,128)(2,1)S(1)} %append.1.refs_3_), channel_id=1, source_target_pairs={{0,2},{1,5},{2,0},{3,7},{4,6},{5,1},{6,4},{7,3},{8,10},{9,13},{10,... | collective-permute-start | bytes 1990664 | tf_op jit(solution)/shard_map/ppermute | solution.py:35
  15.9 1.8 %expert.7 = (f32[64,2560]{1,0:T(8,128)S(1)}, f32[64,2560]{1,0:T(8,128)S(1)}) custom-call(bf16[2560,768]{1,0:T(8,128)(2,1)S(1)} %get-tuple-element.24.refs_0_, bf16[2560,768]{1,0:T(8,128)(2,1)S(1)} %get-tuple-element.25.refs_1_, bf16[768,2560]{1,0:T(8,128)(2,1)S(1)} %get-tuple-element.26.refs_2_, bf16[2592,128]{1,0:T(8,128)(2,1)S(1)} %append.1.refs_3_, ...), custom_call_target="tpu_custom_call" | custom-call | flops 1509949440 | bytes 1310720 | tf_op jit(solution)/shard_map/expert/pallas_call | solution.py:241
  17.7 1.0 %collective-permute-done.3.refs_3_ = bf16[2592,128]{1,0:T(8,128)(2,1)S(1)} collective-permute-done((bf16[2592,128]{1,0:T(8,128)(2,1)S(1)}, bf16[2592,128]{1,0:T(8,128)(2,1)S(1)}, u32[]{:S(2)}, u32[]{:S(2)}) %collective-permute-start.3) | collective-permute-done | bytes 663584 | tf_op jit(solution)/shard_map/ppermute | solution.py:35
  18.7 1.8 %expert.8.refs_4_ = f32[128,2560]{1,0:T(8,128)S(1)} custom-call(bf16[2560,768]{1,0:T(8,128)(2,1)S(1)} %get-tuple-element.24.refs_0_, bf16[2560,768]{1,0:T(8,128)(2,1)S(1)} %get-tuple-element.25.refs_1_, bf16[768,2560]{1,0:T(8,128)(2,1)S(1)} %get-tuple-element.26.refs_2_, bf16[2592,128]{1,0:T(8,128)(2,1)S(1)} %collective-permute-done.3.refs_3_, ...), custom_call_target="tpu_custom_call" | custom-call | flops 1509949440 | bytes 1310720 | tf_op jit(solution)/shard_map/expert/pallas_call | solution.py:241
  20.5 1.8 %expert.9.refs_4_ = bf16[128,2560]{1,0:T(8,128)(2,1)S(1)} custom-call(bf16[2560,768]{1,0:T(8,128)(2,1)S(1)} %collective-permute-done.refs_1_.refs_0_, bf16[2560,768]{1,0:T(8,128)(2,1)S(1)} %collective-permute-done.1.refs_1_, bf16[768,2560]{1,0:T(8,128)(2,1)S(1)} %collective-permute-done.2.refs_2_, bf16[2592,128]{1,0:T(8,128)(2,1)S(1)} %collective-permute-done.3.refs_3_, ...), custom_call_target="tpu_custom_call" | custom-call | flops 1509949440 | bytes 1310720 | tf_op jit(solution)/shard_map/expert/pallas_call | solution.py:241
  22.3 1.8 %collective-permute-start.6 = (bf16[128,2560]{1,0:T(8,128)(2,1)S(1)}, bf16[128,2560]{1,0:T(8,128)(2,1)S(1)}, u32[]{:S(2)}, u32[]{:S(2)}) collective-permute-start(bf16[128,2560]{1,0:T(8,128)(2,1)S(1)} %expert.9.refs_4_), channel_id=1, source_target_pairs={{0,2},{1,5},{2,0},{3,7},{4,6},{5,1},{6,4},{7,3},{8,10},{9,13},{10,... | collective-permute-start | bytes 1966088 | tf_op jit(solution)/shard_map/ppermute | solution.py:35
  24.1 1.7 %collective-permute-done.7.refs_3_ = bf16[2592,128]{1,0:T(8,128)(2,1)S(1)} collective-permute-done((bf16[2592,128]{1,0:T(8,128)(2,1)S(1)}, bf16[2592,128]{1,0:T(8,128)(2,1)S(1)}, u32[]{:S(2)}, u32[]{:S(2)}) %collective-permute-start.7) | collective-permute-done | bytes 663584 | tf_op jit(solution)/shard_map/ppermute | solution.py:35
  25.8 1.8 %expert.10 = (f32[64,2560]{1,0:T(8,128)S(1)}, f32[64,2560]{1,0:T(8,128)S(1)}) custom-call(bf16[2560,768]{1,0:T(8,128)(2,1)S(1)} %get-tuple-element.24.refs_0_, bf16[2560,768]{1,0:T(8,128)(2,1)S(1)} %get-tuple-element.25.refs_1_, bf16[768,2560]{1,0:T(8,128)(2,1)S(1)} %get-tuple-element.26.refs_2_, bf16[2592,128]{1,0:T(8,128)(2,1)S(1)} %collective-permute-done.7.refs_3_, ...), custom_call_target="tpu_custom_call" | custom-call | flops 1509949440 | bytes 1310720 | tf_op jit(solution)/shard_map/expert/pallas_call | solution.py:241
  27.6 1.8 %expert.11 = (bf16[64,2560]{1,0:T(8,128)(2,1)S(1)}, bf16[64,2560]{1,0:T(8,128)(2,1)S(1)}) custom-call(bf16[2560,768]{1,0:T(8,128)(2,1)S(1)} %collective-permute-done.refs_1_.refs_0_, bf16[2560,768]{1,0:T(8,128)(2,1)S(1)} %collective-permute-done.1.refs_1_, bf16[768,2560]{1,0:T(8,128)(2,1)S(1)} %collective-permute-done.2.refs_2_, ...), custom_call_target="tpu_custom_call" | custom-call | flops 1509949440 | bytes 1310720 | tf_op jit(solution)/shard_map/expert/pallas_call | solution.py:241
  29.4 1.8 %collective-permute-start.10 = (bf16[64,2560]{1,0:T(8,128)(2,1)S(1)}, bf16[64,2560]{1,0:T(8,128)(2,1)S(1)}, u32[]{:S(2)}, u32[]{:S(2)}) collective-permute-start(bf16[64,2560]{1,0:T(8,128)(2,1)S(1)} %get-tuple-element.32.refs_7_), channel_id=1, source_target_pairs={{0,2},{1,5},{2,0},{3,7},{4,6},{5,1},{6,4},{7,3},{8,10},{9,13},{10,... | collective-permute-start | bytes 983048 | tf_op jit(solution)/shard_map/ppermute | solution.py:35
  31.2 0.3 collective-permute-start.8
  31.5 2.0 %expert.12 = (f32[64,2560]{1,0:T(8,128)S(1)}, f32[64,2560]{1,0:T(8,128)S(1)}) custom-call(bf16[2560,768]{1,0:T(8,128)(2,1)S(1)} %collective-permute-done.refs_1_.refs_0_, bf16[2560,768]{1,0:T(8,128)(2,1)S(1)} %collective-permute-done.1.refs_1_, bf16[768,2560]{1,0:T(8,128)(2,1)S(1)} %collective-permute-done.2.refs_2_, bf16[2592,128]{1,0:T(8,128)(2,1)S(1)} %append.1.refs_3_, ...), custom_call_target="tpu_custom_call" | custom-call | flops 1509949440 | bytes 1310720 | tf_op jit(solution)/shard_map/expert/pallas_call | solution.py:241
  33.5 3.0 %collective-permute-done.10.second_ref = bf16[64,2560]{1,0:T(8,128)(2,1)S(1)} collective-permute-done((bf16[64,2560]{1,0:T(8,128)(2,1)S(1)}, bf16[64,2560]{1,0:T(8,128)(2,1)S(1)}, u32[]{:S(2)}, u32[]{:S(2)}) %collective-permute-start.10) | collective-permute-done | bytes 327712 | tf_op jit(solution)/shard_map/ppermute | solution.py:35
  36.5 0.1 sums.3
  36.6 1.8 %collective-permute-start.11 = (bf16[64,2560]{1,0:T(8,128)(2,1)S(1)}, bf16[64,2560]{1,0:T(8,128)(2,1)S(1)}, u32[]{:S(2)}, u32[]{:S(2)}) collective-permute-start(bf16[64,2560]{1,0:T(8,128)(2,1)S(1)} %sums.3), channel_id=1, source_target_pairs={{0,4},{1,3},{2,6},{3,1},{4,0},{5,7},{6,2},{7,5},{8,12},{9,11},{10,... | collective-permute-start | bytes 983048 | tf_op jit(solution)/shard_map/ppermute | solution.py:35
  38.4 1.9 %collective-permute-done.8.second_ref = bf16[64,2560]{1,0:T(8,128)(2,1)S(1)} collective-permute-done((bf16[64,2560]{1,0:T(8,128)(2,1)S(1)}, bf16[64,2560]{1,0:T(8,128)(2,1)S(1)}, u32[]{:S(2)}, u32[]{:S(2)}) %collective-permute-start.8) | collective-permute-done | bytes 327712 | tf_op jit(solution)/shard_map/ppermute | solution.py:35
  40.4 0.1 sums.2
  40.4 1.8 %collective-permute-start.9 = (bf16[64,2560]{1,0:T(8,128)(2,1)S(1)}, bf16[64,2560]{1,0:T(8,128)(2,1)S(1)}, u32[]{:S(2)}, u32[]{:S(2)}) collective-permute-start(bf16[64,2560]{1,0:T(8,128)(2,1)S(1)} %sums.2), channel_id=1, source_target_pairs={{0,4},{1,3},{2,6},{3,1},{4,0},{5,7},{6,2},{7,5},{8,12},{9,11},{10,... | collective-permute-start | bytes 983048 | tf_op jit(solution)/shard_map/ppermute | solution.py:35
  42.3 1.9 %expert.13.total_ref = f32[128,2560]{1,0:T(8,128)S(1)} custom-call(bf16[2560,768]{1,0:T(8,128)(2,1)S(1)} %collective-permute-done.refs_1_.refs_0_, bf16[2560,768]{1,0:T(8,128)(2,1)S(1)} %collective-permute-done.1.refs_1_, bf16[768,2560]{1,0:T(8,128)(2,1)S(1)} %collective-permute-done.2.refs_2_, bf16[2592,128]{1,0:T(8,128)(2,1)S(1)} %get-tuple-element.20.refs_3_, ...), custom_call_target="tpu_custom_call" | custom-call | flops 1509949440 | bytes 1310720 | tf_op jit(solution)/shard_map/expert/pallas_call | solution.py:241
  44.2 3.4 %collective-permute-done.9.upper_ref = bf16[64,2560]{1,0:T(8,128)(2,1)S(1)} collective-permute-done((bf16[64,2560]{1,0:T(8,128)(2,1)S(1)}, bf16[64,2560]{1,0:T(8,128)(2,1)S(1)}, u32[]{:S(2)}, u32[]{:S(2)}) %collective-permute-start.9) | collective-permute-done | bytes 327712 | tf_op jit(solution)/shard_map/ppermute | solution.py:35
  47.6 0.9 %finish.1 = bf16[128,2560]{1,0:T(8,128)(2,1)} custom-call(f32[128,2560]{1,0:T(8,128)S(1)} %expert.13.total_ref, bf16[64,2560]{1,0:T(8,128)(2,1)S(1)} %collective-permute-done.9.upper_ref, bf16[64,2560]{1,0:T(8,128)(2,1)S(1)} %collective-permute-done.11.lower_ref), custom_call_target="tpu_custom_call" | custom-call | bytes 1310720 | tf_op jit(solution)/shard_map/finish/pallas_call | solution.py:285
  (6 shorter events, 0.0 us)
Async XLA Ops:
  0.0 9.3 %collective-permute-start = (bf16[2560,768]{1,0:T(8,128)(2,1)}, bf16[2560,768]{1,0:T(8,128)(2,1)S(1)}, u32[]{:S(2)}, u32[]{:S(2)}) collective-permute-start(bf16[2560,768]{1,0:T(8,128)(2,1)} %bitcast.7), channel_id=1, source_target_pairs={{0,1},{1,0},{2,3},{3,2},{4,5},{5,4},{6,7},{7,6},{8,9},{9,8},{10,11... | collective-permute-start | bytes 11796488 | tf_op jit(solution)/shard_map/ppermute | solution.py:35
  0.5 12.6 %collective-permute-start.4 = (bf16[128,2560]{1,0:T(8,128)(2,1)}, bf16[128,2560]{1,0:T(8,128)(2,1)S(1)}, u32[]{:S(2)}, u32[]{:S(2)}) collective-permute-start(bf16[128,2560]{1,0:T(8,128)(2,1)} %tokens_hbm.1), channel_id=1, source_target_pairs={{0,4},{1,3},{2,6},{3,1},{4,0},{5,7},{6,2},{7,5},{8,12},{9,11},{10,... | collective-permute-start | bytes 1966088 | tf_op jit(solution)/shard_map/ppermute | solution.py:35
  3.0 17.5 %collective-permute-start.1 = (bf16[2560,768]{1,0:T(8,128)(2,1)}, bf16[2560,768]{1,0:T(8,128)(2,1)S(1)}, u32[]{:S(2)}, u32[]{:S(2)}) collective-permute-start(bf16[2560,768]{1,0:T(8,128)(2,1)} %bitcast.9), channel_id=1, source_target_pairs={{0,1},{1,0},{2,3},{3,2},{4,5},{5,4},{6,7},{7,6},{8,9},{9,8},{10,11... | collective-permute-start | bytes 11796488 | tf_op jit(solution)/shard_map/ppermute | solution.py:35
  3.2 17.3 %collective-permute-start.2 = (bf16[768,2560]{1,0:T(8,128)(2,1)}, bf16[768,2560]{1,0:T(8,128)(2,1)S(1)}, u32[]{:S(2)}, u32[]{:S(2)}) collective-permute-start(bf16[768,2560]{1,0:T(8,128)(2,1)} %bitcast.5), channel_id=1, source_target_pairs={{0,1},{1,0},{2,3},{3,2},{4,5},{5,4},{6,7},{7,6},{8,9},{9,8},{10,11... | collective-permute-start | bytes 11796488 | tf_op jit(solution)/shard_map/ppermute | solution.py:35
  7.7 11.0 %collective-permute-start.3 = (bf16[2592,128]{1,0:T(8,128)(2,1)S(1)}, bf16[2592,128]{1,0:T(8,128)(2,1)S(1)}, u32[]{:S(2)}, u32[]{:S(2)}) collective-permute-start(bf16[2592,128]{1,0:T(8,128)(2,1)S(1)} %get-tuple-element.20.refs_3_), channel_id=1, source_target_pairs={{0,2},{1,5},{2,0},{3,7},{4,6},{5,1},{6,4},{7,3},{8,10},{9,13},{10,... | collective-permute-start | bytes 1990664 | tf_op jit(solution)/shard_map/ppermute | solution.py:35
  9.3 3.8 %collective-permute-start.5 = (bf16[32,128]{1,0:T(8,128)(2,1)S(1)}, bf16[32,128]{1,0:T(8,128)(2,1)S(1)}, u32[]{:S(2)}, u32[]{:S(2)}) collective-permute-start(bf16[32,128]{1,0:T(8,128)(2,1)S(1)} %held.1.terms_ref), channel_id=1, source_target_pairs={{0,4},{1,3},{2,6},{3,1},{4,0},{5,7},{6,2},{7,5},{8,12},{9,11},{10,... | collective-permute-start | bytes 24584 | tf_op jit(solution)/shard_map/ppermute | solution.py:35
  13.2 12.7 %collective-permute-start.7 = (bf16[2592,128]{1,0:T(8,128)(2,1)S(1)}, bf16[2592,128]{1,0:T(8,128)(2,1)S(1)}, u32[]{:S(2)}, u32[]{:S(2)}) collective-permute-start(bf16[2592,128]{1,0:T(8,128)(2,1)S(1)} %append.1.refs_3_), channel_id=1, source_target_pairs={{0,2},{1,5},{2,0},{3,7},{4,6},{5,1},{6,4},{7,3},{8,10},{9,13},{10,... | collective-permute-start | bytes 1990664 | tf_op jit(solution)/shard_map/ppermute | solution.py:35
  22.3 20.0 %collective-permute-start.6 = (bf16[128,2560]{1,0:T(8,128)(2,1)S(1)}, bf16[128,2560]{1,0:T(8,128)(2,1)S(1)}, u32[]{:S(2)}, u32[]{:S(2)}) collective-permute-start(bf16[128,2560]{1,0:T(8,128)(2,1)S(1)} %expert.9.refs_4_), channel_id=1, source_target_pairs={{0,2},{1,5},{2,0},{3,7},{4,6},{5,1},{6,4},{7,3},{8,10},{9,13},{10,... | collective-permute-start | bytes 1966088 | tf_op jit(solution)/shard_map/ppermute | solution.py:35
  29.4 7.1 %collective-permute-start.10 = (bf16[64,2560]{1,0:T(8,128)(2,1)S(1)}, bf16[64,2560]{1,0:T(8,128)(2,1)S(1)}, u32[]{:S(2)}, u32[]{:S(2)}) collective-permute-start(bf16[64,2560]{1,0:T(8,128)(2,1)S(1)} %get-tuple-element.32.refs_7_), channel_id=1, source_target_pairs={{0,2},{1,5},{2,0},{3,7},{4,6},{5,1},{6,4},{7,3},{8,10},{9,13},{10,... | collective-permute-start | bytes 983048 | tf_op jit(solution)/shard_map/ppermute | solution.py:35
  31.2 9.2 %collective-permute-start.8 = (bf16[64,2560]{1,0:T(8,128)(2,1)S(1)}, bf16[64,2560]{1,0:T(8,128)(2,1)S(1)}, u32[]{:S(2)}, u32[]{:S(2)}) collective-permute-start(bf16[64,2560]{1,0:T(8,128)(2,1)S(1)} %get-tuple-element.31.refs_6_), channel_id=1, source_target_pairs={{0,2},{1,5},{2,0},{3,7},{4,6},{5,1},{6,4},{7,3},{8,10},{9,13},{10,... | collective-permute-start | bytes 983048 | tf_op jit(solution)/shard_map/ppermute | solution.py:35
  36.6 7.5 %collective-permute-start.11 = (bf16[64,2560]{1,0:T(8,128)(2,1)S(1)}, bf16[64,2560]{1,0:T(8,128)(2,1)S(1)}, u32[]{:S(2)}, u32[]{:S(2)}) collective-permute-start(bf16[64,2560]{1,0:T(8,128)(2,1)S(1)} %sums.3), channel_id=1, source_target_pairs={{0,4},{1,3},{2,6},{3,1},{4,0},{5,7},{6,2},{7,5},{8,12},{9,11},{10,... | collective-permute-start | bytes 983048 | tf_op jit(solution)/shard_map/ppermute | solution.py:35
  40.4 7.1 %collective-permute-start.9 = (bf16[64,2560]{1,0:T(8,128)(2,1)S(1)}, bf16[64,2560]{1,0:T(8,128)(2,1)S(1)}, u32[]{:S(2)}, u32[]{:S(2)}) collective-permute-start(bf16[64,2560]{1,0:T(8,128)(2,1)S(1)} %sums.2), channel_id=1, source_target_pairs={{0,4},{1,3},{2,6},{3,1},{4,0},{5,7},{6,2},{7,5},{8,12},{9,11},{10,... | collective-permute-start | bytes 983048 | tf_op jit(solution)/shard_map/ppermute | solution.py:35
